TPU v7x, 512 devices: a whole 4x8x8 slice. The times are simulated.
512 devices in a mesh: dp: 8 (over y_lo, core), ctx: 64 (over x, y_hi, z).
Axes of the slice: x: 4, y: 8 (y_hi: 2, y_lo: 4; y = y_hi * 4 + y_lo), z: 8, core: 2. Of those that a mesh axis runs over, the one named last changes fastest.
Arguments:
- frozen_query: bfloat16 [8, 8192, 4096], P('dp', 'ctx'), may hold values from -27 to 27, as said below
- frozen_key_value: bfloat16 [8, 8192, 1024], P('dp', 'ctx'), may hold values from -6 to 6, as said below
- lowrank: bfloat16 [8, 8192, 48], P('dp', 'ctx'), may hold values from -6 to 6
- adapter_up_weight: bfloat16 [16, 5120], replicated, may hold values from -0.5 to 0.5
- output_gradient: bfloat16 [8, 8192, 4096], P('dp', 'ctx'), may hold values from -6 to 6
Outputs:
- attended: bfloat16 [8, 8192, 4096], P('dp', 'ctx')
- grad_lowrank: float32 [8, 8192, 48], P('dp', 'ctx')
- grad_up: float32 [16, 5120], replicated
Inputs may be any that keep to these rules, and one draw needn't show every extreme that they name: `frozen_query`: finite values. `frozen_key_value`: finite values.
All inputs are finite; a program needn't handle non-finite values.
Results may differ from a plain program's by a relative error of at most 0.005.
The roundings to bfloat16 on the way count: a program that leaves them out, or rounds other values in their place, can miss the bound.
Values may be sent and summed in bfloat16 or wider, within the bound.
No kernel may reach another device: no remote copies, remote signals or barrier semaphores. Data moves between devices by JAX's collectives and lax.ppermute only.
A program may use at most 64 MiB of HBM per device.

v0:
```python
import math

import jax
import jax.numpy as jnp
from jax import lax
from jax.sharding import PartitionSpec as P

HEADS = 32
KV_HEADS = 4
D_HEAD = 128
ADAPTER_RANK = 16
GROUP = 512


def from_behind(value, axis, by):
    length = lax.axis_size(axis)
    return lax.ppermute(value, axis, [(i, (i + by) % length) for i in range(length)])


def head_attention(query_head, grad_head, key_stack, value_stack, reach):
    blocks = key_stack.shape[0]
    tok_rows = key_stack.shape[1]
    score_scale = 1.0 / math.sqrt(D_HEAD)
    keys_flat = key_stack.reshape(blocks * tok_rows, D_HEAD)
    values_flat = value_stack.reshape(blocks * tok_rows, D_HEAD)
    row_ids = lax.broadcasted_iota(jnp.int32, (tok_rows, blocks * tok_rows), 0)
    col_ids = lax.broadcasted_iota(jnp.int32, (tok_rows, blocks * tok_rows), 1)
    block_ids = col_ids // tok_rows
    inside = col_ids % tok_rows
    allowed = jnp.logical_and(block_ids <= reach, jnp.logical_or(block_ids > 0, inside <= row_ids))
    logits = (
        jnp.einsum("tgd,sd->gts", query_head, keys_flat, preferred_element_type=jnp.float32)
        * score_scale
    )
    logits = jnp.where(allowed[None], logits, -1e30)
    row_max = jnp.max(logits, axis=-1, keepdims=True)
    exp_terms = jnp.exp(logits - row_max)
    weights = (exp_terms / jnp.sum(exp_terms, axis=-1, keepdims=True)).astype(jnp.bfloat16)
    output_f = jnp.einsum("gts,sd->tgd", weights, values_flat, preferred_element_type=jnp.float32)
    row_dot = jnp.einsum("tgd,tgd->gt", grad_head.astype(jnp.float32), output_f)
    prob_grad = jnp.einsum(
        "tgd,sd->gts", grad_head, values_flat, preferred_element_type=jnp.float32
    )
    score_grad = (weights.astype(jnp.float32) * (prob_grad - row_dot[..., None])).astype(
        jnp.bfloat16
    )
    grad_query = (
        jnp.einsum("gts,sd->tgd", score_grad, keys_flat, preferred_element_type=jnp.float32)
        * score_scale
    )
    key_part = (
        jnp.einsum("gts,tgd->sd", score_grad, query_head, preferred_element_type=jnp.float32)
        * score_scale
    )
    value_part = jnp.einsum("gts,tgd->sd", weights, grad_head, preferred_element_type=jnp.float32)
    grad_store = jnp.stack([key_part, value_part], axis=1).reshape(blocks, tok_rows, 2, D_HEAD)
    return (output_f, grad_query, grad_store)


def half_attention(query_half, grad_half, key_stack, value_stack, reach):
    gradient_results = lax.map(
        lambda gradient_parts: head_attention(
            gradient_parts[0], gradient_parts[1], gradient_parts[2], gradient_parts[3], reach
        ),
        (
            jnp.moveaxis(query_half, 1, 0),
            jnp.moveaxis(grad_half, 1, 0),
            jnp.moveaxis(key_stack, 2, 0),
            jnp.moveaxis(value_stack, 2, 0),
        ),
    )
    output_f = jnp.moveaxis(gradient_results[0], 0, 1)
    grad_query = jnp.moveaxis(gradient_results[1], 0, 1)
    grad_store = jnp.transpose(gradient_results[2], (1, 2, 3, 0, 4))
    return (output_f, grad_query, grad_store)


def shards(frozen_query, frozen_key_value, lowrank, adapter_up_weight, output_gradient):
    tok_rows = frozen_query.shape[1]
    per_head_width = HEADS * D_HEAD
    key_column_width = KV_HEADS * D_HEAD
    group_size = HEADS // KV_HEADS
    split_heads = KV_HEADS // 2
    blocks = GROUP // tok_rows
    rank_width = lowrank[0]
    query_up_weight = adapter_up_weight[:, :per_head_width]
    key_up_weight = adapter_up_weight[:, per_head_width : per_head_width + key_column_width]
    value_up_weight = adapter_up_weight[:, per_head_width + key_column_width :]
    low_query = rank_width[:, :ADAPTER_RANK]
    low_key = rank_width[:, ADAPTER_RANK : 2 * ADAPTER_RANK]
    low_value = rank_width[:, 2 * ADAPTER_RANK :]
    queries = (
        frozen_query[0]
        + 2.0 * jnp.dot(low_query, query_up_weight, preferred_element_type=jnp.float32)
    ).astype(jnp.bfloat16)
    key_rows = frozen_key_value[0, :, :key_column_width] + 2.0 * jnp.dot(
        low_key, key_up_weight, preferred_element_type=jnp.float32
    )
    value_rows = frozen_key_value[0, :, key_column_width:] + 2.0 * jnp.dot(
        low_value, value_up_weight, preferred_element_type=jnp.float32
    )
    keyval = jnp.concatenate([key_rows, value_rows], axis=1).astype(jnp.bfloat16)
    others = [from_behind(keyval, "ctx", offset) for offset in range(1, blocks)]
    stacked = jnp.stack([keyval] + others)
    kv_split = stacked.reshape(blocks, tok_rows, 2, KV_HEADS, D_HEAD)
    query_heads = queries.reshape(tok_rows, KV_HEADS, group_size, D_HEAD)
    grad_heads = output_gradient[0].reshape(tok_rows, KV_HEADS, group_size, D_HEAD)
    position = lax.axis_index("ctx")
    plain_reach = position % blocks
    moved_reach = (position + blocks // 2) % blocks
    plain_out = half_attention(
        query_heads[:, :split_heads],
        grad_heads[:, :split_heads],
        kv_split[:, :, 0, :split_heads],
        kv_split[:, :, 1, :split_heads],
        plain_reach,
    )
    moved_out = half_attention(
        query_heads[:, split_heads:],
        grad_heads[:, split_heads:],
        kv_split[:, :, 0, split_heads:],
        kv_split[:, :, 1, split_heads:],
        moved_reach,
    )
    attended = (
        jnp.concatenate([plain_out[0], moved_out[0]], axis=1)
        .reshape(tok_rows, per_head_width)
        .astype(jnp.bfloat16)
    )
    grad_query = (
        jnp.concatenate([plain_out[1], moved_out[1]], axis=1)
        .reshape(tok_rows, per_head_width)
        .astype(jnp.bfloat16)
    )
    grad_terms = jnp.concatenate([plain_out[2], moved_out[2]], axis=3).reshape(
        blocks, tok_rows, 2 * key_column_width
    )
    returned = grad_terms[0]
    for offset in range(1, blocks):
        returned = returned + from_behind(grad_terms[offset], "ctx", -offset)
    grad_key = returned[:, :key_column_width].astype(jnp.bfloat16)
    grad_value = returned[:, key_column_width:].astype(jnp.bfloat16)
    grad_low = 2.0 * jnp.concatenate(
        [
            jnp.dot(grad_query, query_up_weight.T, preferred_element_type=jnp.float32),
            jnp.dot(grad_key, key_up_weight.T, preferred_element_type=jnp.float32),
            jnp.dot(grad_value, value_up_weight.T, preferred_element_type=jnp.float32),
        ],
        axis=1,
    )
    up_terms = 2.0 * jnp.concatenate(
        [
            jnp.dot(low_query.T, grad_query, preferred_element_type=jnp.float32),
            jnp.dot(low_key.T, grad_key, preferred_element_type=jnp.float32),
            jnp.dot(low_value.T, grad_value, preferred_element_type=jnp.float32),
        ],
        axis=1,
    )
    grad_up = lax.psum(up_terms, ("dp", "ctx"))
    return (attended[None], grad_low[None], grad_up)


def solution(mesh):
    return jax.shard_map(
        shards,
        mesh=mesh,
        in_specs=(
            P("dp", "ctx", None),
            P("dp", "ctx", None),
            P("dp", "ctx", None),
            P(),
            P("dp", "ctx", None),
        ),
        out_specs=(P("dp", "ctx", None), P("dp", "ctx", None), P()),
        check_vma=False,
    )
```

profile of v0, /device:TPU:1, one launch (start us, length us, event | category | flops | bytes accessed | tf_op | source)
XLA Modules:
  0.0 547.0 jit_solution(9125045892395140253)
XLA Ops:
  10.4 4.8 collective-permute-start
  15.2 5.8 %collective-permute-start.1 = (bf16[128,1024]{1,0:T(8,128)(2,1)}, bf16[128,1024]{1,0:T(8,128)(2,1)}, u32[]{:S(2)}, u32[]{:S(2)}) collective-permute-start(bf16[128,1024]{1,0:T(8,128)(2,1)} %pad_maximum_fusion.6), channel_id=1, source_target_pairs={{0,2},{1,3},{2,4},{3,5},{4,6},{5,7},{6,8},{7,9},{8,10},{9,11},{10,... | collective-permute-start | bytes 786440 | tf_op jit(solution)/shard_map/ppermute | solution.py:17
  21.0 7.0 %collective-permute-start.2 = (bf16[128,1024]{1,0:T(8,128)(2,1)}, bf16[128,1024]{1,0:T(8,128)(2,1)}, u32[]{:S(2)}, u32[]{:S(2)}) collective-permute-start(bf16[128,1024]{1,0:T(8,128)(2,1)} %pad_maximum_fusion.6), channel_id=1, source_target_pairs={{0,3},{1,4},{2,5},{3,6},{4,7},{5,8},{6,9},{7,10},{8,11},{9,12},{10... | collective-permute-start | bytes 786440 | tf_op jit(solution)/shard_map/ppermute | solution.py:17
  33.4 5.5 collective-permute-done
  40.1 8.6 %collective-permute-done.1 = bf16[128,1024]{1,0:T(8,128)(2,1)} collective-permute-done((bf16[128,1024]{1,0:T(8,128)(2,1)}, bf16[128,1024]{1,0:T(8,128)(2,1)}, u32[]{:S(2)}, u32[]{:S(2)}) %collective-permute-start.1) | collective-permute-done | bytes 262176 | tf_op jit(solution)/shard_map/ppermute | solution.py:17
  49.8 3.8 collective-permute-done.2
  58.7 29.3 %while.32 = (s32[]{:T(128)}, bf16[2,128,8,128]{1,3,2,0:T(8,128)(2,1)}, bf16[2,128,8,128]{1,3,2,0:T(8,128)(2,1)}, f32[2,4,128,2,128]{2,4,0,3,1:T(8,128)}, bf16[2,...) while((s32[]{:T(128)}, ...), condition=%wide.region_3.4_spmd, body=%wide.region_0.3_spmd.sunk | while | flops 817958400 | bytes 48693768 | solution.py:61
  59.4 1.6 constant_dynamic-slice_fusion.10
  64.0 2.2 convolution_bitcast_fusion.12
  74.0 1.6 constant_dynamic-slice_fusion.10
  78.7 2.2 convolution_bitcast_fusion.12
  90.9 29.6 %while.33 = (s32[]{:T(128)}, bf16[2,128,8,128]{1,3,2,0:T(8,128)(2,1)}, bf16[2,128,8,128]{1,3,2,0:T(8,128)(2,1)}, f32[2,4,128,2,128]{2,4,0,3,1:T(8,128)}, bf16[2,...) while((s32[]{:T(128)}, ...), condition=%wide.region_7.8_spmd, body=%wide.region_4.7_spmd.sunk | while | flops 817958400 | bytes 48693684 | solution.py:61
  91.6 1.7 constant_dynamic-slice_fusion.12
  97.2 2.2 convolution_bitcast_fusion.13
  106.4 1.7 constant_dynamic-slice_fusion.12
  112.0 2.2 convolution_bitcast_fusion.13
  120.5 2.8 fusion.68
  123.3 23.4 %collective-permute-start.3 = (f32[128,1024]{0,1:T(8,128)}, f32[128,1024]{0,1:T(8,128)S(1)}, u32[]{:S(2)}, u32[]{:S(2)}) collective-permute-start(f32[128,1024]{0,1:T(8,128)} %bitcast.77), channel_id=1, source_target_pairs={{0,63},{1,0},{2,1},{3,2},{4,3},{5,4},{6,5},{7,6},{8,7},{9,8},{10,9... | collective-permute-start | bytes 1572872 | tf_op jit(solution)/shard_map/ppermute | solution.py:17
  146.7 1.9 collective-permute-start.4
  148.6 1.9 collective-permute-start.5
  153.1 4.6 collective-permute-done.3
  157.7 64.7 %collective-permute-done.4 = f32[128,1024]{0,1:T(8,128)} collective-permute-done((f32[128,1024]{0,1:T(8,128)}, f32[128,1024]{0,1:T(8,128)}, u32[]{:S(2)}, u32[]{:S(2)}) %collective-permute-start.4) | collective-permute-done | bytes 524320 | tf_op jit(solution)/shard_map/ppermute | solution.py:17
  225.6 312.8 %all-reduce.2.cloned.1.call-done = f32[16,5120]{1,0:T(8,128)} async-done(((f32[16,5120]{1,0:T(8,128)}), f32[16,5120]{1,0:T(8,128)}) %all-reduce.2.cloned.1.call-update) | async-done | bytes 327696 | tf_op jit(solution)/shard_map/psum | solution.py:159
  538.4 1.7 copy.149
  (244 shorter events, 67.2 us)
Async XLA Ops:
  7.2 21.0 %copy-start.31 = (bf16[16,5120]{1,0:T(8,128)(2,1)S(1)}, bf16[16,5120]{1,0:T(8,128)(2,1)}, u32[]{:S(2)}) copy-start(bf16[16,5120]{1,0:T(8,128)(2,1)} %param.12) | copy-start | bytes 491524
  7.2 21.0 %copy-start.29 = (bf16[1,128,4096]{2,1,0:T(8,128)(2,1)S(1)}, bf16[1,128,4096]{2,1,0:T(8,128)(2,1)}, u32[]{:S(2)}) copy-start(bf16[1,128,4096]{2,1,0:T(8,128)(2,1)} %param.9) | copy-start | bytes 3145732
  7.2 531.2 %all-reduce.2.cloned.1.call-start = ((), (), s32[]{:S(2)}) async-start(), calls=%async_computation | async-start | bytes 655360 | tf_op jit(solution)/shard_map/psum | solution.py:159
  10.4 28.5 %collective-permute-start = (bf16[128,1024]{1,0:T(8,128)(2,1)}, bf16[128,1024]{1,0:T(8,128)(2,1)}, u32[]{:S(2)}, u32[]{:S(2)}) collective-permute-start(bf16[128,1024]{1,0:T(8,128)(2,1)} %pad_maximum_fusion.6), channel_id=1, source_target_pairs={{0,1},{1,2},{2,3},{3,4},{4,5},{5,6},{6,7},{7,8},{8,9},{9,10},{10,1... | collective-permute-start | bytes 786440 | tf_op jit(solution)/shard_map/ppermute | solution.py:17
  15.2 33.5 %collective-permute-start.1 = (bf16[128,1024]{1,0:T(8,128)(2,1)}, bf16[128,1024]{1,0:T(8,128)(2,1)}, u32[]{:S(2)}, u32[]{:S(2)}) collective-permute-start(bf16[128,1024]{1,0:T(8,128)(2,1)} %pad_maximum_fusion.6), channel_id=1, source_target_pairs={{0,2},{1,3},{2,4},{3,5},{4,6},{5,7},{6,8},{7,9},{8,10},{9,11},{10,... | collective-permute-start | bytes 786440 | tf_op jit(solution)/shard_map/ppermute | solution.py:17
  21.0 32.6 %collective-permute-start.2 = (bf16[128,1024]{1,0:T(8,128)(2,1)}, bf16[128,1024]{1,0:T(8,128)(2,1)}, u32[]{:S(2)}, u32[]{:S(2)}) collective-permute-start(bf16[128,1024]{1,0:T(8,128)(2,1)} %pad_maximum_fusion.6), channel_id=1, source_target_pairs={{0,3},{1,4},{2,5},{3,6},{4,7},{5,8},{6,9},{7,10},{8,11},{9,12},{10... | collective-permute-start | bytes 786440 | tf_op jit(solution)/shard_map/ppermute | solution.py:17
  58.7 3.2 copy-start.11
  64.0 3.6 copy-start.2
  64.0 3.6 copy-start.23
  73.3 2.8 copy-start.17
  73.4 3.2 copy-start.11
  78.7 3.6 copy-start.2
  78.7 3.6 copy-start.23
  91.6 3.5 copy-start.7
  97.2 3.6 copy-start.4
  97.2 3.6 copy-start.19
  106.4 3.5 copy-start.7
  112.0 3.6 copy-start.4
  112.0 3.6 copy-start.19
  120.5 30.0 %copy-start.21 = (bf16[2,128,8,128]{1,3,2,0:T(8,128)(2,1)S(1)}, bf16[2,128,8,128]{1,3,2,0:T(8,128)(2,1)}, u32[]{:S(2)}) copy-start(bf16[2,128,8,128]{1,3,2,0:T(8,128)(2,1)} %get-tuple-element.240) | copy-start | bytes 1572868
  120.5 30.0 %copy-start.25 = (bf16[2,128,8,128]{1,3,2,0:T(8,128)(2,1)S(1)}, bf16[2,128,8,128]{1,3,2,0:T(8,128)(2,1)}, u32[]{:S(2)}) copy-start(bf16[2,128,8,128]{1,3,2,0:T(8,128)(2,1)} %get-tuple-element.239) | copy-start | bytes 1572868
  123.3 34.4 %collective-permute-start.3 = (f32[128,1024]{0,1:T(8,128)}, f32[128,1024]{0,1:T(8,128)S(1)}, u32[]{:S(2)}, u32[]{:S(2)}) collective-permute-start(f32[128,1024]{0,1:T(8,128)} %bitcast.77), channel_id=1, source_target_pairs={{0,63},{1,0},{2,1},{3,2},{4,3},{5,4},{6,5},{7,6},{8,7},{9,8},{10,9... | collective-permute-start | bytes 1572872 | tf_op jit(solution)/shard_map/ppermute | solution.py:17
  146.7 75.7 %collective-permute-start.4 = (f32[128,1024]{0,1:T(8,128)}, f32[128,1024]{0,1:T(8,128)}, u32[]{:S(2)}, u32[]{:S(2)}) collective-permute-start(f32[128,1024]{0,1:T(8,128)} %bitcast.78), channel_id=1, source_target_pairs={{0,62},{1,63},{2,0},{3,1},{4,2},{5,3},{6,4},{7,5},{8,6},{9,7},{10,... | collective-permute-start | bytes 1572872 | tf_op jit(solution)/shard_map/ppermute | solution.py:17
  148.6 73.8 %collective-permute-start.5 = (f32[128,1024]{0,1:T(8,128)}, f32[128,1024]{0,1:T(8,128)}, u32[]{:S(2)}, u32[]{:S(2)}) collective-permute-start(f32[128,1024]{0,1:T(8,128)} %bitcast.79), channel_id=1, source_target_pairs={{0,61},{1,62},{2,63},{3,0},{4,1},{5,2},{6,3},{7,4},{8,5},{9,6},{10... | collective-permute-start | bytes 1572872 | tf_op jit(solution)/shard_map/ppermute | solution.py:17
  (42 other events, 68.1 us)
Sparse Core Ops, SparseCore 0:
  225.0 313.3 all-reduce.1
where the time goes:
time: 549 us; the launch traced here: 547 us
  waiting for transfers between devices  400 us (73%)
  starting transfers between devices  44.9 us (8%)
  local copies, waits for them, and re-layouts  38.1 us (7%)
  matrix products  27.1 us (5%)
  other arithmetic  21.6 us (4%)
  between operations  14.3 us (3%)
    psum x1, waiting for transfers between devices, shards(): grad_up = lax.psum(up_terms, ('dp', 'ctx'))  313 us
    ppermute x6, waiting for transfers between devices, from_behind(): lax.ppermute(value, axis, [(i, (i + by) % length) for i in range(length)])  87.1 us
    ppermute x6, starting transfers between devices, from_behind(): lax.ppermute(value, axis, [(i, (i + by) % length) for i in range(length)])  44.9 us
  transfers between devices with their start and end apart: 7, of which 6 were waited for; matrix products, arithmetic and copies ran while one was open for 2% of the time, Pallas kernels for 0%

commit v1 on v0

v1 whole, which is shorter than its diff:
```python
import math

import jax
import jax.numpy as jnp
from jax import lax
from jax.experimental import pallas as pl
from jax.experimental.pallas import tpu as pltpu
from jax.sharding import PartitionSpec as P

HEADS = 32
KV_HEADS = 4
D_HEAD = 128
RANK = 16
GROUP = 512
ROWS = 128
MESSAGE = ROWS + RANK
SHARE = HEADS // KV_HEADS
WIDE = SHARE * D_HEAD
TERMS = WIDE + 2 * D_HEAD
Z_RING = 8
BLOCKED = -1e30
F32 = jnp.float32
BF16 = jnp.bfloat16


def mul(a, b):
    return lax.dot_general(a, b, (((1,), (0,)), ((), ())), preferred_element_type=F32)


def mul_t(a, b):
    return lax.dot_general(a, b, (((1,), (1,)), ((), ())), preferred_element_type=F32)


def prepare_kernel(place, frozen, low, up, light, heavy):
    zeros = jnp.zeros((RANK, 2 * 2 * D_HEAD), BF16)
    up_k = jnp.concatenate([zeros, up[:, : 4 * D_HEAD], zeros], axis=0)
    up_v = jnp.concatenate([zeros, zeros, up[:, 4 * D_HEAD :]], axis=0)
    lows = low[0]
    keys = (frozen[0, :, : 4 * D_HEAD].astype(F32) + 2.0 * mul(lows, up_k)).astype(BF16)
    values = (frozen[0, :, 4 * D_HEAD :].astype(F32) + 2.0 * mul(lows, up_v)).astype(BF16)
    row = lax.broadcasted_iota(jnp.int32, (3 * RANK, 3 * RANK), 0)
    col = lax.broadcasted_iota(jnp.int32, (3 * RANK, 3 * RANK), 1)
    turned = mul_t((row == col).astype(F32).astype(BF16), lows).astype(BF16)
    tail = jnp.concatenate(
        [turned[RANK : 2 * RANK], turned[2 * RANK :], turned[:RANK], jnp.zeros((RANK, D_HEAD), BF16)],
        axis=1,
    )
    half = 2 * D_HEAD

    def write(plain, moved):
        plain[:ROWS, :half] = keys[:, :half]
        plain[:ROWS, half:] = values[:, :half]
        plain[ROWS:, :] = tail
        moved[:ROWS, :half] = keys[:, half:]
        moved[:ROWS, half:] = values[:, half:]
        moved[ROWS:, :] = tail

    @pl.when(place[0] == 0)
    def _():
        write(light, heavy)

    @pl.when(place[0] != 0)
    def _():
        write(heavy, light)


def attend(place, query, grad, low, up_q, up_k, up_v, blocks, closed, attended, terms):
    head = pl.program_id(0)
    key_cols = pl.ds(pl.multiple_of(head * D_HEAD, D_HEAD), D_HEAD)
    value_cols = pl.ds(pl.multiple_of((head + 2) * D_HEAD, D_HEAD), D_HEAD)
    bias = jnp.where(place[1] == 1, 0.0, BLOCKED).astype(F32)
    scale = 1.0 / math.sqrt(D_HEAD)
    keys = jnp.concatenate([b(slice(0, ROWS), key_cols) for b in blocks], axis=0)
    values = jnp.concatenate([b(slice(0, ROWS), value_cols) for b in blocks], axis=0)
    tail = slice(ROWS, MESSAGE)
    low_k = jnp.concatenate([b(tail, slice(0, D_HEAD)) for b in blocks], axis=1)
    low_v = jnp.concatenate([b(tail, slice(D_HEAD, 2 * D_HEAD)) for b in blocks], axis=1)
    low_q = blocks[0](tail, slice(2 * D_HEAD, 3 * D_HEAD))
    keys_t = keys.T
    values_t = values.T
    up_rows = up_q[...]
    padded = jnp.concatenate([up_rows, jnp.zeros((2 * RANK, WIDE), BF16)], axis=0)
    queries = (query[0].astype(F32) + 2.0 * mul(low[0], padded)).astype(BF16)
    grads = grad[0]
    row = lax.broadcasted_iota(jnp.int32, (ROWS, 2 * ROWS), 0)
    col = lax.broadcasted_iota(jnp.int32, (ROWS, 2 * ROWS), 1)
    causal = row <= jnp.where(col >= ROWS, col - ROWS, col)
    low_grad = jnp.zeros((RANK, ROWS), F32)
    all_queries, all_grads, all_weights, all_scores = [], [], [], []
    for pair in range(SHARE // 2):
        sides = [slice((2 * pair + s) * D_HEAD, (2 * pair + s + 1) * D_HEAD) for s in range(2)]
        query_two = jnp.concatenate([queries[:, s] for s in sides], axis=0)
        grad_two = jnp.concatenate([grads[:, s] for s in sides], axis=0)
        logits = mul_t(keys, query_two)
        parts = [jnp.where(causal, logits[:ROWS], BLOCKED)]
        for i, shut in enumerate(closed):
            part = logits[(i + 1) * ROWS : (i + 2) * ROWS]
            parts.append(part + bias if shut else part)
        logits = jnp.concatenate(parts, axis=0)
        peak = jnp.max(logits, axis=0, keepdims=True)
        exps = jnp.exp2((logits - peak) * (scale * math.log2(math.e)))
        weights = (exps * (1.0 / jnp.sum(exps, axis=0, keepdims=True))).astype(BF16)
        out_t = mul(values_t, weights)
        prob_grad = mul_t(values, grad_two)
        weights_f = weights.astype(F32)
        product = weights_f * prob_grad
        row_dot = jnp.sum(product, axis=0, keepdims=True)
        scores = (product - weights_f * row_dot).astype(BF16)
        grad_query_t = (mul(keys_t, scores) * scale).astype(BF16)
        for i, side in enumerate(sides):
            mine = slice(i * ROWS, (i + 1) * ROWS)
            attended[0, :, side] = out_t[:, mine].T.astype(BF16)
            low_grad = low_grad + mul(up_rows[:, side], grad_query_t[:, mine])
            terms[0, :, side] = (2.0 * mul_t(low_q, grad_query_t[:, mine])).astype(terms.dtype)
        all_queries.append(query_two)
        all_grads.append(grad_two)
        all_weights.append(weights)
        all_scores.append(scores)
    grad_keys = mul(jnp.concatenate(all_scores, axis=1), jnp.concatenate(all_queries, axis=0))
    grad_keys = (grad_keys * scale).astype(BF16)
    grad_values = mul(jnp.concatenate(all_weights, axis=1), jnp.concatenate(all_grads, axis=0)).astype(BF16)
    terms[0, :, WIDE : WIDE + D_HEAD] = (2.0 * mul(low_k, grad_keys)).astype(terms.dtype)
    terms[0, :, WIDE + D_HEAD :] = (2.0 * mul(low_v, grad_values)).astype(terms.dtype)
    return 2.0 * low_grad, 2.0 * mul_t(up_k[...], grad_keys), 2.0 * mul_t(up_v[...], grad_values)


def light_kernel(place, query, grad, low, up_q, up_k, up_v, own, one, attended, terms, low_terms):
    blocks = [lambda r, c: own[r, c], lambda r, c: one[r, c]]
    by_query, by_key, by_value = attend(
        place, query, grad, low, up_q, up_k, up_v, blocks, [True], attended, terms
    )
    found = jnp.concatenate(
        [jnp.concatenate([by_query, jnp.zeros_like(by_query)], axis=1), by_key, by_value], axis=0
    )

    @pl.when(pl.program_id(0) == 0)
    def _():
        low_terms[...] = found

    @pl.when(pl.program_id(0) != 0)
    def _():
        low_terms[...] += found


def heavy_kernel(
    place, query, grad, low, up_q, up_k, up_v, own, one_even, one_odd, two, three, before,
    _attended, _terms, attended, terms, mine, back_one, back_two, back_three,
):
    odd = place[1] == 1
    blocks = [
        lambda r, c: own[r, c],
        lambda r, c: jnp.where(odd, one_odd[r, c], one_even[r, c]),
        lambda r, c: two[r, c],
        lambda r, c: three[r, c],
    ]

    @pl.when(pl.program_id(0) == 0)
    def _():
        mine[...] = before[:, :ROWS]
        back_one[...] = before[RANK:, ROWS:]
        back_two[...] = jnp.zeros_like(back_two)
        back_three[...] = jnp.zeros_like(back_three)

    by_query, by_key, by_value = attend(
        place, query, grad, low, up_q, up_k, up_v, blocks, [False, False, True], attended, terms
    )
    mine[:RANK, :] += by_query
    mine[RANK : 2 * RANK, :] += by_key[:, :ROWS]
    mine[2 * RANK :, :] += by_value[:, :ROWS]
    for i, back in enumerate((back_one, back_two, back_three)):
        block = slice((i + 1) * ROWS, (i + 2) * ROWS)
        back[:RANK, :] += by_key[:, block]
        back[RANK:, :] += by_value[:, block]


def whole(*shape):
    return pl.BlockSpec(shape, lambda head, place: (0,) * len(shape))


def at_half(rows, width, first=0):
    return pl.BlockSpec((rows, width), lambda head, place: (0, first + place[0] * 2 + head))


def wide_half():
    return pl.BlockSpec((1, ROWS, WIDE), lambda head, place: (0, 0, place[0] * 2 + head))


def term_half():
    return pl.BlockSpec((1, RANK, TERMS), lambda head, place: (place[0] * 2 + head, 0, 0))


def common_specs():
    return [
        wide_half(),
        wide_half(),
        whole(1, ROWS, 3 * RANK),
        at_half(RANK, WIDE),
        at_half(RANK, D_HEAD, HEADS),
        at_half(RANK, D_HEAD, HEADS + KV_HEADS),
    ]


def params():
    return pltpu.CompilerParams(
        dimension_semantics=("arbitrary",), vmem_limit_bytes=40 * 1024 * 1024
    )


def cost(blocks):
    sizes = 16 * blocks * ROWS * ROWS
    return pl.CostEstimate(
        flops=12 * sizes * D_HEAD, bytes_accessed=6 * ROWS * WIDE * 2, transcendentals=sizes
    )


def exchange(value, axis, groups=None):
    return lax.all_to_all(value, axis, 0, 0, axis_index_groups=groups)


def summed(parts):
    return jnp.sum(parts.astype(F32), axis=0).astype(BF16)


def everywhere(terms):
    seqs, spans = lax.axis_size("dp"), lax.axis_size("ctx")
    along = [[first + i for i in range(Z_RING)] for first in range(0, spans, Z_RING)]
    across = [list(range(i, spans, Z_RING)) for i in range(Z_RING)]
    shape = terms.shape
    part = summed(exchange(terms.reshape(seqs, -1, TERMS), "dp"))
    part = summed(exchange(jnp.broadcast_to(part, (Z_RING,) + part.shape), "ctx", along))
    part = summed(exchange(jnp.broadcast_to(part, (spans // Z_RING,) + part.shape), "ctx", across))
    return exchange(jnp.broadcast_to(part, (seqs,) + part.shape), "dp").reshape(shape)


def shards(frozen_query, frozen_key_value, lowrank, adapter_up_weight, output_gradient):
    spans = lax.axis_size("ctx")
    position = lax.axis_index("ctx") % (GROUP // ROWS)
    light_half = position // 2
    odd = position % 2
    light_place = jnp.stack([light_half, odd]).astype(jnp.int32)
    heavy_place = jnp.stack([1 - light_half, odd]).astype(jnp.int32)
    message = jax.ShapeDtypeStruct((MESSAGE, 4 * D_HEAD), BF16)
    message_spec = whole(MESSAGE, 4 * D_HEAD)
    up_block = pl.BlockSpec((RANK, 8 * D_HEAD), lambda head, place: (0, HEADS // 8))
    light, heavy = pl.pallas_call(
        prepare_kernel,
        out_shape=(message, message),
        grid_spec=pltpu.PrefetchScalarGridSpec(
            num_scalar_prefetch=1,
            grid=(1,),
            in_specs=[whole(1, ROWS, 8 * D_HEAD), whole(1, ROWS, 3 * RANK), up_block],
            out_specs=[message_spec, message_spec],
        ),
        name="prepare",
    )(light_place, frozen_key_value, lowrank, adapter_up_weight)

    def send(value, by, step=1):
        return lax.ppermute(value, "ctx", [(i, (i + by) % spans) for i in range(0, spans, step)])

    one = send(light, 1)
    one_odd = send(heavy, 1, 2)
    two = send(light, 2)
    three = send(light, 3, 2)
    wide_out = jax.ShapeDtypeStruct((1, ROWS, HEADS * D_HEAD), BF16)
    terms_out = jax.ShapeDtypeStruct((KV_HEADS, RANK, TERMS), BF16)
    arguments = (frozen_query, output_gradient, lowrank) + (adapter_up_weight,) * 3
    attended, terms, low_terms = pl.pallas_call(
        light_kernel,
        out_shape=(wide_out, terms_out, jax.ShapeDtypeStruct((3 * RANK, 2 * ROWS), F32)),
        grid_spec=pltpu.PrefetchScalarGridSpec(
            num_scalar_prefetch=1,
            grid=(2,),
            in_specs=common_specs() + [message_spec] * 2,
            out_specs=[wide_half(), term_half(), whole(3 * RANK, 2 * ROWS)],
        ),
        compiler_params=params(),
        cost_estimate=cost(2),
        name="light_heads",
    )(light_place, *arguments, light, one)
    back_out = jax.ShapeDtypeStruct((2 * RANK, ROWS), F32)
    back_spec = whole(2 * RANK, ROWS)
    attended, terms, mine, *backs = pl.pallas_call(
        heavy_kernel,
        out_shape=(wide_out, terms_out, jax.ShapeDtypeStruct((3 * RANK, ROWS), F32)) + (back_out,) * 3,
        grid_spec=pltpu.PrefetchScalarGridSpec(
            num_scalar_prefetch=1,
            grid=(2,),
            in_specs=common_specs()
            + [message_spec] * 5
            + [whole(3 * RANK, 2 * ROWS)]
            + [pl.BlockSpec(memory_space=pl.ANY)] * 2,
            out_specs=[wide_half(), term_half(), whole(3 * RANK, ROWS)] + [back_spec] * 3,
        ),
        input_output_aliases={13: 0, 14: 1},
        compiler_params=params(),
        cost_estimate=cost(4),
        name="heavy_heads",
    )(heavy_place, *arguments, heavy, one, one_odd, two, three, low_terms, attended, terms)
    returned = send(backs[0], -1) + send(backs[1], -2)
    last = [(i, (i - 3) % spans) for i in range(1, spans, 2)]
    returned = returned + lax.ppermute(backs[2], "ctx", last)
    grad_low = (mine + jnp.pad(returned, ((RANK, 0), (0, 0)))).T
    total = everywhere(terms).astype(F32)
    pieces = [total[:, :, :WIDE], total[:, :, WIDE : WIDE + D_HEAD], total[:, :, WIDE + D_HEAD :]]
    grad_up = jnp.concatenate(
        [jnp.moveaxis(p, 0, 1).reshape(RANK, -1) for p in pieces], axis=1
    )
    return (attended, grad_low[None], grad_up)


def solution(mesh):
    return jax.shard_map(
        shards,
        mesh=mesh,
        in_specs=(
            P("dp", "ctx", None),
            P("dp", "ctx", None),
            P("dp", "ctx", None),
            P(),
            P("dp", "ctx", None),
        ),
        out_specs=(P("dp", "ctx", None), P("dp", "ctx", None), P()),
        check_vma=False,
    )
```

time: 549 us -> 113 us (0.21)
  the two profiles are of different devices: /device:TPU:1 before, /device:TPU:64 now
where the time goes in v1:
time: 113 us; the launch traced here: 112 us
  starting transfers between devices  39.8 us (35%)
  blocking collectives  27 us (24%)
  Pallas kernels  23.3 us (21%)
  waiting for transfers between devices  12.2 us (11%)
  local copies, waits for them, and re-layouts  6.77 us (6%)
  other arithmetic  2.2 us (2%)
    ppermute x6, starting transfers between devices, send(): lax.ppermute(value, 'ctx', [(i, (i + by) % spans) for i in range(0, spans...  27.3 us
    all_to_all x2, blocking collectives, exchange(): return lax.all_to_all(value, axis, 0, 0, axis_index_groups=groups)  27 us
    pallas_call x1, Pallas kernels, shards(): pl.pallas_call(heavy_kernel, out_shape=(wide_out, terms_out, jax.ShapeDty...  11.6 us
    pallas_call x1, Pallas kernels, shards(): pl.pallas_call(light_kernel, out_shape=(wide_out, terms_out, jax.ShapeDty...  8.98 us
    all_to_all x2, starting transfers between devices, exchange(): return lax.all_to_all(value, axis, 0, 0, axis_index_groups=groups)  7.93 us
    all_to_all x2, waiting for transfers between devices, exchange(): return lax.all_to_all(value, axis, 0, 0, axis_index_groups=groups)  6.57 us
    ppermute x6, waiting for transfers between devices, send(): lax.ppermute(value, 'ctx', [(i, (i + by) % spans) for i in range(0, spans...  5.64 us
    unnamed x23, local copies, waits for them, and re-layouts  5.37 us
  transfers between devices with their start and end apart: 9, of which 3 were waited for; matrix products, arithmetic and copies ran while one was open for 1% of the time, Pallas kernels for 8%

profile of v1, /device:TPU:64, one launch (start us, length us, event | category | flops | bytes accessed | tf_op | source)
XLA Modules:
  0.0 112.1 jit_solution(7335140968072331492)
XLA Ops:
  0.7 0.7 copy-done.9
  1.4 0.7 copy.24.low
  2.7 2.7 %prepare.1 = (bf16[144,512]{1,0:T(8,128)(2,1)}, bf16[144,512]{1,0:T(8,128)(2,1)}) custom-call(s32[2]{0:T(128)} %pad_add_fusion.1.place, bf16[1,128,1024]{2,1,0:T(8,128)(2,1)} %frozen.1, bf16[1,128,48]{2,1,0:T(8,128)(2,1)} %copy.24.low, bf16[16,5120]{1,0:T(8,128)(2,1)} %up_v.3), custom_call_target="tpu_custom_call" | custom-call | tf_op jit(solution)/shard_map/prepare/pallas_call | solution.py:245
  5.4 4.3 %collective-permute-start = (bf16[144,512]{1,0:T(8,128)(2,1)}, bf16[144,512]{1,0:T(8,128)(2,1)S(1)}, u32[]{:S(2)}, u32[]{:S(2)}) collective-permute-start(bf16[144,512]{1,0:T(8,128)(2,1)} %get-tuple-element.15.own), channel_id=1, source_target_pairs={{0,1},{1,2},{2,3},{3,4},{4,5},{5,6},{6,7},{7,8},{8,9},{9,10},{10,1... | collective-permute-start | bytes 442376 | tf_op jit(solution)/shard_map/ppermute | solution.py:258
  9.7 1.3 %collective-permute-start.3 = (bf16[144,512]{1,0:T(8,128)(2,1)}, bf16[144,512]{1,0:T(8,128)(2,1)S(1)}, u32[]{:S(2)}, u32[]{:S(2)}) collective-permute-start(bf16[144,512]{1,0:T(8,128)(2,1)} %get-tuple-element.15.own), channel_id=1, source_target_pairs={{0,3},{2,5},{4,7},{6,9},{8,11},{10,13},{12,15},{14,17},{16,19},{18... | collective-permute-start | bytes 442376 | tf_op jit(solution)/shard_map/ppermute | solution.py:258
  11.0 7.3 %collective-permute-start.2 = (bf16[144,512]{1,0:T(8,128)(2,1)}, bf16[144,512]{1,0:T(8,128)(2,1)S(1)}, u32[]{:S(2)}, u32[]{:S(2)}) collective-permute-start(bf16[144,512]{1,0:T(8,128)(2,1)} %get-tuple-element.15.own), channel_id=1, source_target_pairs={{0,2},{1,3},{2,4},{3,5},{4,6},{5,7},{6,8},{7,9},{8,10},{9,11},{10,... | collective-permute-start | bytes 442376 | tf_op jit(solution)/shard_map/ppermute | solution.py:258
  18.3 1.3 %collective-permute-start.1 = (bf16[144,512]{1,0:T(8,128)(2,1)}, bf16[144,512]{1,0:T(8,128)(2,1)S(1)}, u32[]{:S(2)}, u32[]{:S(2)}) collective-permute-start(bf16[144,512]{1,0:T(8,128)(2,1)} %get-tuple-element.14.own), channel_id=1, source_target_pairs={{0,1},{2,3},{4,5},{6,7},{8,9},{10,11},{12,13},{14,15},{16,17},{18,... | collective-permute-start | bytes 442376 | tf_op jit(solution)/shard_map/ppermute | solution.py:258
  20.3 1.2 %copy-done.3 = bf16[1,128,4096]{2,1,0:T(8,128)(2,1)S(1)} copy-done((bf16[1,128,4096]{2,1,0:T(8,128)(2,1)S(1)}, bf16[1,128,4096]{2,1,0:T(8,128)(2,1)}, u32[]{:S(2)}) %copy-start.3) | copy-done | bytes 1048600
  21.5 1.2 %copy-done.5 = bf16[1,128,4096]{2,1,0:T(8,128)(2,1)S(1)} copy-done((bf16[1,128,4096]{2,1,0:T(8,128)(2,1)S(1)}, bf16[1,128,4096]{2,1,0:T(8,128)(2,1)}, u32[]{:S(2)}) %copy-start.5) | copy-done | bytes 1048600
  22.8 0.9 copy-done.8
  23.7 9.0 %light_heads.1 = (bf16[1,128,4096]{2,1,0:T(8,128)(2,1)}, bf16[4,16,1280]{2,1,0:T(8,128)(2,1)S(1)}, f32[48,256]{1,0:T(8,128)S(1)}) custom-call(s32[2]{0:T(128)S(1)} %copy-done.2, bf16[1,128,4096]{2,1,0:T(8,128)(2,1)S(1)} %copy-done.3, bf16[1,128,4096]{2,1,0:T(8,128)(2,1)S(1)} %copy-done.5, bf16[1,128,48]{2,1,0:T(8,128)(2,1)S(1)} %copy-done.1, ...), custom_call_target="tpu_custom_call" | custom-call | flops 805306368 | bytes 1572864 | tf_op jit(solution)/shard_map/light_heads/pallas_call | solution.py:267
  32.6 2.3 %collective-permute-done.1.one_odd = bf16[144,512]{1,0:T(8,128)(2,1)S(1)} collective-permute-done((bf16[144,512]{1,0:T(8,128)(2,1)}, bf16[144,512]{1,0:T(8,128)(2,1)S(1)}, u32[]{:S(2)}, u32[]{:S(2)}) %collective-permute-start.1) | collective-permute-done | bytes 147488 | tf_op jit(solution)/shard_map/ppermute | solution.py:258
  35.0 3.3 %collective-permute-done.2.two = bf16[144,512]{1,0:T(8,128)(2,1)S(1)} collective-permute-done((bf16[144,512]{1,0:T(8,128)(2,1)}, bf16[144,512]{1,0:T(8,128)(2,1)S(1)}, u32[]{:S(2)}, u32[]{:S(2)}) %collective-permute-start.2) | collective-permute-done | bytes 147488 | tf_op jit(solution)/shard_map/ppermute | solution.py:258
  38.3 11.6 %heavy_heads.1 = (bf16[1,128,4096]{2,1,0:T(8,128)(2,1)}, bf16[4,16,1280]{2,1,0:T(8,128)(2,1)S(1)}, f32[48,128]{1,0:T(8,128)S(1)}, f32[32,128]{1,0:T(8,128)S(1)},...) custom-call(s32[2]{0:T(128)S(1)} %pad_add_fusion.place, ...), custom_call_target="tpu_custom_call", output_to_operand_aliasing={{0}: (13, {}), {1}: (14, {})} | custom-call | flops 1610612736 | bytes 1572864 | tf_op jit(solution)/shard_map/heavy_heads/pallas_call | solution.py:282
  49.9 9.6 %all_to_all.20 = bf16[8,8,1280]{2,1,0:T(8,128)(2,1)S(1)} all-to-all(bf16[8,8,1280]{2,1,0:T(8,128)(2,1)S(1)} %bitcast.26), channel_id=1, replica_groups=mesh['dp'=8,'ctx'=64] {'dp'}, dimensions={0} | all-to-all | bytes 327680 | tf_op jit(solution)/shard_map/all_to_all | solution.py:217
  59.6 17.4 %all_to_all.21 = bf16[8,8,1280]{2,1,0:T(8,128)(2,1)S(1)} all-to-all(bf16[8,8,1280]{2,1,0:T(8,128)(2,1)S(1)} %broadcast_in_dim.13), channel_id=1, replica_groups={{0,1,2,3,4,5,6,7},{8,9,10,11,12,13,14,15},{16,17,18,19,20,21,22,23},{24..., dimensions={0} | all-to-all | bytes 327680 | tf_op jit(solution)/shard_map/all_to_all | solution.py:217
  76.9 0.7 broadcast_in_dim.14
  77.6 4.3 %all-to-all-start.2 = ((bf16[8,8,1280]{2,1,0:T(8,128)(2,1)}), bf16[8,8,1280]{2,1,0:T(8,128)(2,1)S(1)}, u32[]{:S(2)}, u32[]{:S(2)}) async-start(bf16[8,8,1280]{2,1,0:T(8,128)(2,1)} %broadcast_in_dim.14), calls=%async_computation.2 | async-start | bytes 327680 | tf_op jit(solution)/shard_map/all_to_all | solution.py:217
  81.9 3.4 %collective-permute-start.4 = (f32[32,128]{1,0:T(8,128)S(1)}, f32[32,128]{1,0:T(8,128)S(1)}, u32[]{:S(2)}, u32[]{:S(2)}) collective-permute-start(f32[32,128]{1,0:T(8,128)S(1)} %get-tuple-element.21), channel_id=1, source_target_pairs={{0,63},{1,0},{2,1},{3,2},{4,3},{5,4},{6,5},{7,6},{8,7},{9,8},{10,9... | collective-permute-start | bytes 49160 | tf_op jit(solution)/shard_map/ppermute | solution.py:258
  85.3 9.8 %collective-permute-start.5 = (f32[32,128]{1,0:T(8,128)S(1)}, f32[32,128]{1,0:T(8,128)S(1)}, u32[]{:S(2)}, u32[]{:S(2)}) collective-permute-start(f32[32,128]{1,0:T(8,128)S(1)} %get-tuple-element.22), channel_id=1, source_target_pairs={{0,62},{1,63},{2,0},{3,1},{4,2},{5,3},{6,4},{7,5},{8,6},{9,7},{10,... | collective-permute-start | bytes 49160 | tf_op jit(solution)/shard_map/ppermute | solution.py:258
  95.1 4.6 %collective-permute-start.6 = (f32[32,128]{1,0:T(8,128)S(1)}, f32[32,128]{1,0:T(8,128)S(1)}, u32[]{:S(2)}, u32[]{:S(2)}) collective-permute-start(f32[32,128]{1,0:T(8,128)S(1)} %get-tuple-element.23), channel_id=1, source_target_pairs={{1,62},{3,0},{5,2},{7,4},{9,6},{11,8},{13,10},{15,12},{17,14},{19,... | collective-permute-start | bytes 49160 | tf_op jit(solution)/shard_map/ppermute | solution.py:301
  100.4 3.6 %all-to-all-start.3 = ((bf16[8,8,1280]{2,1,0:T(8,128)(2,1)}), bf16[8,8,1280]{2,1,0:T(8,128)(2,1)S(1)}, u32[]{:S(2)}, u32[]{:S(2)}) async-start(bf16[8,8,1280]{2,1,0:T(8,128)(2,1)} %broadcast_in_dim.15), calls=%async_computation.3 | async-start | bytes 327680 | tf_op jit(solution)/shard_map/all_to_all | solution.py:217
  104.6 6.6 %all-to-all-done.3 = bf16[8,8,1280]{2,1,0:T(8,128)(2,1)S(1)} async-done(((bf16[8,8,1280]{2,1,0:T(8,128)(2,1)}), bf16[8,8,1280]{2,1,0:T(8,128)(2,1)S(1)}, u32[]{:S(2)}, u32[]{:S(2)}) %all-to-all-start.3) | async-done | bytes 163872 | tf_op jit(solution)/shard_map/all_to_all | solution.py:217
  111.3 0.7 pad_maximum_fusion
  (36 shorter events, 2.8 us)
Async XLA Ops:
  0.6 0.7 copy-start.9
  2.7 17.0 %copy-start = (bf16[16,5120]{1,0:T(8,128)(2,1)S(1)}, bf16[16,5120]{1,0:T(8,128)(2,1)}, u32[]{:S(2)}) copy-start(bf16[16,5120]{1,0:T(8,128)(2,1)} %up_v.3) | copy-start | bytes 491524
  2.7 17.0 %copy-start.1 = (bf16[1,128,48]{2,1,0:T(8,128)(2,1)S(1)}, bf16[1,128,48]{2,1,0:T(8,128)(2,1)}, u32[]{:S(2)}) copy-start(bf16[1,128,48]{2,1,0:T(8,128)(2,1)} %copy.24.low) | copy-start | bytes 36868
  5.4 14.3 %collective-permute-start = (bf16[144,512]{1,0:T(8,128)(2,1)}, bf16[144,512]{1,0:T(8,128)(2,1)S(1)}, u32[]{:S(2)}, u32[]{:S(2)}) collective-permute-start(bf16[144,512]{1,0:T(8,128)(2,1)} %get-tuple-element.15.own), channel_id=1, source_target_pairs={{0,1},{1,2},{2,3},{3,4},{4,5},{5,6},{6,7},{7,8},{8,9},{9,10},{10,1... | collective-permute-start | bytes 442376 | tf_op jit(solution)/shard_map/ppermute | solution.py:258
  9.7 25.2 %collective-permute-start.3 = (bf16[144,512]{1,0:T(8,128)(2,1)}, bf16[144,512]{1,0:T(8,128)(2,1)S(1)}, u32[]{:S(2)}, u32[]{:S(2)}) collective-permute-start(bf16[144,512]{1,0:T(8,128)(2,1)} %get-tuple-element.15.own), channel_id=1, source_target_pairs={{0,3},{2,5},{4,7},{6,9},{8,11},{10,13},{12,15},{14,17},{16,19},{18... | collective-permute-start | bytes 442376 | tf_op jit(solution)/shard_map/ppermute | solution.py:258
  11.0 27.3 %collective-permute-start.2 = (bf16[144,512]{1,0:T(8,128)(2,1)}, bf16[144,512]{1,0:T(8,128)(2,1)S(1)}, u32[]{:S(2)}, u32[]{:S(2)}) collective-permute-start(bf16[144,512]{1,0:T(8,128)(2,1)} %get-tuple-element.15.own), channel_id=1, source_target_pairs={{0,2},{1,3},{2,4},{3,5},{4,6},{5,7},{6,8},{7,9},{8,10},{9,11},{10,... | collective-permute-start | bytes 442376 | tf_op jit(solution)/shard_map/ppermute | solution.py:258
  18.3 16.6 %collective-permute-start.1 = (bf16[144,512]{1,0:T(8,128)(2,1)}, bf16[144,512]{1,0:T(8,128)(2,1)S(1)}, u32[]{:S(2)}, u32[]{:S(2)}) collective-permute-start(bf16[144,512]{1,0:T(8,128)(2,1)} %get-tuple-element.14.own), channel_id=1, source_target_pairs={{0,1},{2,3},{4,5},{6,7},{8,9},{10,11},{12,13},{14,15},{16,17},{18,... | collective-permute-start | bytes 442376 | tf_op jit(solution)/shard_map/ppermute | solution.py:258
  19.6 0.7 copy-start.2
  20.3 1.2 %copy-start.3 = (bf16[1,128,4096]{2,1,0:T(8,128)(2,1)S(1)}, bf16[1,128,4096]{2,1,0:T(8,128)(2,1)}, u32[]{:S(2)}) copy-start(bf16[1,128,4096]{2,1,0:T(8,128)(2,1)} %query.3) | copy-start | bytes 3145732
  21.5 1.2 %copy-start.5 = (bf16[1,128,4096]{2,1,0:T(8,128)(2,1)S(1)}, bf16[1,128,4096]{2,1,0:T(8,128)(2,1)}, u32[]{:S(2)}) copy-start(bf16[1,128,4096]{2,1,0:T(8,128)(2,1)} %grad.3) | copy-start | bytes 3145732
  22.7 0.9 copy-start.8
  23.7 14.6 %copy-start.4 = (bf16[1,128,4096]{2,1,0:T(8,128)(2,1)S(1)}, bf16[1,128,4096]{2,1,0:T(8,128)(2,1)}, u32[]{:S(2)}) copy-start(bf16[1,128,4096]{2,1,0:T(8,128)(2,1)} %query.3) | copy-start | bytes 3145732
  23.7 14.6 %copy-start.6 = (bf16[1,128,4096]{2,1,0:T(8,128)(2,1)S(1)}, bf16[1,128,4096]{2,1,0:T(8,128)(2,1)}, u32[]{:S(2)}) copy-start(bf16[1,128,4096]{2,1,0:T(8,128)(2,1)} %grad.3) | copy-start | bytes 3145732
  23.7 14.6 %copy-start.7 = (bf16[144,512]{1,0:T(8,128)(2,1)S(1)}, bf16[144,512]{1,0:T(8,128)(2,1)}, u32[]{:S(2)}) copy-start(bf16[144,512]{1,0:T(8,128)(2,1)} %get-tuple-element.14.own) | copy-start | bytes 442372
  77.6 22.0 %all-to-all-start.2 = ((bf16[8,8,1280]{2,1,0:T(8,128)(2,1)}), bf16[8,8,1280]{2,1,0:T(8,128)(2,1)S(1)}, u32[]{:S(2)}, u32[]{:S(2)}) async-start(bf16[8,8,1280]{2,1,0:T(8,128)(2,1)} %broadcast_in_dim.14), calls=%async_computation.2 | async-start | bytes 327680 | tf_op jit(solution)/shard_map/all_to_all | solution.py:217
  81.9 22.0 %collective-permute-start.4 = (f32[32,128]{1,0:T(8,128)S(1)}, f32[32,128]{1,0:T(8,128)S(1)}, u32[]{:S(2)}, u32[]{:S(2)}) collective-permute-start(f32[32,128]{1,0:T(8,128)S(1)} %get-tuple-element.21), channel_id=1, source_target_pairs={{0,63},{1,0},{2,1},{3,2},{4,3},{5,4},{6,5},{7,6},{8,7},{9,8},{10,9... | collective-permute-start | bytes 49160 | tf_op jit(solution)/shard_map/ppermute | solution.py:258
  85.3 18.7 %collective-permute-start.5 = (f32[32,128]{1,0:T(8,128)S(1)}, f32[32,128]{1,0:T(8,128)S(1)}, u32[]{:S(2)}, u32[]{:S(2)}) collective-permute-start(f32[32,128]{1,0:T(8,128)S(1)} %get-tuple-element.22), channel_id=1, source_target_pairs={{0,62},{1,63},{2,0},{3,1},{4,2},{5,3},{6,4},{7,5},{8,6},{9,7},{10,... | collective-permute-start | bytes 49160 | tf_op jit(solution)/shard_map/ppermute | solution.py:258
  95.1 8.9 %collective-permute-start.6 = (f32[32,128]{1,0:T(8,128)S(1)}, f32[32,128]{1,0:T(8,128)S(1)}, u32[]{:S(2)}, u32[]{:S(2)}) collective-permute-start(f32[32,128]{1,0:T(8,128)S(1)} %get-tuple-element.23), channel_id=1, source_target_pairs={{1,62},{3,0},{5,2},{7,4},{9,6},{11,8},{13,10},{15,12},{17,14},{19,... | collective-permute-start | bytes 49160 | tf_op jit(solution)/shard_map/ppermute | solution.py:301
  100.4 10.8 %all-to-all-start.3 = ((bf16[8,8,1280]{2,1,0:T(8,128)(2,1)}), bf16[8,8,1280]{2,1,0:T(8,128)(2,1)S(1)}, u32[]{:S(2)}, u32[]{:S(2)}) async-start(bf16[8,8,1280]{2,1,0:T(8,128)(2,1)} %broadcast_in_dim.15), calls=%async_computation.3 | async-start | bytes 327680 | tf_op jit(solution)/shard_map/all_to_all | solution.py:217

commit v2 on v1

v2 whole, which is shorter than its diff:
```python
import functools
import math

import jax
import jax.numpy as jnp
from jax import lax
from jax.experimental import pallas as pl
from jax.experimental.pallas import tpu as pltpu
from jax.sharding import PartitionSpec as P

HEADS = 32
KV_HEADS = 4
D_HEAD = 128
RANK = 16
GROUP = 512
ROWS = 128
MESSAGE = ROWS + RANK
SHARE = HEADS // KV_HEADS
WIDE = SHARE * D_HEAD
TILES = SHARE + 2
PART = TILES // 2 * RANK
BACK = 2 * RANK
Z_RING = 8
BLOCKED = -1e30
F32 = jnp.float32
BF16 = jnp.bfloat16


def mul(a, b):
    return lax.dot_general(a, b, (((1,), (0,)), ((), ())), preferred_element_type=F32)


def mul_t(a, b):
    return lax.dot_general(a, b, (((1,), (1,)), ((), ())), preferred_element_type=F32)


def t_mul(a, b):
    return lax.dot_general(a, b, (((0,), (0,)), ((), ())), preferred_element_type=F32)


def prepare_kernel(frozen, low, up, light, heavy):
    low_k, low_v = low[0, RANK : 2 * RANK, :], low[0, 2 * RANK :, :]
    wide = KV_HEADS * D_HEAD
    keys = (frozen[0, :, :wide].astype(F32) + 2.0 * t_mul(low_k, up[:, :wide])).astype(BF16)
    values = (frozen[0, :, wide:].astype(F32) + 2.0 * t_mul(low_v, up[:, wide:])).astype(BF16)
    tail = jnp.concatenate([low_k, low_v, jnp.zeros((RANK, 2 * D_HEAD), BF16)], axis=1)
    half = 2 * D_HEAD

    def write(plain, moved):
        plain[:ROWS, :half] = keys[:, :half]
        plain[:ROWS, half:] = values[:, :half]
        plain[ROWS:, :] = tail
        moved[:ROWS, :half] = keys[:, half:]
        moved[:ROWS, half:] = values[:, half:]
        moved[ROWS:, :] = tail

    plain_light = lax.axis_index("ctx") % 4 < 2

    @pl.when(plain_light)
    def _():
        write(light, heavy)

    @pl.when(jnp.logical_not(plain_light))
    def _():
        write(heavy, light)


def stack_kernel(query, grad, low, up_q, queries, grads):
    found = (query[0].astype(F32) + 2.0 * t_mul(low[0, :RANK, :], up_q[...])).astype(BF16)
    for i in range(SHARE):
        rows, cols = slice(i * ROWS, (i + 1) * ROWS), slice(i * D_HEAD, (i + 1) * D_HEAD)
        queries[rows, :] = found[:, cols]
        grads[rows, :] = grad[0, :, cols]


def attend(place, query, grad, low, up_q, up_k, up_v, blocks, closed, attended, terms):
    head = pl.program_id(0)
    key_cols = pl.ds(pl.multiple_of(head * D_HEAD, D_HEAD), D_HEAD)
    value_cols = pl.ds(pl.multiple_of((head + 2) * D_HEAD, D_HEAD), D_HEAD)
    bias = jnp.where(place[1] == 1, 0.0, BLOCKED).astype(F32)
    scale = 1.0 / math.sqrt(D_HEAD)
    keys = jnp.concatenate([b(slice(0, ROWS), key_cols) for b in blocks], axis=0)
    values = jnp.concatenate([b(slice(0, ROWS), value_cols) for b in blocks], axis=0)
    tail = slice(ROWS, MESSAGE)
    low_k = jnp.concatenate([b(tail, slice(0, D_HEAD)) for b in blocks], axis=1)
    low_v = jnp.concatenate([b(tail, slice(D_HEAD, 2 * D_HEAD)) for b in blocks], axis=1)
    low_q = low[0, :RANK, :]
    keys_t = keys.T
    values_t = values.T
    up_rows = up_q[...]
    wide = 2 * ROWS
    row = lax.broadcasted_iota(jnp.int32, (ROWS, wide), 0)
    col = lax.broadcasted_iota(jnp.int32, (ROWS, wide), 1)
    causal = row <= jnp.where(col >= ROWS, col - ROWS, col)
    sides = [slice(h * D_HEAD, (h + 1) * D_HEAD) for h in range(SHARE)]
    all_queries = query[...]
    all_grads = grad[...]
    pairs = [slice(i * wide, (i + 1) * wide) for i in range(SHARE // 2)]
    products = [(mul_t(keys, all_queries[p]), mul_t(values, all_grads[p])) for p in pairs]
    all_weights, all_scores = [], []
    for logits, prob_grad in products:
        parts = [jnp.where(causal, logits[:ROWS], BLOCKED)]
        for i, shut in enumerate(closed):
            part = logits[(i + 1) * ROWS : (i + 2) * ROWS]
            parts.append(part + bias if shut else part)
        logits = jnp.concatenate(parts, axis=0)
        peak = jnp.max(logits, axis=0, keepdims=True)
        exps = jnp.exp2((logits - peak) * (scale * math.log2(math.e)))
        weights = (exps * (1.0 / jnp.sum(exps, axis=0, keepdims=True))).astype(BF16)
        weights_f = weights.astype(F32)
        product = weights_f * prob_grad
        row_dot = jnp.sum(product, axis=0, keepdims=True)
        all_weights.append(weights)
        all_scores.append((product - weights_f * row_dot).astype(BF16))
    grad_queries = []
    for i in range(SHARE // 2):
        out_t = mul(values_t, all_weights[i])
        grad_query_t = (mul(keys_t, all_scores[i]) * scale).astype(BF16)
        for k in range(2):
            mine = slice(k * ROWS, (k + 1) * ROWS)
            attended[0, :, sides[2 * i + k]] = out_t[:, mine].T.astype(BF16)
            grad_queries.append(grad_query_t[:, mine])
    stacked = jnp.concatenate(grad_queries, axis=0)
    low_grad = mul(up_rows, stacked)
    found = [2.0 * mul_t(low_q, stacked)]
    grad_keys = mul(jnp.concatenate(all_scores, axis=1), all_queries)
    grad_keys = (grad_keys * scale).astype(BF16)
    grad_values = mul(jnp.concatenate(all_weights, axis=1), all_grads).astype(BF16)
    found += [2.0 * mul(low_k, grad_keys), 2.0 * mul(low_v, grad_values)]
    found = jnp.concatenate(found, axis=1).astype(BF16)
    for tile in range(TILES):
        rows = slice(tile * RANK % PART, tile * RANK % PART + RANK)
        terms[tile * RANK // PART, rows, :] = found[:, tile * D_HEAD : (tile + 1) * D_HEAD]
    return 2.0 * low_grad, 2.0 * mul_t(up_k[...], grad_keys), 2.0 * mul_t(up_v[...], grad_values)


def light_kernel(place, query, grad, low, up_q, up_k, up_v, own, one, attended, terms, low_terms):
    blocks = [lambda r, c: own[r, c], lambda r, c: one[r, c]]
    by_query, by_key, by_value = attend(
        place, query, grad, low, up_q, up_k, up_v, blocks, [True], attended, terms
    )
    found = jnp.concatenate(
        [jnp.concatenate([by_query, jnp.zeros_like(by_query)], axis=1), by_key, by_value], axis=0
    )

    @pl.when(pl.program_id(0) == 0)
    def _():
        low_terms[...] = found

    @pl.when(pl.program_id(0) != 0)
    def _():
        low_terms[...] += found


def heavy_kernel(
    place, query, grad, low, up_q, up_k, up_v, own, one_even, one_odd, two, three, before,
    _attended, _terms, attended, terms, mine, back_one, back_two, back_three,
):
    odd = place[1] == 1
    blocks = [
        lambda r, c: own[r, c],
        lambda r, c: jnp.where(odd, one_odd[r, c], one_even[r, c]),
        lambda r, c: two[r, c],
        lambda r, c: three[r, c],
    ]

    @pl.when(pl.program_id(0) == 0)
    def _():
        mine[...] = before[:, :ROWS]
        back_one[...] = before[RANK:, ROWS:]
        back_two[...] = jnp.zeros_like(back_two)
        back_three[...] = jnp.zeros_like(back_three)

    by_query, by_key, by_value = attend(
        place, query, grad, low, up_q, up_k, up_v, blocks, [False, False, True], attended, terms
    )
    mine[:RANK, :] += by_query
    mine[RANK : 2 * RANK, :] += by_key[:, :ROWS]
    mine[2 * RANK :, :] += by_value[:, :ROWS]
    for i, back in enumerate((back_one, back_two, back_three)):
        block = slice((i + 1) * ROWS, (i + 2) * ROWS)
        back[:RANK, :] += by_key[:, block]
        back[RANK:, :] += by_value[:, block]


def whole(*shape):
    return pl.BlockSpec(shape, lambda head, place: (0,) * len(shape))


def at_half(rows, width, first=0):
    return pl.BlockSpec((rows, width), lambda head, place: (0, first + place[0] * 2 + head))


def wide_half():
    return pl.BlockSpec((1, ROWS, WIDE), lambda head, place: (0, 0, place[0] * 2 + head))


def term_half():
    return pl.BlockSpec((2, PART, D_HEAD), lambda head, place: (place[0] * 2 + head, 0, 0))


def common_specs():
    stacked = pl.BlockSpec((SHARE * ROWS, D_HEAD), lambda head, place: (place[0] * 2 + head, 0))
    return [
        stacked,
        stacked,
        whole(1, 3 * RANK, ROWS),
        at_half(RANK, WIDE),
        at_half(RANK, D_HEAD, HEADS),
        at_half(RANK, D_HEAD, HEADS + KV_HEADS),
    ]


def params():
    return pltpu.CompilerParams(
        dimension_semantics=("arbitrary",), vmem_limit_bytes=28 * 1024 * 1024
    )


def cost(blocks):
    sizes = 16 * blocks * ROWS * ROWS
    return pl.CostEstimate(
        flops=12 * sizes * D_HEAD, bytes_accessed=6 * ROWS * WIDE * 2, transcendentals=sizes
    )


def exchange(value, axis, groups=None):
    return lax.all_to_all(value, axis, 0, 0, axis_index_groups=groups)


def total(parts, rows):
    return jnp.sum(parts[:, :rows, :].astype(F32), axis=0).astype(BF16)


def along_kernel(spans, parts, back_one, back_two, back_three, out):
    rows = parts.shape[1]
    out[:, :rows, :] = jnp.broadcast_to(total(parts, rows), (Z_RING, rows, D_HEAD))
    out[:, rows:, :] = jnp.zeros((Z_RING, BACK, D_HEAD), BF16)
    place = lax.axis_index("ctx") % Z_RING
    for by, back in enumerate((back_one, back_two, back_three)):
        out[(place + Z_RING - 1 - by) % Z_RING, rows:, :] = back[...].astype(BF16)


def across_kernel(spans, parts, out, near):
    rows = parts.shape[1] - BACK
    place = lax.axis_index("ctx") % Z_RING
    ahead = jnp.zeros((BACK, D_HEAD), F32)
    behind = jnp.zeros((BACK, D_HEAD), F32)
    for i in range(Z_RING):
        came = parts[i, rows:, :].astype(F32)
        ahead = ahead + jnp.where(i > place, came, 0.0)
        behind = behind + jnp.where(i > place, 0.0, came)
    near[...] = ahead
    found = jnp.concatenate([total(parts, rows), behind.astype(BF16)], axis=0)
    out[...] = jnp.broadcast_to(found, out.shape)


def gather_kernel(spans, parts, near, mine, out, low_grad):
    rows = parts.shape[1] - BACK
    out[...] = jnp.broadcast_to(total(parts, rows), out.shape)
    after = (lax.axis_index("ctx") // Z_RING + 1) % (spans // Z_RING)
    low_grad[0, :RANK, :] = mine[:RANK, :]
    low_grad[0, RANK:, :] = mine[RANK:, :] + near[...] + parts[after, rows:, :].astype(F32)


def assemble_kernel(spans, parts, grad_up):
    for tile in range(KV_HEADS * TILES):
        head, inside = tile // TILES, tile % TILES
        column = head * SHARE + inside if inside < SHARE else HEADS + (inside - SHARE) * KV_HEADS + head
        rows = slice(inside * RANK % PART, inside * RANK % PART + RANK)
        grad_up[:, column * D_HEAD : (column + 1) * D_HEAD] = parts[
            2 * head + inside * RANK // PART, rows, :
        ].astype(F32)


def small(kernel, spans, name, out_shape, *operands):
    return pl.pallas_call(
        functools.partial(kernel, spans),
        out_shape=out_shape,
        compiler_params=pltpu.CompilerParams(vmem_limit_bytes=16 * 1024 * 1024),
        name=name,
    )(*operands)


def everywhere(terms, mine, backs):
    seqs, spans = lax.axis_size("dp"), lax.axis_size("ctx")
    along = [[first + i for i in range(Z_RING)] for first in range(0, spans, Z_RING)]
    across = [list(range(i, spans, Z_RING)) for i in range(Z_RING)]
    shape = terms.shape
    rows = shape[0] * shape[1] // seqs
    sent = lambda n, m: jax.ShapeDtypeStruct((n, m, D_HEAD), BF16)
    parts = exchange(terms.reshape(seqs, rows, D_HEAD), "dp")
    parts = small(along_kernel, spans, "along", sent(Z_RING, rows + BACK), parts, *backs)
    parts = exchange(parts, "ctx", along)
    near = jax.ShapeDtypeStruct((BACK, ROWS), F32)
    parts, near = small(across_kernel, spans, "across", (sent(spans // Z_RING, rows + BACK), near), parts)
    parts = exchange(parts, "ctx", across)
    low_grad = jax.ShapeDtypeStruct((1, 3 * RANK, ROWS), F32)
    parts, low_grad = small(
        gather_kernel, spans, "gather", (sent(seqs, rows), low_grad), parts, near, mine
    )
    parts = exchange(parts, "dp").reshape(shape)
    grad_up = jax.ShapeDtypeStruct((RANK, (HEADS + 2 * KV_HEADS) * D_HEAD), F32)
    return jnp.swapaxes(low_grad, 1, 2), small(assemble_kernel, spans, "assemble", grad_up, parts)


def shards(frozen_query, frozen_key_value, lowrank, adapter_up_weight, output_gradient):
    spans = lax.axis_size("ctx")
    position = lax.axis_index("ctx") % (GROUP // ROWS)
    light_half = position // 2
    odd = position % 2
    light_place = jnp.stack([light_half, odd]).astype(jnp.int32)
    heavy_place = jnp.stack([1 - light_half, odd]).astype(jnp.int32)
    message = jax.ShapeDtypeStruct((MESSAGE, 4 * D_HEAD), BF16)
    message_spec = whole(MESSAGE, 4 * D_HEAD)
    columns_first = jnp.swapaxes(lowrank, 1, 2)
    only = lambda *shape: pl.BlockSpec(shape, lambda i: (0,) * len(shape))
    light, heavy = pl.pallas_call(
        prepare_kernel,
        out_shape=(message, message),
        grid=(1,),
        in_specs=[
            only(1, ROWS, 8 * D_HEAD),
            only(1, 3 * RANK, ROWS),
            pl.BlockSpec((RANK, 8 * D_HEAD), lambda i: (0, HEADS // 8)),
        ],
        out_specs=[only(MESSAGE, 4 * D_HEAD)] * 2,
        compiler_params=pltpu.CompilerParams(vmem_limit_bytes=8 * 1024 * 1024),
        name="prepare",
    )(frozen_key_value, columns_first, adapter_up_weight)

    def send(value, by, step=1):
        return lax.ppermute(value, "ctx", [(i, (i + by) % spans) for i in range(0, spans, step)])

    one = send(light, 1)
    one_odd = send(heavy, 1, 2)
    two = send(one, 1)
    three = send(light, 3, 2)
    wide_out = jax.ShapeDtypeStruct((1, ROWS, HEADS * D_HEAD), BF16)
    terms_out = jax.ShapeDtypeStruct((2 * KV_HEADS, PART, D_HEAD), BF16)
    stacked_out = jax.ShapeDtypeStruct((HEADS * ROWS, D_HEAD), BF16)
    wide_block = pl.BlockSpec((1, ROWS, WIDE), lambda i: (0, 0, i))
    stacked_block = pl.BlockSpec((SHARE * ROWS, D_HEAD), lambda i: (i, 0))
    queries, grads = pl.pallas_call(
        stack_kernel,
        out_shape=(stacked_out, stacked_out),
        grid=(KV_HEADS,),
        in_specs=[
            wide_block,
            wide_block,
            only(1, 3 * RANK, ROWS),
            pl.BlockSpec((RANK, WIDE), lambda i: (0, i)),
        ],
        out_specs=[stacked_block, stacked_block],
        compiler_params=pltpu.CompilerParams(vmem_limit_bytes=16 * 1024 * 1024),
        cost_estimate=pl.CostEstimate(
            flops=2 * ROWS * RANK * WIDE * 4, bytes_accessed=16 * ROWS * WIDE * 2, transcendentals=0
        ),
        name="stack",
    )(frozen_query, output_gradient, columns_first, adapter_up_weight)
    arguments = (queries, grads, columns_first) + (adapter_up_weight,) * 3
    attended, terms, low_terms = pl.pallas_call(
        light_kernel,
        out_shape=(wide_out, terms_out, jax.ShapeDtypeStruct((3 * RANK, 2 * ROWS), F32)),
        grid_spec=pltpu.PrefetchScalarGridSpec(
            num_scalar_prefetch=1,
            grid=(2,),
            in_specs=common_specs() + [message_spec] * 2,
            out_specs=[wide_half(), term_half(), whole(3 * RANK, 2 * ROWS)],
        ),
        compiler_params=params(),
        cost_estimate=cost(2),
        name="light_heads",
    )(light_place, *arguments, light, one)
    back_out = jax.ShapeDtypeStruct((2 * RANK, ROWS), F32)
    back_spec = whole(2 * RANK, ROWS)
    attended, terms, mine, *backs = pl.pallas_call(
        heavy_kernel,
        out_shape=(wide_out, terms_out, jax.ShapeDtypeStruct((3 * RANK, ROWS), F32)) + (back_out,) * 3,
        grid_spec=pltpu.PrefetchScalarGridSpec(
            num_scalar_prefetch=1,
            grid=(2,),
            in_specs=common_specs()
            + [message_spec] * 5
            + [whole(3 * RANK, 2 * ROWS)]
            + [pl.BlockSpec(memory_space=pl.ANY)] * 2,
            out_specs=[wide_half(), term_half(), whole(3 * RANK, ROWS)] + [back_spec] * 3,
        ),
        input_output_aliases={13: 0, 14: 1},
        compiler_params=params(),
        cost_estimate=cost(4),
        name="heavy_heads",
    )(heavy_place, *arguments, heavy, one, one_odd, two, three, low_terms, attended, terms)
    grad_low, grad_up = everywhere(terms, mine, backs)
    return (attended, grad_low, grad_up)


def solution(mesh):
    return jax.shard_map(
        shards,
        mesh=mesh,
        in_specs=(
            P("dp", "ctx", None),
            P("dp", "ctx", None),
            P("dp", "ctx", None),
            P(),
            P("dp", "ctx", None),
        ),
        out_specs=(P("dp", "ctx", None), P("dp", "ctx", None), P()),
        check_vma=False,
    )
```

time: 113 us -> 104 us (0.920)
  the two profiles are of different devices: /device:TPU:64 before, /device:TPU:1 now
where the time goes in v2:
time: 104 us
  blocking collectives  55.5 us (53%)
  starting transfers between devices  16.9 us (16%)
  Pallas kernels  14.2 us (14%)
  waiting for transfers between devices  10.5 us (10%)
  local copies, waits for them, and re-layouts  5.69 us (5%)
    all_to_all x4, blocking collectives, exchange(): return lax.all_to_all(value, axis, 0, 0, axis_index_groups=groups)  55.5 us
    ppermute x4, starting transfers between devices, send(): lax.ppermute(value, 'ctx', [(i, (i + by) % spans) for i in range(0, spans...  16.9 us
    ppermute x4, waiting for transfers between devices, send(): lax.ppermute(value, 'ctx', [(i, (i + by) % spans) for i in range(0, spans...  10.5 us
    pallas_call x1, Pallas kernels, shards(): pl.pallas_call(heavy_kernel, out_shape=(wide_out, terms_out, jax.ShapeDty...  6.51 us
    unnamed x14, local copies, waits for them, and re-layouts  5.69 us
    pallas_call x1, Pallas kernels, shards(): pl.pallas_call(light_kernel, out_shape=(wide_out, terms_out, jax.ShapeDty...  4.69 us
  transfers between devices with their start and end apart: 4, of which 2 were waited for; matrix products, arithmetic and copies ran while one was open for 0% of the time, Pallas kernels for 6%

profile of v2, /device:TPU:1, one launch (start us, length us, event | category | flops | bytes accessed | tf_op | source)
XLA Modules:
  0.0 103.7 jit_solution(1404656885836551881)
XLA Ops:
  0.6 0.9 copy-done.2
  1.5 0.9 copy-done.4
  2.5 0.7 copy-done.5
  3.2 0.3 prepare.1
  3.5 4.8 %collective-permute-start = (bf16[144,512]{1,0:T(8,128)(2,1)S(1)}, bf16[144,512]{1,0:T(8,128)(2,1)S(1)}, u32[]{:S(2)}, u32[]{:S(2)}) collective-permute-start(bf16[144,512]{1,0:T(8,128)(2,1)S(1)} %get-tuple-element.23.own), channel_id=1, source_target_pairs={{0,1},{1,2},{2,3},{3,4},{4,5},{5,6},{6,7},{7,8},{8,9},{9,10},{10,1... | collective-permute-start | bytes 442376 | tf_op jit(solution)/shard_map/ppermute | solution.py:333
  8.3 8.8 %collective-permute-start.3 = (bf16[144,512]{1,0:T(8,128)(2,1)S(1)}, bf16[144,512]{1,0:T(8,128)(2,1)S(1)}, u32[]{:S(2)}, u32[]{:S(2)}) collective-permute-start(bf16[144,512]{1,0:T(8,128)(2,1)S(1)} %get-tuple-element.23.own), channel_id=1, source_target_pairs={{0,3},{2,5},{4,7},{6,9},{8,11},{10,13},{12,15},{14,17},{16,19},{18... | collective-permute-start | bytes 442376 | tf_op jit(solution)/shard_map/ppermute | solution.py:333
  17.2 1.3 %collective-permute-start.1 = (bf16[144,512]{1,0:T(8,128)(2,1)S(1)}, bf16[144,512]{1,0:T(8,128)(2,1)S(1)}, u32[]{:S(2)}, u32[]{:S(2)}) collective-permute-start(bf16[144,512]{1,0:T(8,128)(2,1)S(1)} %get-tuple-element.22.own), channel_id=1, source_target_pairs={{0,1},{2,3},{4,5},{6,7},{8,9},{10,11},{12,13},{14,15},{16,17},{18,... | collective-permute-start | bytes 442376 | tf_op jit(solution)/shard_map/ppermute | solution.py:333
  18.5 0.7 copy-done.6
  19.2 1.2 %copy-done = bf16[1,128,4096]{2,1,0:T(8,128)(2,1)S(1)} copy-done((bf16[1,128,4096]{2,1,0:T(8,128)(2,1)S(1)}, bf16[1,128,4096]{2,1,0:T(8,128)(2,1)}, u32[]{:S(2)}) %copy-start) | copy-done | bytes 1048600
  20.4 1.2 %copy-done.1 = bf16[1,128,4096]{2,1,0:T(8,128)(2,1)S(1)} copy-done((bf16[1,128,4096]{2,1,0:T(8,128)(2,1)S(1)}, bf16[1,128,4096]{2,1,0:T(8,128)(2,1)}, u32[]{:S(2)}) %copy-start.1) | copy-done | bytes 1048600
  21.7 1.3 %stack.22 = (bf16[4096,128]{1,0:T(8,128)(2,1)S(1)}, bf16[4096,128]{1,0:T(8,128)(2,1)S(1)}) custom-call(bf16[1,128,4096]{2,1,0:T(8,128)(2,1)S(1)} %copy-done, bf16[1,128,4096]{2,1,0:T(8,128)(2,1)S(1)} %copy-done.1, bf16[1,48,128]{2,1,0:T(8,128)(2,1)S(1)} %bitcast.6, bf16[16,5120]{1,0:T(8,128)(2,1)S(1)} %copy-done.3), custom_call_target="tpu_custom_call" | custom-call | flops 16777216 | bytes 4194304 | tf_op jit(solution)/shard_map/stack/pallas_call | solution.py:344
  22.9 0.1 pad_add_fusion.place
  23.0 3.2 %collective-permute-done.one.one_even = bf16[144,512]{1,0:T(8,128)(2,1)S(1)} collective-permute-done((bf16[144,512]{1,0:T(8,128)(2,1)S(1)}, bf16[144,512]{1,0:T(8,128)(2,1)S(1)}, u32[]{:S(2)}, u32[]{:S(2)}) %collective-permute-start) | collective-permute-done | bytes 147488 | tf_op jit(solution)/shard_map/ppermute | solution.py:333
  26.2 1.9 %collective-permute-start.2 = (bf16[144,512]{1,0:T(8,128)(2,1)S(1)}, bf16[144,512]{1,0:T(8,128)(2,1)S(1)}, u32[]{:S(2)}, u32[]{:S(2)}) collective-permute-start(bf16[144,512]{1,0:T(8,128)(2,1)S(1)} %collective-permute-done.one.one_even), channel_id=1, source_target_pairs={{0,1},{1,2},{2,3},{3,4},{4,5},{5,6},{6,7},{7,8},{8,9},{9,10},{10,1... | collective-permute-start | bytes 442376 | tf_op jit(solution)/shard_map/ppermute | solution.py:333
  28.1 0.1 pad_add_fusion.1.place
  28.2 4.7 %light_heads.1 = (bf16[1,128,4096]{2,1,0:T(8,128)(2,1)}, bf16[8,80,128]{2,1,0:T(8,128)(2,1)S(1)}, f32[48,256]{1,0:T(8,128)S(1)}) custom-call(s32[2]{0:T(128)S(1)} %pad_add_fusion.1.place, bf16[4096,128]{1,0:T(8,128)(2,1)S(1)} %get-tuple-element.20.query, bf16[4096,128]{1,0:T(8,128)(2,1)S(1)} %get-tuple-element.21.grad, bf16[1,48,128]{2,1,0:T(8,128)(2,1)S(1)} %bitcast.7, ...), custom_call_target="tpu_custom_call" | custom-call | flops 805306368 | bytes 1572864 | tf_op jit(solution)/shard_map/light_heads/pallas_call | solution.py:362
  32.9 7.3 %collective-permute-done.2.two = bf16[144,512]{1,0:T(8,128)(2,1)S(1)} collective-permute-done((bf16[144,512]{1,0:T(8,128)(2,1)S(1)}, bf16[144,512]{1,0:T(8,128)(2,1)S(1)}, u32[]{:S(2)}, u32[]{:S(2)}) %collective-permute-start.2) | collective-permute-done | bytes 147488 | tf_op jit(solution)/shard_map/ppermute | solution.py:333
  40.2 6.5 %heavy_heads.1 = (bf16[1,128,4096]{2,1,0:T(8,128)(2,1)}, bf16[8,80,128]{2,1,0:T(8,128)(2,1)S(1)}, f32[48,128]{1,0:T(8,128)S(1)}, f32[32,128]{1,0:T(8,128)S(1)}, ...) custom-call(s32[2]{0:T(128)S(1)} %pad_add_fusion.place, ...), custom_call_target="tpu_custom_call", output_to_operand_aliasing={{0}: (13, {}), {1}: (14, {})} | custom-call | flops 1610612736 | bytes 1572864 | tf_op jit(solution)/shard_map/heavy_heads/pallas_call | solution.py:377
  46.7 17.1 %all_to_all.20.parts = bf16[8,80,128]{2,1,0:T(8,128)(2,1)S(1)} all-to-all(bf16[8,80,128]{2,1,0:T(8,128)(2,1)S(1)} %get-tuple-element.28), channel_id=1, replica_groups=mesh['dp'=8,'ctx'=64] {'dp'}, dimensions={0} | all-to-all | bytes 327680 | tf_op jit(solution)/shard_map/all_to_all | solution.py:228
  63.9 11.8 %all_to_all.21.parts = bf16[8,112,128]{2,1,0:T(8,128)(2,1)S(1)} all-to-all(bf16[8,112,128]{2,1,0:T(8,128)(2,1)S(1)} %along.1), channel_id=1, replica_groups={{0,1,2,3,4,5,6,7},{8,9,10,11,12,13,14,15},{16,17,18,19,20,21,22,23},{24..., dimensions={0} | all-to-all | bytes 458752 | tf_op jit(solution)/shard_map/all_to_all | solution.py:228
  75.8 12.3 %all_to_all.22.parts = bf16[8,112,128]{2,1,0:T(8,128)(2,1)S(1)} all-to-all(bf16[8,112,128]{2,1,0:T(8,128)(2,1)S(1)} %get-tuple-element.32), channel_id=1, replica_groups={{0,8,16,24,32,40,48,56},{1,9,17,25,33,41,49,57},{2,10,18,26,34,42,50,58..., dimensions={0} | all-to-all | bytes 458752 | tf_op jit(solution)/shard_map/all_to_all | solution.py:228
  88.0 0.6 gather.1
  88.7 14.3 %all_to_all.23.parts = bf16[8,80,128]{2,1,0:T(8,128)(2,1)S(1)} all-to-all(bf16[8,80,128]{2,1,0:T(8,128)(2,1)S(1)} %get-tuple-element.36), channel_id=1, replica_groups=mesh['dp'=8,'ctx'=64] {'dp'}, dimensions={0} | all-to-all | bytes 327680 | tf_op jit(solution)/shard_map/all_to_all | solution.py:228
  102.9 0.7 assemble.1
  (12 shorter events, 0.1 us)
Async XLA Ops:
  0.6 0.9 copy-start.2
  1.5 0.9 copy-start.4
  2.5 0.7 copy-start.5
  3.2 15.3 %copy-start.3 = (bf16[16,5120]{1,0:T(8,128)(2,1)S(1)}, bf16[16,5120]{1,0:T(8,128)(2,1)}, u32[]{:S(2)}) copy-start(bf16[16,5120]{1,0:T(8,128)(2,1)} %up_v.3) | copy-start | bytes 491524
  3.5 22.7 %collective-permute-start = (bf16[144,512]{1,0:T(8,128)(2,1)S(1)}, bf16[144,512]{1,0:T(8,128)(2,1)S(1)}, u32[]{:S(2)}, u32[]{:S(2)}) collective-permute-start(bf16[144,512]{1,0:T(8,128)(2,1)S(1)} %get-tuple-element.23.own), channel_id=1, source_target_pairs={{0,1},{1,2},{2,3},{3,4},{4,5},{5,6},{6,7},{7,8},{8,9},{9,10},{10,1... | collective-permute-start | bytes 442376 | tf_op jit(solution)/shard_map/ppermute | solution.py:333
  8.3 24.5 %collective-permute-start.3 = (bf16[144,512]{1,0:T(8,128)(2,1)S(1)}, bf16[144,512]{1,0:T(8,128)(2,1)S(1)}, u32[]{:S(2)}, u32[]{:S(2)}) collective-permute-start(bf16[144,512]{1,0:T(8,128)(2,1)S(1)} %get-tuple-element.23.own), channel_id=1, source_target_pairs={{0,3},{2,5},{4,7},{6,9},{8,11},{10,13},{12,15},{14,17},{16,19},{18... | collective-permute-start | bytes 442376 | tf_op jit(solution)/shard_map/ppermute | solution.py:333
  17.2 15.7 %collective-permute-start.1 = (bf16[144,512]{1,0:T(8,128)(2,1)S(1)}, bf16[144,512]{1,0:T(8,128)(2,1)S(1)}, u32[]{:S(2)}, u32[]{:S(2)}) collective-permute-start(bf16[144,512]{1,0:T(8,128)(2,1)S(1)} %get-tuple-element.22.own), channel_id=1, source_target_pairs={{0,1},{2,3},{4,5},{6,7},{8,9},{10,11},{12,13},{14,15},{16,17},{18,... | collective-permute-start | bytes 442376 | tf_op jit(solution)/shard_map/ppermute | solution.py:333
  18.5 0.7 copy-start.6
  19.2 1.2 %copy-start = (bf16[1,128,4096]{2,1,0:T(8,128)(2,1)S(1)}, bf16[1,128,4096]{2,1,0:T(8,128)(2,1)}, u32[]{:S(2)}) copy-start(bf16[1,128,4096]{2,1,0:T(8,128)(2,1)} %query.1) | copy-start | bytes 3145732
  20.4 1.2 %copy-start.1 = (bf16[1,128,4096]{2,1,0:T(8,128)(2,1)S(1)}, bf16[1,128,4096]{2,1,0:T(8,128)(2,1)}, u32[]{:S(2)}) copy-start(bf16[1,128,4096]{2,1,0:T(8,128)(2,1)} %grad.1) | copy-start | bytes 3145732
  26.2 14.0 %collective-permute-start.2 = (bf16[144,512]{1,0:T(8,128)(2,1)S(1)}, bf16[144,512]{1,0:T(8,128)(2,1)S(1)}, u32[]{:S(2)}, u32[]{:S(2)}) collective-permute-start(bf16[144,512]{1,0:T(8,128)(2,1)S(1)} %collective-permute-done.one.one_even), channel_id=1, source_target_pairs={{0,1},{1,2},{2,3},{3,4},{4,5},{5,6},{6,7},{7,8},{8,9},{9,10},{10,1... | collective-permute-start | bytes 442376 | tf_op jit(solution)/shard_map/ppermute | solution.py:333

commit v3 on v2

--- a/solution.py
+++ b/solution.py
@@ -153,14 +153,14 @@
 
 
 def heavy_kernel(
-    place, query, grad, low, up_q, up_k, up_v, own, one_even, one_odd, two, three, before,
+    place, query, grad, low, up_q, up_k, up_v, own, one_even, one_odd, two_even, two_odd, three, before,
     _attended, _terms, attended, terms, mine, back_one, back_two, back_three,
 ):
     odd = place[1] == 1
     blocks = [
         lambda r, c: own[r, c],
         lambda r, c: jnp.where(odd, one_odd[r, c], one_even[r, c]),
-        lambda r, c: two[r, c],
+        lambda r, c: jnp.where(odd, two_odd[r, c], two_even[r, c]),
         lambda r, c: three[r, c],
     ]
 
@@ -325,7 +325,7 @@
             pl.BlockSpec((RANK, 8 * D_HEAD), lambda i: (0, HEADS // 8)),
         ],
         out_specs=[only(MESSAGE, 4 * D_HEAD)] * 2,
-        compiler_params=pltpu.CompilerParams(vmem_limit_bytes=8 * 1024 * 1024),
+        compiler_params=pltpu.CompilerParams(vmem_limit_bytes=56 * 1024 * 1024),
         name="prepare",
     )(frozen_key_value, columns_first, adapter_up_weight)
 
@@ -333,9 +333,10 @@
         return lax.ppermute(value, "ctx", [(i, (i + by) % spans) for i in range(0, spans, step)])
 
     one = send(light, 1)
+    two_even = send(light, 2, 2)
     one_odd = send(heavy, 1, 2)
-    two = send(one, 1)
-    three = send(light, 3, 2)
+    two_odd = send(one, 1, 2)
+    three = send(two_even, 1, 2)
     wide_out = jax.ShapeDtypeStruct((1, ROWS, HEADS * D_HEAD), BF16)
     terms_out = jax.ShapeDtypeStruct((2 * KV_HEADS, PART, D_HEAD), BF16)
     stacked_out = jax.ShapeDtypeStruct((HEADS * ROWS, D_HEAD), BF16)
@@ -381,16 +382,16 @@
             num_scalar_prefetch=1,
             grid=(2,),
             in_specs=common_specs()
-            + [message_spec] * 5
+            + [message_spec] * 6
             + [whole(3 * RANK, 2 * ROWS)]
             + [pl.BlockSpec(memory_space=pl.ANY)] * 2,
             out_specs=[wide_half(), term_half(), whole(3 * RANK, ROWS)] + [back_spec] * 3,
         ),
-        input_output_aliases={13: 0, 14: 1},
+        input_output_aliases={14: 0, 15: 1},
         compiler_params=params(),
         cost_estimate=cost(4),
         name="heavy_heads",
-    )(heavy_place, *arguments, heavy, one, one_odd, two, three, low_terms, attended, terms)
+    )(heavy_place, *arguments, heavy, one, one_odd, two_even, two_odd, three, low_terms, attended, terms)
     grad_low, grad_up = everywhere(terms, mine, backs)
     return (attended, grad_low, grad_up)
 

time: 104 us -> 95.6 us (0.919)
  waiting for transfers between devices: 10.5 us -> 4.34 us
  blocking collectives: 55.5 us -> 52.3 us
  local copies, waits for them, and re-layouts: 5.69 us -> 3.14 us
  Pallas kernels: 14.2 us -> 15.9 us
  starting transfers between devices: 16.9 us -> 18.4 us
    ppermute x4 -> x5, waiting for transfers between devices: 10.5 us -> 4.34 us  [send(): lax.ppermute(value, 'ctx', [(i, (i + by) % spans) for i in range(0, spans...]
    all_to_all x4, blocking collectives: 55.5 us -> 52.3 us  [exchange(): return lax.all_to_all(value, axis, 0, 0, axis_index_groups=groups)]
    unnamed x14 -> x12, local copies, waits for them, and re-layouts: 5.69 us -> 3.14 us
    pallas_call x1, Pallas kernels: 0.28 us -> 1.99 us  [shards(): pl.pallas_call(prepare_kernel, out_shape=(message, message), grid=(1,), i...]
    ppermute x4 -> x5, starting transfers between devices: 16.9 us -> 18.4 us  [send(): lax.ppermute(value, 'ctx', [(i, (i + by) % spans) for i in range(0, spans...]
  transfers between devices with their start and end apart: 4 -> 5, of which waited for: 2 -> 1; matrix products, arithmetic and copies ran while one was open for 0% -> 0% of each run, Pallas kernels for 6% -> 6%
where the time goes in v3:
time: 95.6 us; the launch traced here: 95.1 us
  blocking collectives  52.3 us (55%)
  starting transfers between devices  18.4 us (19%)
  Pallas kernels  15.9 us (17%)
  waiting for transfers between devices  4.34 us (5%)
  local copies, waits for them, and re-layouts  3.14 us (3%)
    all_to_all x4, blocking collectives, exchange(): return lax.all_to_all(value, axis, 0, 0, axis_index_groups=groups)  52.3 us
    ppermute x5, starting transfers between devices, send(): lax.ppermute(value, 'ctx', [(i, (i + by) % spans) for i in range(0, spans...  18.4 us
    pallas_call x1, Pallas kernels, shards(): pl.pallas_call(heavy_kernel, out_shape=(wide_out, terms_out, jax.ShapeDty...  6.53 us
    pallas_call x1, Pallas kernels, shards(): pl.pallas_call(light_kernel, out_shape=(wide_out, terms_out, jax.ShapeDty...  4.69 us
    ppermute x5, waiting for transfers between devices, send(): lax.ppermute(value, 'ctx', [(i, (i + by) % spans) for i in range(0, spans...  4.34 us
    unnamed x12, local copies, waits for them, and re-layouts  3.14 us
    pallas_call x1, Pallas kernels, shards(): pl.pallas_call(prepare_kernel, out_shape=(message, message), grid=(1,), i...  1.99 us
  transfers between devices with their start and end apart: 5, of which 1 were waited for; matrix products, arithmetic and copies ran while one was open for 0% of the time, Pallas kernels for 6%

profile of v3, /device:TPU:1, one launch (start us, length us, event | category | flops | bytes accessed | tf_op | source)
XLA Modules:
  0.0 95.1 jit_solution(10771833849569335687)
XLA Ops:
  0.6 2.0 %prepare.1 = (bf16[144,512]{1,0:T(8,128)(2,1)}, bf16[144,512]{1,0:T(8,128)(2,1)}) custom-call(bf16[1,128,1024]{2,1,0:T(8,128)(2,1)} %frozen.1, bf16[1,48,128]{2,1,0:T(8,128)(2,1)} %bitcast.5, bf16[16,5120]{1,0:T(8,128)(2,1)} %up_v.3), custom_call_target="tpu_custom_call" | custom-call | tf_op jit(solution)/shard_map/prepare/pallas_call | solution.py:318
  2.6 6.6 %collective-permute-start.2 = (bf16[144,512]{1,0:T(8,128)(2,1)}, bf16[144,512]{1,0:T(8,128)(2,1)S(1)}, u32[]{:S(2)}, u32[]{:S(2)}) collective-permute-start(bf16[144,512]{1,0:T(8,128)(2,1)} %get-tuple-element.23.own), channel_id=1, source_target_pairs={{0,2},{2,4},{4,6},{6,8},{8,10},{10,12},{12,14},{14,16},{16,18},{18... | collective-permute-start | bytes 442376 | tf_op jit(solution)/shard_map/ppermute | solution.py:333
  9.3 1.9 %collective-permute-start = (bf16[144,512]{1,0:T(8,128)(2,1)}, bf16[144,512]{1,0:T(8,128)(2,1)S(1)}, u32[]{:S(2)}, u32[]{:S(2)}) collective-permute-start(bf16[144,512]{1,0:T(8,128)(2,1)} %get-tuple-element.23.own), channel_id=1, source_target_pairs={{0,1},{1,2},{2,3},{3,4},{4,5},{5,6},{6,7},{7,8},{8,9},{9,10},{10,1... | collective-permute-start | bytes 442376 | tf_op jit(solution)/shard_map/ppermute | solution.py:333
  11.2 7.3 %collective-permute-start.1 = (bf16[144,512]{1,0:T(8,128)(2,1)}, bf16[144,512]{1,0:T(8,128)(2,1)S(1)}, u32[]{:S(2)}, u32[]{:S(2)}) collective-permute-start(bf16[144,512]{1,0:T(8,128)(2,1)} %get-tuple-element.22.own), channel_id=1, source_target_pairs={{0,1},{2,3},{4,5},{6,7},{8,9},{10,11},{12,13},{14,15},{16,17},{18,... | collective-permute-start | bytes 442376 | tf_op jit(solution)/shard_map/ppermute | solution.py:333
  18.5 0.0 copy-start.3
  18.6 0.7 copy-done.3
  19.2 1.2 %copy-done = bf16[1,128,4096]{2,1,0:T(8,128)(2,1)S(1)} copy-done((bf16[1,128,4096]{2,1,0:T(8,128)(2,1)S(1)}, bf16[1,128,4096]{2,1,0:T(8,128)(2,1)}, u32[]{:S(2)}) %copy-start) | copy-done | bytes 1048600
  20.5 1.2 %copy-done.1 = bf16[1,128,4096]{2,1,0:T(8,128)(2,1)S(1)} copy-done((bf16[1,128,4096]{2,1,0:T(8,128)(2,1)S(1)}, bf16[1,128,4096]{2,1,0:T(8,128)(2,1)}, u32[]{:S(2)}) %copy-start.1) | copy-done | bytes 1048600
  21.7 1.3 %stack.22 = (bf16[4096,128]{1,0:T(8,128)(2,1)S(1)}, bf16[4096,128]{1,0:T(8,128)(2,1)S(1)}) custom-call(bf16[1,128,4096]{2,1,0:T(8,128)(2,1)S(1)} %copy-done, bf16[1,128,4096]{2,1,0:T(8,128)(2,1)S(1)} %copy-done.1, bf16[1,48,128]{2,1,0:T(8,128)(2,1)S(1)} %bitcast.6, bf16[16,5120]{1,0:T(8,128)(2,1)S(1)} %copy-done.2), custom_call_target="tpu_custom_call" | custom-call | flops 16777216 | bytes 4194304 | tf_op jit(solution)/shard_map/stack/pallas_call | solution.py:345
  23.0 0.1 pad_add_fusion.place
  23.0 4.3 %collective-permute-done.2.two_even = bf16[144,512]{1,0:T(8,128)(2,1)S(1)} collective-permute-done((bf16[144,512]{1,0:T(8,128)(2,1)}, bf16[144,512]{1,0:T(8,128)(2,1)S(1)}, u32[]{:S(2)}, u32[]{:S(2)}) %collective-permute-start.2) | collective-permute-done | bytes 147488 | tf_op jit(solution)/shard_map/ppermute | solution.py:333
  27.4 1.3 %collective-permute-start.4 = (bf16[144,512]{1,0:T(8,128)(2,1)S(1)}, bf16[144,512]{1,0:T(8,128)(2,1)S(1)}, u32[]{:S(2)}, u32[]{:S(2)}) collective-permute-start(bf16[144,512]{1,0:T(8,128)(2,1)S(1)} %collective-permute-done.2.two_even), channel_id=1, source_target_pairs={{0,1},{2,3},{4,5},{6,7},{8,9},{10,11},{12,13},{14,15},{16,17},{18,... | collective-permute-start | bytes 442376 | tf_op jit(solution)/shard_map/ppermute | solution.py:333
  28.7 0.0 collective-permute-done.one.one_even
  28.7 1.3 %collective-permute-start.3 = (bf16[144,512]{1,0:T(8,128)(2,1)S(1)}, bf16[144,512]{1,0:T(8,128)(2,1)S(1)}, u32[]{:S(2)}, u32[]{:S(2)}) collective-permute-start(bf16[144,512]{1,0:T(8,128)(2,1)S(1)} %collective-permute-done.one.one_even), channel_id=1, source_target_pairs={{0,1},{2,3},{4,5},{6,7},{8,9},{10,11},{12,13},{14,15},{16,17},{18,... | collective-permute-start | bytes 442376 | tf_op jit(solution)/shard_map/ppermute | solution.py:333
  30.0 0.1 pad_add_fusion.1.place
  30.1 4.7 %light_heads.1 = (bf16[1,128,4096]{2,1,0:T(8,128)(2,1)}, bf16[8,80,128]{2,1,0:T(8,128)(2,1)S(1)}, f32[48,256]{1,0:T(8,128)S(1)}) custom-call(s32[2]{0:T(128)S(1)} %pad_add_fusion.1.place, bf16[4096,128]{1,0:T(8,128)(2,1)S(1)} %get-tuple-element.20.query, bf16[4096,128]{1,0:T(8,128)(2,1)S(1)} %get-tuple-element.21.grad, bf16[1,48,128]{2,1,0:T(8,128)(2,1)S(1)} %bitcast.7, ...), custom_call_target="tpu_custom_call" | custom-call | flops 805306368 | bytes 1572864 | tf_op jit(solution)/shard_map/light_heads/pallas_call | solution.py:363
  34.8 6.5 %heavy_heads.1 = (bf16[1,128,4096]{2,1,0:T(8,128)(2,1)}, bf16[8,80,128]{2,1,0:T(8,128)(2,1)S(1)}, f32[48,128]{1,0:T(8,128)S(1)}, f32[32,128]{1,0:T(8,128)S(1)}, ...) custom-call(s32[2]{0:T(128)S(1)} %pad_add_fusion.place, ...), custom_call_target="tpu_custom_call", output_to_operand_aliasing={{0}: (14, {}), {1}: (15, {})} | custom-call | flops 1610612736 | bytes 1572864 | tf_op jit(solution)/shard_map/heavy_heads/pallas_call | solution.py:378
  41.3 12.0 %all_to_all.20.parts = bf16[8,80,128]{2,1,0:T(8,128)(2,1)S(1)} all-to-all(bf16[8,80,128]{2,1,0:T(8,128)(2,1)S(1)} %get-tuple-element.28), channel_id=1, replica_groups=mesh['dp'=8,'ctx'=64] {'dp'}, dimensions={0} | all-to-all | bytes 327680 | tf_op jit(solution)/shard_map/all_to_all | solution.py:228
  53.4 12.4 %all_to_all.21.parts = bf16[8,112,128]{2,1,0:T(8,128)(2,1)S(1)} all-to-all(bf16[8,112,128]{2,1,0:T(8,128)(2,1)S(1)} %along.1), channel_id=1, replica_groups={{0,1,2,3,4,5,6,7},{8,9,10,11,12,13,14,15},{16,17,18,19,20,21,22,23},{24..., dimensions={0} | all-to-all | bytes 458752 | tf_op jit(solution)/shard_map/all_to_all | solution.py:228
  65.8 0.1 across.1
  65.9 13.8 %all_to_all.22.parts = bf16[8,112,128]{2,1,0:T(8,128)(2,1)S(1)} all-to-all(bf16[8,112,128]{2,1,0:T(8,128)(2,1)S(1)} %get-tuple-element.32), channel_id=1, replica_groups={{0,8,16,24,32,40,48,56},{1,9,17,25,33,41,49,57},{2,10,18,26,34,42,50,58..., dimensions={0} | all-to-all | bytes 458752 | tf_op jit(solution)/shard_map/all_to_all | solution.py:228
  79.7 0.6 gather.1
  80.3 14.0 %all_to_all.23.parts = bf16[8,80,128]{2,1,0:T(8,128)(2,1)S(1)} all-to-all(bf16[8,80,128]{2,1,0:T(8,128)(2,1)S(1)} %get-tuple-element.36), channel_id=1, replica_groups=mesh['dp'=8,'ctx'=64] {'dp'}, dimensions={0} | all-to-all | bytes 327680 | tf_op jit(solution)/shard_map/all_to_all | solution.py:228
  94.3 0.7 assemble.1
  (12 shorter events, 0.1 us)
Async XLA Ops:
  0.6 17.9 %copy-start.2 = (bf16[16,5120]{1,0:T(8,128)(2,1)S(1)}, bf16[16,5120]{1,0:T(8,128)(2,1)}, u32[]{:S(2)}) copy-start(bf16[16,5120]{1,0:T(8,128)(2,1)} %up_v.3) | copy-start | bytes 491524
  2.6 24.7 %collective-permute-start.2 = (bf16[144,512]{1,0:T(8,128)(2,1)}, bf16[144,512]{1,0:T(8,128)(2,1)S(1)}, u32[]{:S(2)}, u32[]{:S(2)}) collective-permute-start(bf16[144,512]{1,0:T(8,128)(2,1)} %get-tuple-element.23.own), channel_id=1, source_target_pairs={{0,2},{2,4},{4,6},{6,8},{8,10},{10,12},{12,14},{14,16},{16,18},{18... | collective-permute-start | bytes 442376 | tf_op jit(solution)/shard_map/ppermute | solution.py:333
  9.3 19.4 %collective-permute-start = (bf16[144,512]{1,0:T(8,128)(2,1)}, bf16[144,512]{1,0:T(8,128)(2,1)S(1)}, u32[]{:S(2)}, u32[]{:S(2)}) collective-permute-start(bf16[144,512]{1,0:T(8,128)(2,1)} %get-tuple-element.23.own), channel_id=1, source_target_pairs={{0,1},{1,2},{2,3},{3,4},{4,5},{5,6},{6,7},{7,8},{8,9},{9,10},{10,1... | collective-permute-start | bytes 442376 | tf_op jit(solution)/shard_map/ppermute | solution.py:333
  11.2 23.6 %collective-permute-start.1 = (bf16[144,512]{1,0:T(8,128)(2,1)}, bf16[144,512]{1,0:T(8,128)(2,1)S(1)}, u32[]{:S(2)}, u32[]{:S(2)}) collective-permute-start(bf16[144,512]{1,0:T(8,128)(2,1)} %get-tuple-element.22.own), channel_id=1, source_target_pairs={{0,1},{2,3},{4,5},{6,7},{8,9},{10,11},{12,13},{14,15},{16,17},{18,... | collective-permute-start | bytes 442376 | tf_op jit(solution)/shard_map/ppermute | solution.py:333
  18.5 0.7 copy-start.3
  19.2 1.2 %copy-start = (bf16[1,128,4096]{2,1,0:T(8,128)(2,1)S(1)}, bf16[1,128,4096]{2,1,0:T(8,128)(2,1)}, u32[]{:S(2)}) copy-start(bf16[1,128,4096]{2,1,0:T(8,128)(2,1)} %query.1) | copy-start | bytes 3145732
  20.4 1.2 %copy-start.1 = (bf16[1,128,4096]{2,1,0:T(8,128)(2,1)S(1)}, bf16[1,128,4096]{2,1,0:T(8,128)(2,1)}, u32[]{:S(2)}) copy-start(bf16[1,128,4096]{2,1,0:T(8,128)(2,1)} %grad.1) | copy-start | bytes 3145732
  21.7 8.4 %copy-start.5 = (bf16[144,512]{1,0:T(8,128)(2,1)S(1)}, bf16[144,512]{1,0:T(8,128)(2,1)}, u32[]{:S(2)}) copy-start(bf16[144,512]{1,0:T(8,128)(2,1)} %get-tuple-element.23.own) | copy-start | bytes 442372
  27.4 7.4 %collective-permute-start.4 = (bf16[144,512]{1,0:T(8,128)(2,1)S(1)}, bf16[144,512]{1,0:T(8,128)(2,1)S(1)}, u32[]{:S(2)}, u32[]{:S(2)}) collective-permute-start(bf16[144,512]{1,0:T(8,128)(2,1)S(1)} %collective-permute-done.2.two_even), channel_id=1, source_target_pairs={{0,1},{2,3},{4,5},{6,7},{8,9},{10,11},{12,13},{14,15},{16,17},{18,... | collective-permute-start | bytes 442376 | tf_op jit(solution)/shard_map/ppermute | solution.py:333
  28.7 6.1 %collective-permute-start.3 = (bf16[144,512]{1,0:T(8,128)(2,1)S(1)}, bf16[144,512]{1,0:T(8,128)(2,1)S(1)}, u32[]{:S(2)}, u32[]{:S(2)}) collective-permute-start(bf16[144,512]{1,0:T(8,128)(2,1)S(1)} %collective-permute-done.one.one_even), channel_id=1, source_target_pairs={{0,1},{2,3},{4,5},{6,7},{8,9},{10,11},{12,13},{14,15},{16,17},{18,... | collective-permute-start | bytes 442376 | tf_op jit(solution)/shard_map/ppermute | solution.py:333
  30.1 4.7 %copy-start.4 = (bf16[144,512]{1,0:T(8,128)(2,1)S(1)}, bf16[144,512]{1,0:T(8,128)(2,1)}, u32[]{:S(2)}) copy-start(bf16[144,512]{1,0:T(8,128)(2,1)} %get-tuple-element.22.own) | copy-start | bytes 442372

commit v4 on v3

--- a/solution.py
+++ b/solution.py
@@ -1,4 +1,3 @@
-import functools
 import math
 
 import jax
@@ -20,7 +19,8 @@
 TILES = SHARE + 2
 PART = TILES // 2 * RANK
 BACK = 2 * RANK
-Z_RING = 8
+X_SIZE, Y_LOW, Z_SIZE, CORES = 4, 4, 8, 2
+Y_SIZE = 2 * Y_LOW
 BLOCKED = -1e30
 F32 = jnp.float32
 BF16 = jnp.bfloat16
@@ -224,46 +224,62 @@
     )
 
 
-def exchange(value, axis, groups=None):
-    return lax.all_to_all(value, axis, 0, 0, axis_index_groups=groups)
+def exchange(value, groups):
+    return lax.all_to_all(value, ("dp", "ctx"), 0, 0, axis_index_groups=groups)
+
+
+def index_of(x, y, z, core):
+    dp = y % Y_LOW * CORES + core
+    return dp * (2 * X_SIZE * Z_SIZE) + (x * 2 + y // Y_LOW) * Z_SIZE + z
+
+
+def lines():
+    xs, ys, zs, cores = range(X_SIZE), range(Y_SIZE), range(Z_SIZE), range(CORES)
+    by_x = [[index_of(x, y, z, c) for x in xs for c in cores] for y in ys for z in zs]
+    by_z = [[index_of(x, y, z, c) for z in zs] for x in xs for y in ys for c in cores]
+    by_y = [[index_of(x, y, z, c) for y in ys] for x in xs for z in zs for c in cores]
+    return by_x, by_z, by_y
 
 
 def total(parts, rows):
     return jnp.sum(parts[:, :rows, :].astype(F32), axis=0).astype(BF16)
 
 
-def along_kernel(spans, parts, back_one, back_two, back_three, out):
+def along_kernel(parts, back_one, back_two, back_three, out):
     rows = parts.shape[1]
-    out[:, :rows, :] = jnp.broadcast_to(total(parts, rows), (Z_RING, rows, D_HEAD))
-    out[:, rows:, :] = jnp.zeros((Z_RING, BACK, D_HEAD), BF16)
-    place = lax.axis_index("ctx") % Z_RING
+    out[:, :rows, :] = jnp.broadcast_to(total(parts, rows), (Z_SIZE, rows, D_HEAD))
+    out[:, rows:, :] = jnp.zeros((Z_SIZE, BACK, D_HEAD), BF16)
+    z = lax.axis_index("ctx") % Z_SIZE
     for by, back in enumerate((back_one, back_two, back_three)):
-        out[(place + Z_RING - 1 - by) % Z_RING, rows:, :] = back[...].astype(BF16)
-
-
-def across_kernel(spans, parts, out, near):
+        out[(z + Z_SIZE - 1 - by) % Z_SIZE, rows:, :] = back[...].astype(BF16)
+
+
+def beside_kernel(parts, out, near):
     rows = parts.shape[1] - BACK
-    place = lax.axis_index("ctx") % Z_RING
+    z = lax.axis_index("ctx") % Z_SIZE
     ahead = jnp.zeros((BACK, D_HEAD), F32)
     behind = jnp.zeros((BACK, D_HEAD), F32)
-    for i in range(Z_RING):
+    for i in range(Z_SIZE):
         came = parts[i, rows:, :].astype(F32)
-        ahead = ahead + jnp.where(i > place, came, 0.0)
-        behind = behind + jnp.where(i > place, 0.0, came)
+        ahead = ahead + jnp.where(i > z, came, 0.0)
+        behind = behind + jnp.where(i > z, 0.0, came)
     near[...] = ahead
     found = jnp.concatenate([total(parts, rows), behind.astype(BF16)], axis=0)
     out[...] = jnp.broadcast_to(found, out.shape)
 
 
-def gather_kernel(spans, parts, near, mine, out, low_grad):
+def across_kernel(parts, out, near):
     rows = parts.shape[1] - BACK
-    out[...] = jnp.broadcast_to(total(parts, rows), out.shape)
-    after = (lax.axis_index("ctx") // Z_RING + 1) % (spans // Z_RING)
-    low_grad[0, :RANK, :] = mine[:RANK, :]
-    low_grad[0, RANK:, :] = mine[RANK:, :] + near[...] + parts[after, rows:, :].astype(F32)
-
-
-def assemble_kernel(spans, parts, grad_up):
+    high = lax.axis_index("ctx") // Z_SIZE % 2
+    y = high * Y_LOW + lax.axis_index("dp") // CORES
+    came = parts[(y + Y_LOW) % Y_SIZE, rows:, :].astype(F32)
+    near[...] = jnp.where(high == 1, 0.0, came)
+    behind = jnp.where(high == 1, came, 0.0).astype(BF16)
+    found = jnp.concatenate([total(parts, rows), behind], axis=0)
+    out[...] = jnp.broadcast_to(found, out.shape)
+
+
+def assemble_kernel(parts, mine, near_z, near_y, grad_up, low_grad):
     for tile in range(KV_HEADS * TILES):
         head, inside = tile // TILES, tile % TILES
         column = head * SHARE + inside if inside < SHARE else HEADS + (inside - SHARE) * KV_HEADS + head
@@ -271,11 +287,16 @@
         grad_up[:, column * D_HEAD : (column + 1) * D_HEAD] = parts[
             2 * head + inside * RANK // PART, rows, :
         ].astype(F32)
-
-
-def small(kernel, spans, name, out_shape, *operands):
+    x = lax.axis_index("ctx") // (2 * Z_SIZE)
+    after = (x + 1) % X_SIZE * CORES + lax.axis_index("dp") % CORES
+    low_grad[0, :RANK, :] = mine[:RANK, :]
+    returned = near_z[...] + near_y[...] + parts[after, PART:, :].astype(F32)
+    low_grad[0, RANK:, :] = mine[RANK:, :] + returned
+
+
+def small(kernel, name, out_shape, *operands):
     return pl.pallas_call(
-        functools.partial(kernel, spans),
+        kernel,
         out_shape=out_shape,
         compiler_params=pltpu.CompilerParams(vmem_limit_bytes=16 * 1024 * 1024),
         name=name,
@@ -283,25 +304,19 @@
 
 
 def everywhere(terms, mine, backs):
-    seqs, spans = lax.axis_size("dp"), lax.axis_size("ctx")
-    along = [[first + i for i in range(Z_RING)] for first in range(0, spans, Z_RING)]
-    across = [list(range(i, spans, Z_RING)) for i in range(Z_RING)]
-    shape = terms.shape
-    rows = shape[0] * shape[1] // seqs
-    sent = lambda n, m: jax.ShapeDtypeStruct((n, m, D_HEAD), BF16)
-    parts = exchange(terms.reshape(seqs, rows, D_HEAD), "dp")
-    parts = small(along_kernel, spans, "along", sent(Z_RING, rows + BACK), parts, *backs)
-    parts = exchange(parts, "ctx", along)
+    by_x, by_z, by_y = lines()
+    sent = jax.ShapeDtypeStruct((Z_SIZE, PART + BACK, D_HEAD), BF16)
     near = jax.ShapeDtypeStruct((BACK, ROWS), F32)
-    parts, near = small(across_kernel, spans, "across", (sent(spans // Z_RING, rows + BACK), near), parts)
-    parts = exchange(parts, "ctx", across)
+    parts = small(along_kernel, "along", sent, exchange(terms, by_x), *backs)
+    parts, near_z = small(beside_kernel, "beside", (sent, near), exchange(parts, by_z))
+    parts, near_y = small(across_kernel, "across", (sent, near), exchange(parts, by_y))
+    parts = exchange(parts, by_x)
+    grad_up = jax.ShapeDtypeStruct((RANK, (HEADS + 2 * KV_HEADS) * D_HEAD), F32)
     low_grad = jax.ShapeDtypeStruct((1, 3 * RANK, ROWS), F32)
-    parts, low_grad = small(
-        gather_kernel, spans, "gather", (sent(seqs, rows), low_grad), parts, near, mine
-    )
-    parts = exchange(parts, "dp").reshape(shape)
-    grad_up = jax.ShapeDtypeStruct((RANK, (HEADS + 2 * KV_HEADS) * D_HEAD), F32)
-    return jnp.swapaxes(low_grad, 1, 2), small(assemble_kernel, spans, "assemble", grad_up, parts)
+    grad_up, low_grad = small(
+        assemble_kernel, "assemble", (grad_up, low_grad), parts, mine, near_z, near_y
+    )
+    return jnp.swapaxes(low_grad, 1, 2), grad_up
 
 
 def shards(frozen_query, frozen_key_value, lowrank, adapter_up_weight, output_gradient):

time: 95.6 us -> 91.9 us (0.961)
  blocking collectives: 52.3 us -> 49.2 us
    all_to_all x4, blocking collectives: 52.3 us -> 49.2 us  [exchange(): return lax.all_to_all(value, ('dp', 'ctx'), 0, 0, axis_index_groups=groups)]
  transfers between devices with their start and end apart: 5 -> 5, of which waited for: 1 -> 1; matrix products, arithmetic and copies ran while one was open for 0% -> 0% of each run, Pallas kernels for 6% -> 7%
where the time goes in v4:
time: 91.9 us; the launch traced here: 91.4 us
  blocking collectives  49.2 us (54%)
  starting transfers between devices  18.4 us (20%)
  Pallas kernels  15.4 us (17%)
  waiting for transfers between devices  4.35 us (5%)
  local copies, waits for them, and re-layouts  3.14 us (3%)
    all_to_all x4, blocking collectives, exchange(): return lax.all_to_all(value, ('dp', 'ctx'), 0, 0, axis_index_groups=groups)  49.2 us
    ppermute x5, starting transfers between devices, send(): lax.ppermute(value, 'ctx', [(i, (i + by) % spans) for i in range(0, spans...  18.4 us
    pallas_call x1, Pallas kernels, shards(): pl.pallas_call(heavy_kernel, out_shape=(wide_out, terms_out, jax.ShapeDty...  6.53 us
    pallas_call x1, Pallas kernels, shards(): pl.pallas_call(light_kernel, out_shape=(wide_out, terms_out, jax.ShapeDty...  4.69 us
    ppermute x5, waiting for transfers between devices, send(): lax.ppermute(value, 'ctx', [(i, (i + by) % spans) for i in range(0, spans...  4.35 us
    unnamed x12, local copies, waits for them, and re-layouts  3.14 us
    pallas_call x1, Pallas kernels, shards(): pl.pallas_call(prepare_kernel, out_shape=(message, message), grid=(1,), i...  2 us
  transfers between devices with their start and end apart: 5, of which 1 were waited for; matrix products, arithmetic and copies ran while one was open for 0% of the time, Pallas kernels for 7%

profile of v4, /device:TPU:1, one launch (start us, length us, event | category | flops | bytes accessed | tf_op | source)
XLA Modules:
  0.0 91.4 jit_solution(895195251674794273)
XLA Ops:
  0.6 2.0 %prepare.1 = (bf16[144,512]{1,0:T(8,128)(2,1)}, bf16[144,512]{1,0:T(8,128)(2,1)}) custom-call(bf16[1,128,1024]{2,1,0:T(8,128)(2,1)} %frozen.1, bf16[1,48,128]{2,1,0:T(8,128)(2,1)} %bitcast.5, bf16[16,5120]{1,0:T(8,128)(2,1)} %up_v.3), custom_call_target="tpu_custom_call" | custom-call | tf_op jit(solution)/shard_map/prepare/pallas_call | solution.py:333
  2.6 6.6 %collective-permute-start.2 = (bf16[144,512]{1,0:T(8,128)(2,1)}, bf16[144,512]{1,0:T(8,128)(2,1)S(1)}, u32[]{:S(2)}, u32[]{:S(2)}) collective-permute-start(bf16[144,512]{1,0:T(8,128)(2,1)} %get-tuple-element.25.own), channel_id=1, source_target_pairs={{0,2},{2,4},{4,6},{6,8},{8,10},{10,12},{12,14},{14,16},{16,18},{18... | collective-permute-start | bytes 442376 | tf_op jit(solution)/shard_map/ppermute | solution.py:348
  9.3 1.9 %collective-permute-start = (bf16[144,512]{1,0:T(8,128)(2,1)}, bf16[144,512]{1,0:T(8,128)(2,1)S(1)}, u32[]{:S(2)}, u32[]{:S(2)}) collective-permute-start(bf16[144,512]{1,0:T(8,128)(2,1)} %get-tuple-element.25.own), channel_id=1, source_target_pairs={{0,1},{1,2},{2,3},{3,4},{4,5},{5,6},{6,7},{7,8},{8,9},{9,10},{10,1... | collective-permute-start | bytes 442376 | tf_op jit(solution)/shard_map/ppermute | solution.py:348
  11.2 7.3 %collective-permute-start.1 = (bf16[144,512]{1,0:T(8,128)(2,1)}, bf16[144,512]{1,0:T(8,128)(2,1)S(1)}, u32[]{:S(2)}, u32[]{:S(2)}) collective-permute-start(bf16[144,512]{1,0:T(8,128)(2,1)} %get-tuple-element.24.own), channel_id=1, source_target_pairs={{0,1},{2,3},{4,5},{6,7},{8,9},{10,11},{12,13},{14,15},{16,17},{18,... | collective-permute-start | bytes 442376 | tf_op jit(solution)/shard_map/ppermute | solution.py:348
  18.5 0.0 copy-start.3
  18.6 0.7 copy-done.3
  19.2 1.2 %copy-done = bf16[1,128,4096]{2,1,0:T(8,128)(2,1)S(1)} copy-done((bf16[1,128,4096]{2,1,0:T(8,128)(2,1)S(1)}, bf16[1,128,4096]{2,1,0:T(8,128)(2,1)}, u32[]{:S(2)}) %copy-start) | copy-done | bytes 1048600
  20.5 1.2 %copy-done.1 = bf16[1,128,4096]{2,1,0:T(8,128)(2,1)S(1)} copy-done((bf16[1,128,4096]{2,1,0:T(8,128)(2,1)S(1)}, bf16[1,128,4096]{2,1,0:T(8,128)(2,1)}, u32[]{:S(2)}) %copy-start.1) | copy-done | bytes 1048600
  21.7 1.3 %stack.22 = (bf16[4096,128]{1,0:T(8,128)(2,1)S(1)}, bf16[4096,128]{1,0:T(8,128)(2,1)S(1)}) custom-call(bf16[1,128,4096]{2,1,0:T(8,128)(2,1)S(1)} %copy-done, bf16[1,128,4096]{2,1,0:T(8,128)(2,1)S(1)} %copy-done.1, bf16[1,48,128]{2,1,0:T(8,128)(2,1)S(1)} %bitcast.6, bf16[16,5120]{1,0:T(8,128)(2,1)S(1)} %copy-done.2), custom_call_target="tpu_custom_call" | custom-call | flops 16777216 | bytes 4194304 | tf_op jit(solution)/shard_map/stack/pallas_call | solution.py:360
  23.0 0.1 pad_add_fusion.place
  23.0 4.3 %collective-permute-done.2.two_even = bf16[144,512]{1,0:T(8,128)(2,1)S(1)} collective-permute-done((bf16[144,512]{1,0:T(8,128)(2,1)}, bf16[144,512]{1,0:T(8,128)(2,1)S(1)}, u32[]{:S(2)}, u32[]{:S(2)}) %collective-permute-start.2) | collective-permute-done | bytes 147488 | tf_op jit(solution)/shard_map/ppermute | solution.py:348
  27.4 1.3 %collective-permute-start.4 = (bf16[144,512]{1,0:T(8,128)(2,1)S(1)}, bf16[144,512]{1,0:T(8,128)(2,1)S(1)}, u32[]{:S(2)}, u32[]{:S(2)}) collective-permute-start(bf16[144,512]{1,0:T(8,128)(2,1)S(1)} %collective-permute-done.2.two_even), channel_id=1, source_target_pairs={{0,1},{2,3},{4,5},{6,7},{8,9},{10,11},{12,13},{14,15},{16,17},{18,... | collective-permute-start | bytes 442376 | tf_op jit(solution)/shard_map/ppermute | solution.py:348
  28.7 0.0 collective-permute-done.one.one_even
  28.7 1.3 %collective-permute-start.3 = (bf16[144,512]{1,0:T(8,128)(2,1)S(1)}, bf16[144,512]{1,0:T(8,128)(2,1)S(1)}, u32[]{:S(2)}, u32[]{:S(2)}) collective-permute-start(bf16[144,512]{1,0:T(8,128)(2,1)S(1)} %collective-permute-done.one.one_even), channel_id=1, source_target_pairs={{0,1},{2,3},{4,5},{6,7},{8,9},{10,11},{12,13},{14,15},{16,17},{18,... | collective-permute-start | bytes 442376 | tf_op jit(solution)/shard_map/ppermute | solution.py:348
  30.0 0.1 pad_add_fusion.1.place
  30.1 4.7 %light_heads.1 = (bf16[1,128,4096]{2,1,0:T(8,128)(2,1)}, bf16[8,80,128]{2,1,0:T(8,128)(2,1)S(1)}, f32[48,256]{1,0:T(8,128)S(1)}) custom-call(s32[2]{0:T(128)S(1)} %pad_add_fusion.1.place, bf16[4096,128]{1,0:T(8,128)(2,1)S(1)} %get-tuple-element.22.query, bf16[4096,128]{1,0:T(8,128)(2,1)S(1)} %get-tuple-element.23.grad, bf16[1,48,128]{2,1,0:T(8,128)(2,1)S(1)} %bitcast.7, ...), custom_call_target="tpu_custom_call" | custom-call | flops 805306368 | bytes 1572864 | tf_op jit(solution)/shard_map/light_heads/pallas_call | solution.py:378
  34.8 0.0 collective-permute-done.1.one_odd
  34.8 6.5 %heavy_heads.1 = (bf16[1,128,4096]{2,1,0:T(8,128)(2,1)}, bf16[8,80,128]{2,1,0:T(8,128)(2,1)S(1)}, f32[48,128]{1,0:T(8,128)S(1)}, f32[32,128]{1,0:T(8,128)S(1)}, ...) custom-call(s32[2]{0:T(128)S(1)} %pad_add_fusion.place, ...), custom_call_target="tpu_custom_call", output_to_operand_aliasing={{0}: (14, {}), {1}: (15, {})} | custom-call | flops 1610612736 | bytes 1572864 | tf_op jit(solution)/shard_map/heavy_heads/pallas_call | solution.py:393
  41.3 10.6 %all_to_all.20.parts = bf16[8,80,128]{2,1,0:T(8,128)(2,1)S(1)} all-to-all(bf16[8,80,128]{2,1,0:T(8,128)(2,1)S(1)} %get-tuple-element.30), channel_id=1, replica_groups={{0,64,16,80,32,96,48,112},{1,65,17,81,33,97,49,113},{2,66,18,82,34,98,5..., dimensions={0} | all-to-all | bytes 327680 | tf_op jit(solution)/shard_map/all_to_all | solution.py:228
  51.9 12.2 %all_to_all.21.parts = bf16[8,112,128]{2,1,0:T(8,128)(2,1)S(1)} all-to-all(bf16[8,112,128]{2,1,0:T(8,128)(2,1)S(1)} %along.1), channel_id=1, replica_groups={{0,1,2,3,4,5,6,7},{64,65,66,67,68,69,70,71},{128,129,130,131,132,133,13..., dimensions={0} | all-to-all | bytes 458752 | tf_op jit(solution)/shard_map/all_to_all | solution.py:228
  64.1 0.1 beside.1
  64.1 13.8 %all_to_all.22.parts = bf16[8,112,128]{2,1,0:T(8,128)(2,1)S(1)} all-to-all(bf16[8,112,128]{2,1,0:T(8,128)(2,1)S(1)} %get-tuple-element.34), channel_id=1, replica_groups={{0,128,256,384,8,136,264,392},{64,192,320,448,72,200,328,456},{1,129,25..., dimensions={0} | all-to-all | bytes 458752 | tf_op jit(solution)/shard_map/all_to_all | solution.py:228
  77.9 12.7 %all_to_all.23.parts = bf16[8,112,128]{2,1,0:T(8,128)(2,1)S(1)} all-to-all(bf16[8,112,128]{2,1,0:T(8,128)(2,1)S(1)} %get-tuple-element.35), channel_id=1, replica_groups={{0,64,16,80,32,96,48,112},{1,65,17,81,33,97,49,113},{2,66,18,82,34,98,5..., dimensions={0} | all-to-all | bytes 458752 | tf_op jit(solution)/shard_map/all_to_all | solution.py:228
  90.7 0.8 assemble.1
  (12 shorter events, 0.1 us)
Async XLA Ops:
  0.6 17.9 %copy-start.2 = (bf16[16,5120]{1,0:T(8,128)(2,1)S(1)}, bf16[16,5120]{1,0:T(8,128)(2,1)}, u32[]{:S(2)}) copy-start(bf16[16,5120]{1,0:T(8,128)(2,1)} %up_v.3) | copy-start | bytes 491524
  2.6 24.7 %collective-permute-start.2 = (bf16[144,512]{1,0:T(8,128)(2,1)}, bf16[144,512]{1,0:T(8,128)(2,1)S(1)}, u32[]{:S(2)}, u32[]{:S(2)}) collective-permute-start(bf16[144,512]{1,0:T(8,128)(2,1)} %get-tuple-element.25.own), channel_id=1, source_target_pairs={{0,2},{2,4},{4,6},{6,8},{8,10},{10,12},{12,14},{14,16},{16,18},{18... | collective-permute-start | bytes 442376 | tf_op jit(solution)/shard_map/ppermute | solution.py:348
  9.3 19.4 %collective-permute-start = (bf16[144,512]{1,0:T(8,128)(2,1)}, bf16[144,512]{1,0:T(8,128)(2,1)S(1)}, u32[]{:S(2)}, u32[]{:S(2)}) collective-permute-start(bf16[144,512]{1,0:T(8,128)(2,1)} %get-tuple-element.25.own), channel_id=1, source_target_pairs={{0,1},{1,2},{2,3},{3,4},{4,5},{5,6},{6,7},{7,8},{8,9},{9,10},{10,1... | collective-permute-start | bytes 442376 | tf_op jit(solution)/shard_map/ppermute | solution.py:348
  11.2 23.6 %collective-permute-start.1 = (bf16[144,512]{1,0:T(8,128)(2,1)}, bf16[144,512]{1,0:T(8,128)(2,1)S(1)}, u32[]{:S(2)}, u32[]{:S(2)}) collective-permute-start(bf16[144,512]{1,0:T(8,128)(2,1)} %get-tuple-element.24.own), channel_id=1, source_target_pairs={{0,1},{2,3},{4,5},{6,7},{8,9},{10,11},{12,13},{14,15},{16,17},{18,... | collective-permute-start | bytes 442376 | tf_op jit(solution)/shard_map/ppermute | solution.py:348
  18.5 0.7 copy-start.3
  19.2 1.2 %copy-start = (bf16[1,128,4096]{2,1,0:T(8,128)(2,1)S(1)}, bf16[1,128,4096]{2,1,0:T(8,128)(2,1)}, u32[]{:S(2)}) copy-start(bf16[1,128,4096]{2,1,0:T(8,128)(2,1)} %query.1) | copy-start | bytes 3145732
  20.5 1.2 %copy-start.1 = (bf16[1,128,4096]{2,1,0:T(8,128)(2,1)S(1)}, bf16[1,128,4096]{2,1,0:T(8,128)(2,1)}, u32[]{:S(2)}) copy-start(bf16[1,128,4096]{2,1,0:T(8,128)(2,1)} %grad.1) | copy-start | bytes 3145732
  21.7 8.4 %copy-start.5 = (bf16[144,512]{1,0:T(8,128)(2,1)S(1)}, bf16[144,512]{1,0:T(8,128)(2,1)}, u32[]{:S(2)}) copy-start(bf16[144,512]{1,0:T(8,128)(2,1)} %get-tuple-element.25.own) | copy-start | bytes 442372
  27.4 7.4 %collective-permute-start.4 = (bf16[144,512]{1,0:T(8,128)(2,1)S(1)}, bf16[144,512]{1,0:T(8,128)(2,1)S(1)}, u32[]{:S(2)}, u32[]{:S(2)}) collective-permute-start(bf16[144,512]{1,0:T(8,128)(2,1)S(1)} %collective-permute-done.2.two_even), channel_id=1, source_target_pairs={{0,1},{2,3},{4,5},{6,7},{8,9},{10,11},{12,13},{14,15},{16,17},{18,... | collective-permute-start | bytes 442376 | tf_op jit(solution)/shard_map/ppermute | solution.py:348
  28.7 6.1 %collective-permute-start.3 = (bf16[144,512]{1,0:T(8,128)(2,1)S(1)}, bf16[144,512]{1,0:T(8,128)(2,1)S(1)}, u32[]{:S(2)}, u32[]{:S(2)}) collective-permute-start(bf16[144,512]{1,0:T(8,128)(2,1)S(1)} %collective-permute-done.one.one_even), channel_id=1, source_target_pairs={{0,1},{2,3},{4,5},{6,7},{8,9},{10,11},{12,13},{14,15},{16,17},{18,... | collective-permute-start | bytes 442376 | tf_op jit(solution)/shard_map/ppermute | solution.py:348
  30.1 4.7 %copy-start.4 = (bf16[144,512]{1,0:T(8,128)(2,1)S(1)}, bf16[144,512]{1,0:T(8,128)(2,1)}, u32[]{:S(2)}) copy-start(bf16[144,512]{1,0:T(8,128)(2,1)} %get-tuple-element.24.own) | copy-start | bytes 442372

commit v5 on v4

--- a/solution.py
+++ b/solution.py
@@ -1,3 +1,4 @@
+import functools
 import math
 
 import jax
@@ -73,8 +74,8 @@
         grads[rows, :] = grad[0, :, cols]
 
 
-def attend(place, query, grad, low, up_q, up_k, up_v, blocks, closed, attended, terms):
-    head = pl.program_id(0)
+def attend(place, head, all_queries, all_grads, low_q, ups, blocks, closed, attended, terms):
+    up_rows, up_k, up_v = ups
     key_cols = pl.ds(pl.multiple_of(head * D_HEAD, D_HEAD), D_HEAD)
     value_cols = pl.ds(pl.multiple_of((head + 2) * D_HEAD, D_HEAD), D_HEAD)
     bias = jnp.where(place[1] == 1, 0.0, BLOCKED).astype(F32)
@@ -84,17 +85,12 @@
     tail = slice(ROWS, MESSAGE)
     low_k = jnp.concatenate([b(tail, slice(0, D_HEAD)) for b in blocks], axis=1)
     low_v = jnp.concatenate([b(tail, slice(D_HEAD, 2 * D_HEAD)) for b in blocks], axis=1)
-    low_q = low[0, :RANK, :]
     keys_t = keys.T
     values_t = values.T
-    up_rows = up_q[...]
     wide = 2 * ROWS
     row = lax.broadcasted_iota(jnp.int32, (ROWS, wide), 0)
     col = lax.broadcasted_iota(jnp.int32, (ROWS, wide), 1)
     causal = row <= jnp.where(col >= ROWS, col - ROWS, col)
-    sides = [slice(h * D_HEAD, (h + 1) * D_HEAD) for h in range(SHARE)]
-    all_queries = query[...]
-    all_grads = grad[...]
     pairs = [slice(i * wide, (i + 1) * wide) for i in range(SHARE // 2)]
     products = [(mul_t(keys, all_queries[p]), mul_t(values, all_grads[p])) for p in pairs]
     all_weights, all_scores = [], []
@@ -118,7 +114,7 @@
         grad_query_t = (mul(keys_t, all_scores[i]) * scale).astype(BF16)
         for k in range(2):
             mine = slice(k * ROWS, (k + 1) * ROWS)
-            attended[0, :, sides[2 * i + k]] = out_t[:, mine].T.astype(BF16)
+            attended(2 * i + k)[...] = out_t[:, mine].T.astype(BF16)
             grad_queries.append(grad_query_t[:, mine])
     stacked = jnp.concatenate(grad_queries, axis=0)
     low_grad = mul(up_rows, stacked)
@@ -130,26 +126,61 @@
     found = jnp.concatenate(found, axis=1).astype(BF16)
     for tile in range(TILES):
         rows = slice(tile * RANK % PART, tile * RANK % PART + RANK)
-        terms[tile * RANK // PART, rows, :] = found[:, tile * D_HEAD : (tile + 1) * D_HEAD]
-    return 2.0 * low_grad, 2.0 * mul_t(up_k[...], grad_keys), 2.0 * mul_t(up_v[...], grad_values)
-
-
-def light_kernel(place, query, grad, low, up_q, up_k, up_v, own, one, attended, terms, low_terms):
-    blocks = [lambda r, c: own[r, c], lambda r, c: one[r, c]]
-    by_query, by_key, by_value = attend(
-        place, query, grad, low, up_q, up_k, up_v, blocks, [True], attended, terms
-    )
-    found = jnp.concatenate(
-        [jnp.concatenate([by_query, jnp.zeros_like(by_query)], axis=1), by_key, by_value], axis=0
-    )
-
-    @pl.when(pl.program_id(0) == 0)
-    def _():
-        low_terms[...] = found
-
-    @pl.when(pl.program_id(0) != 0)
-    def _():
-        low_terms[...] += found
+        terms(tile * RANK // PART)[rows, :] = found[:, tile * D_HEAD : (tile + 1) * D_HEAD]
+    return 2.0 * low_grad, 2.0 * mul_t(up_k, grad_keys), 2.0 * mul_t(up_v, grad_values)
+
+
+def light_heads(place, query, grad, low, up, blocks, closed, attended, terms, low_terms, held, sems):
+    sums, copies = [], []
+    for head in range(2):
+        chosen = place[0] * 2 + head
+        rows = pl.ds(pl.multiple_of(chosen * WIDE, WIDE), WIDE)
+        ups = [
+            up[:, pl.ds(pl.multiple_of(first * D_HEAD + chosen * width, D_HEAD), width)]
+            for first, width in ((0, WIDE), (HEADS, D_HEAD), (HEADS + KV_HEADS, D_HEAD))
+        ]
+        found = attend(
+            place, head, query[rows, :], grad[rows, :], low[0, :RANK, :], ups, blocks, closed,
+            lambda k, head=head: held.at[head, 0, :, k * D_HEAD : (k + 1) * D_HEAD],
+            lambda i, chosen=chosen: terms.at[2 * chosen + i],
+        )
+        sums = [a + b for a, b in zip(sums, found)] if sums else found
+        copies.append(
+            pltpu.make_async_copy(held.at[head], attended.at[:, :, rows], sems.at[head])
+        )
+        copies[-1].start()
+    by_query, by_key, by_value = sums
+    low_terms[...] = jnp.zeros_like(low_terms)
+    reach = by_key.shape[1]
+    low_terms[:RANK, :ROWS] = by_query
+    low_terms[RANK : 2 * RANK, :reach] = by_key
+    low_terms[2 * RANK :, :reach] = by_value
+    for copy in copies:
+        copy.wait()
+
+
+def early_kernel(place, query, grad, low, up, own, attended, terms, low_terms, held, sems):
+    @pl.when(place[2] == 1)
+    def _():
+        blocks = [lambda r, c: own[r, c]]
+        light_heads(place, query, grad, low, up, blocks, [], attended, terms, low_terms, held, sems)
+
+
+def light_kernel(
+    place, query, grad, low, up, own, one, terms_before, low_before, _attended,
+    attended, terms, low_terms, held, sems,
+):
+    @pl.when(place[2] == 1)
+    def _():
+        terms[...] = terms_before[...]
+        low_terms[...] = low_before[...]
+
+    @pl.when(place[2] == 0)
+    def _():
+        blocks = [lambda r, c: own[r, c], lambda r, c: one[r, c]]
+        light_heads(
+            place, query, grad, low, up, blocks, [True], attended, terms, low_terms, held, sems
+        )
 
 
 def heavy_kernel(
@@ -171,8 +202,11 @@
         back_two[...] = jnp.zeros_like(back_two)
         back_three[...] = jnp.zeros_like(back_three)
 
+    ups = (up_q[...], up_k[...], up_v[...])
     by_query, by_key, by_value = attend(
-        place, query, grad, low, up_q, up_k, up_v, blocks, [False, False, True], attended, terms
+        place, pl.program_id(0), query[...], grad[...], low[0, :RANK, :], ups, blocks, [False, False, True],
+        lambda k: attended.at[0, :, k * D_HEAD : (k + 1) * D_HEAD],
+        lambda i: terms.at[i],
     )
     mine[:RANK, :] += by_query
     mine[RANK : 2 * RANK, :] += by_key[:, :ROWS]
@@ -324,7 +358,8 @@
     position = lax.axis_index("ctx") % (GROUP // ROWS)
     light_half = position // 2
     odd = position % 2
-    light_place = jnp.stack([light_half, odd]).astype(jnp.int32)
+    early = lax.axis_index("ctx") % Z_SIZE == 0
+    light_place = jnp.stack([light_half, odd, early]).astype(jnp.int32)
     heavy_place = jnp.stack([1 - light_half, odd]).astype(jnp.int32)
     message = jax.ShapeDtypeStruct((MESSAGE, 4 * D_HEAD), BF16)
     message_spec = whole(MESSAGE, 4 * D_HEAD)
@@ -350,8 +385,6 @@
     one = send(light, 1)
     two_even = send(light, 2, 2)
     one_odd = send(heavy, 1, 2)
-    two_odd = send(one, 1, 2)
-    three = send(two_even, 1, 2)
     wide_out = jax.ShapeDtypeStruct((1, ROWS, HEADS * D_HEAD), BF16)
     terms_out = jax.ShapeDtypeStruct((2 * KV_HEADS, PART, D_HEAD), BF16)
     stacked_out = jax.ShapeDtypeStruct((HEADS * ROWS, D_HEAD), BF16)
@@ -368,26 +401,37 @@
             pl.BlockSpec((RANK, WIDE), lambda i: (0, i)),
         ],
         out_specs=[stacked_block, stacked_block],
-        compiler_params=pltpu.CompilerParams(vmem_limit_bytes=16 * 1024 * 1024),
+        compiler_params=pltpu.CompilerParams(vmem_limit_bytes=51 * 1024 * 1024),
         cost_estimate=pl.CostEstimate(
             flops=2 * ROWS * RANK * WIDE * 4, bytes_accessed=16 * ROWS * WIDE * 2, transcendentals=0
         ),
         name="stack",
     )(frozen_query, output_gradient, columns_first, adapter_up_weight)
     arguments = (queries, grads, columns_first) + (adapter_up_weight,) * 3
-    attended, terms, low_terms = pl.pallas_call(
+    light_arguments = (light_place, queries, grads, columns_first, adapter_up_weight, light)
+    light_outs = (wide_out, terms_out, jax.ShapeDtypeStruct((3 * RANK, 2 * ROWS), F32))
+    vmem = pl.BlockSpec(memory_space=pltpu.VMEM)
+    light_call = functools.partial(
+        pl.pallas_call,
+        out_shape=light_outs,
+        out_specs=[pl.BlockSpec(memory_space=pl.ANY), vmem, vmem],
+        scratch_shapes=[pltpu.VMEM((2, 1, ROWS, WIDE), BF16), pltpu.SemaphoreType.DMA((2,))],
+        compiler_params=pltpu.CompilerParams(vmem_limit_bytes=28 * 1024 * 1024),
+        cost_estimate=cost(2),
+    )
+    in_smem = [pl.BlockSpec(memory_space=pltpu.SMEM)]
+    attended, terms, low_terms = light_call(
+        early_kernel, in_specs=in_smem + [vmem] * 5, name="early_heads"
+    )(*light_arguments)
+    one, two_even, attended = lax.optimization_barrier((one, two_even, attended))
+    two_odd = send(one, 1, 2)
+    three = send(two_even, 1, 2)
+    attended, terms, low_terms = light_call(
         light_kernel,
-        out_shape=(wide_out, terms_out, jax.ShapeDtypeStruct((3 * RANK, 2 * ROWS), F32)),
-        grid_spec=pltpu.PrefetchScalarGridSpec(
-            num_scalar_prefetch=1,
-            grid=(2,),
-            in_specs=common_specs() + [message_spec] * 2,
-            out_specs=[wide_half(), term_half(), whole(3 * RANK, 2 * ROWS)],
-        ),
-        compiler_params=params(),
-        cost_estimate=cost(2),
+        in_specs=in_smem + [vmem] * 8 + [pl.BlockSpec(memory_space=pl.ANY)],
+        input_output_aliases={9: 0},
         name="light_heads",
-    )(light_place, *arguments, light, one)
+    )(*light_arguments, one, terms, low_terms, attended)
     back_out = jax.ShapeDtypeStruct((2 * RANK, ROWS), F32)
     back_spec = whole(2 * RANK, ROWS)
     attended, terms, mine, *backs = pl.pallas_call(

time: 91.9 us -> 93.2 us (1.014)
  blocking collectives: 49.2 us -> 52.8 us
  local copies, waits for them, and re-layouts: 3.14 us -> 0.69 us
    all_to_all x4, blocking collectives: 49.2 us -> 52.8 us  [exchange(): return lax.all_to_all(value, ('dp', 'ctx'), 0, 0, axis_index_groups=groups)]
    unnamed x12 -> x8, local copies, waits for them, and re-layouts: 3.14 us -> 0.69 us
    pallas_call x1, Pallas kernels: 1.26 us -> 2.95 us  [shards(): pl.pallas_call(stack_kernel, out_shape=(stacked_out, stacked_out), grid=(...]
    pallas_call x1 -> x2, Pallas kernels: 4.69 us -> 3.96 us  [the longest x1 3.37 us: shards(): light_call(early_kernel, in_specs=in_smem + [vmem] * 5, name='early_heads')]
  transfers between devices with their start and end apart: 5 -> 5, of which waited for: 1 -> 3; matrix products, arithmetic and copies ran while one was open for 0% -> 0% of each run, Pallas kernels for 7% -> 7%
where the time goes in v5:
time: 93.2 us; the launch traced here: 92.8 us
  blocking collectives  52.8 us (57%)
  starting transfers between devices  18.4 us (20%)
  Pallas kernels  16.3 us (17%)
  waiting for transfers between devices  3.57 us (4%)
    all_to_all x4, blocking collectives, exchange(): return lax.all_to_all(value, ('dp', 'ctx'), 0, 0, axis_index_groups=groups)  52.8 us
    ppermute x5, starting transfers between devices, send(): lax.ppermute(value, 'ctx', [(i, (i + by) % spans) for i in range(0, spans...  18.4 us
    pallas_call x1, Pallas kernels, shards(): pl.pallas_call(heavy_kernel, out_shape=(wide_out, terms_out, jax.ShapeDty...  6.52 us
    ppermute x5, waiting for transfers between devices, send(): lax.ppermute(value, 'ctx', [(i, (i + by) % spans) for i in range(0, spans...  3.57 us
    pallas_call x1, Pallas kernels, shards(): light_call(early_kernel, in_specs=in_smem + [vmem] * 5, name='early_heads')  3.37 us
    pallas_call x1, Pallas kernels, shards(): pl.pallas_call(stack_kernel, out_shape=(stacked_out, stacked_out), grid=(...  2.95 us
    pallas_call x1, Pallas kernels, shards(): pl.pallas_call(prepare_kernel, out_shape=(message, message), grid=(1,), i...  1.99 us
  transfers between devices with their start and end apart: 5, of which 3 were waited for; matrix products, arithmetic and copies ran while one was open for 0% of the time, Pallas kernels for 7%

profile of v5, /device:TPU:1, one launch (start us, length us, event | category | flops | bytes accessed | tf_op | source)
XLA Modules:
  0.0 92.8 jit_solution(1084865489567136205)
XLA Ops:
  0.6 2.0 %prepare.1 = (bf16[144,512]{1,0:T(8,128)(2,1)}, bf16[144,512]{1,0:T(8,128)(2,1)}) custom-call(bf16[1,128,1024]{2,1,0:T(8,128)(2,1)} %frozen.1, bf16[1,48,128]{2,1,0:T(8,128)(2,1)} %bitcast.6, bf16[16,5120]{1,0:T(8,128)(2,1)} %up_v.1), custom_call_target="tpu_custom_call" | custom-call | tf_op jit(solution)/shard_map/prepare/pallas_call | solution.py:368
  2.6 6.6 %collective-permute-start.1 = (bf16[144,512]{1,0:T(8,128)(2,1)}, bf16[144,512]{1,0:T(8,128)(2,1)S(1)}, u32[]{:S(2)}, u32[]{:S(2)}) collective-permute-start(bf16[144,512]{1,0:T(8,128)(2,1)} %get-tuple-element.31.own), channel_id=1, source_target_pairs={{0,2},{2,4},{4,6},{6,8},{8,10},{10,12},{12,14},{14,16},{16,18},{18... | collective-permute-start | bytes 442376 | tf_op jit(solution)/shard_map/ppermute | solution.py:383
  9.3 1.9 %collective-permute-start = (bf16[144,512]{1,0:T(8,128)(2,1)}, bf16[144,512]{1,0:T(8,128)(2,1)S(1)}, u32[]{:S(2)}, u32[]{:S(2)}) collective-permute-start(bf16[144,512]{1,0:T(8,128)(2,1)} %get-tuple-element.31.own), channel_id=1, source_target_pairs={{0,1},{1,2},{2,3},{3,4},{4,5},{5,6},{6,7},{7,8},{8,9},{9,10},{10,1... | collective-permute-start | bytes 442376 | tf_op jit(solution)/shard_map/ppermute | solution.py:383
  11.2 7.3 %collective-permute-start.2 = (bf16[144,512]{1,0:T(8,128)(2,1)}, bf16[144,512]{1,0:T(8,128)(2,1)S(1)}, u32[]{:S(2)}, u32[]{:S(2)}) collective-permute-start(bf16[144,512]{1,0:T(8,128)(2,1)} %get-tuple-element.30.own), channel_id=1, source_target_pairs={{0,1},{2,3},{4,5},{6,7},{8,9},{10,11},{12,13},{14,15},{16,17},{18,... | collective-permute-start | bytes 442376 | tf_op jit(solution)/shard_map/ppermute | solution.py:383
  18.5 0.0 copy-start.2
  18.6 0.7 copy-done.2
  19.2 3.0 %stack.31 = (bf16[4096,128]{1,0:T(8,128)(2,1)S(1)}, bf16[4096,128]{1,0:T(8,128)(2,1)S(1)}) custom-call(bf16[1,128,4096]{2,1,0:T(8,128)(2,1)} %query.1, bf16[1,128,4096]{2,1,0:T(8,128)(2,1)} %grad.1, bf16[1,48,128]{2,1,0:T(8,128)(2,1)S(1)} %bitcast.7, bf16[16,5120]{1,0:T(8,128)(2,1)S(1)} %copy-done), custom_call_target="tpu_custom_call" | custom-call | flops 16777216 | bytes 4194304 | tf_op jit(solution)/shard_map/stack/pallas_call | solution.py:393
  22.2 0.1 pad_add_fusion.1.place
  22.3 3.4 %early_heads.1 = (bf16[1,128,4096]{2,1,0:T(8,128)(2,1)}, bf16[8,80,128]{2,1,0:T(8,128)(2,1)S(1)}, f32[48,256]{1,0:T(8,128)S(1)}) custom-call(s32[3]{0:T(128)S(1)} %pad_add_fusion.1.place, bf16[4096,128]{1,0:T(8,128)(2,1)S(1)} %get-tuple-element.28.query, bf16[4096,128]{1,0:T(8,128)(2,1)S(1)} %get-tuple-element.29.grad, bf16[1,48,128]{2,1,0:T(8,128)(2,1)S(1)} %bitcast.8, ...), custom_call_target="tpu_custom_call" | custom-call | flops 805306368 | bytes 1572864 | tf_op jit(solution)/shard_map/early_heads/pallas_call | solution.py:423
  25.7 1.7 %collective-permute-done.1.two_even = bf16[144,512]{1,0:T(8,128)(2,1)S(1)} collective-permute-done((bf16[144,512]{1,0:T(8,128)(2,1)}, bf16[144,512]{1,0:T(8,128)(2,1)S(1)}, u32[]{:S(2)}, u32[]{:S(2)}) %collective-permute-start.1) | collective-permute-done | bytes 147488 | tf_op jit(solution)/shard_map/ppermute | solution.py:383
  27.4 0.0 collective-permute-done.one.one_even
  27.4 1.3 %collective-permute-start.4 = (bf16[144,512]{1,0:T(8,128)(2,1)S(1)}, bf16[144,512]{1,0:T(8,128)(2,1)S(1)}, u32[]{:S(2)}, u32[]{:S(2)}) collective-permute-start(bf16[144,512]{1,0:T(8,128)(2,1)S(1)} %collective-permute-done.1.two_even), channel_id=1, source_target_pairs={{0,1},{2,3},{4,5},{6,7},{8,9},{10,11},{12,13},{14,15},{16,17},{18,... | collective-permute-start | bytes 442376 | tf_op jit(solution)/shard_map/ppermute | solution.py:383
  28.7 1.3 %collective-permute-start.3 = (bf16[144,512]{1,0:T(8,128)(2,1)S(1)}, bf16[144,512]{1,0:T(8,128)(2,1)S(1)}, u32[]{:S(2)}, u32[]{:S(2)}) collective-permute-start(bf16[144,512]{1,0:T(8,128)(2,1)S(1)} %collective-permute-done.one.one_even), channel_id=1, source_target_pairs={{0,1},{2,3},{4,5},{6,7},{8,9},{10,11},{12,13},{14,15},{16,17},{18,... | collective-permute-start | bytes 442376 | tf_op jit(solution)/shard_map/ppermute | solution.py:383
  30.0 0.1 pad_add_fusion.place
  30.0 0.6 light_heads.1
  30.6 0.1 collective-permute-done.4.three
  30.7 1.8 %collective-permute-done.3.two_odd = bf16[144,512]{1,0:T(8,128)(2,1)S(1)} collective-permute-done((bf16[144,512]{1,0:T(8,128)(2,1)S(1)}, bf16[144,512]{1,0:T(8,128)(2,1)S(1)}, u32[]{:S(2)}, u32[]{:S(2)}) %collective-permute-start.3) | collective-permute-done | bytes 147488 | tf_op jit(solution)/shard_map/ppermute | solution.py:383
  32.5 6.5 %heavy_heads.1 = (bf16[1,128,4096]{2,1,0:T(8,128)(2,1)}, bf16[8,80,128]{2,1,0:T(8,128)(2,1)S(1)}, f32[48,128]{1,0:T(8,128)S(1)}, f32[32,128]{1,0:T(8,128)S(1)}, ...) custom-call(s32[2]{0:T(128)S(1)} %pad_add_fusion.place, ...), custom_call_target="tpu_custom_call", output_to_operand_aliasing={{0}: (14, {}), {1}: (15, {})} | custom-call | flops 1610612736 | bytes 1572864 | tf_op jit(solution)/shard_map/heavy_heads/pallas_call | solution.py:437
  39.0 11.3 %all_to_all.20.parts = bf16[8,80,128]{2,1,0:T(8,128)(2,1)S(1)} all-to-all(bf16[8,80,128]{2,1,0:T(8,128)(2,1)S(1)} %get-tuple-element.42), channel_id=1, replica_groups={{0,64,16,80,32,96,48,112},{1,65,17,81,33,97,49,113},{2,66,18,82,34,98,5..., dimensions={0} | all-to-all | bytes 327680 | tf_op jit(solution)/shard_map/all_to_all | solution.py:262
  50.4 13.0 %all_to_all.21.parts = bf16[8,112,128]{2,1,0:T(8,128)(2,1)S(1)} all-to-all(bf16[8,112,128]{2,1,0:T(8,128)(2,1)S(1)} %along.1), channel_id=1, replica_groups={{0,1,2,3,4,5,6,7},{64,65,66,67,68,69,70,71},{128,129,130,131,132,133,13..., dimensions={0} | all-to-all | bytes 458752 | tf_op jit(solution)/shard_map/all_to_all | solution.py:262
  63.4 0.1 beside.1
  63.4 15.8 %all_to_all.22.parts = bf16[8,112,128]{2,1,0:T(8,128)(2,1)S(1)} all-to-all(bf16[8,112,128]{2,1,0:T(8,128)(2,1)S(1)} %get-tuple-element.46), channel_id=1, replica_groups={{0,128,256,384,8,136,264,392},{64,192,320,448,72,200,328,456},{1,129,25..., dimensions={0} | all-to-all | bytes 458752 | tf_op jit(solution)/shard_map/all_to_all | solution.py:262
  79.3 12.7 %all_to_all.23.parts = bf16[8,112,128]{2,1,0:T(8,128)(2,1)S(1)} all-to-all(bf16[8,112,128]{2,1,0:T(8,128)(2,1)S(1)} %get-tuple-element.47), channel_id=1, replica_groups={{0,64,16,80,32,96,48,112},{1,65,17,81,33,97,49,113},{2,66,18,82,34,98,5..., dimensions={0} | all-to-all | bytes 458752 | tf_op jit(solution)/shard_map/all_to_all | solution.py:262
  92.0 0.8 assemble.1
  (9 shorter events, 0.1 us)
Async XLA Ops:
  0.6 17.9 %copy-start = (bf16[16,5120]{1,0:T(8,128)(2,1)S(1)}, bf16[16,5120]{1,0:T(8,128)(2,1)}, u32[]{:S(2)}) copy-start(bf16[16,5120]{1,0:T(8,128)(2,1)} %up_v.1) | copy-start | bytes 491524
  2.6 24.7 %collective-permute-start.1 = (bf16[144,512]{1,0:T(8,128)(2,1)}, bf16[144,512]{1,0:T(8,128)(2,1)S(1)}, u32[]{:S(2)}, u32[]{:S(2)}) collective-permute-start(bf16[144,512]{1,0:T(8,128)(2,1)} %get-tuple-element.31.own), channel_id=1, source_target_pairs={{0,2},{2,4},{4,6},{6,8},{8,10},{10,12},{12,14},{14,16},{16,18},{18... | collective-permute-start | bytes 442376 | tf_op jit(solution)/shard_map/ppermute | solution.py:383
  9.3 18.1 %collective-permute-start = (bf16[144,512]{1,0:T(8,128)(2,1)}, bf16[144,512]{1,0:T(8,128)(2,1)S(1)}, u32[]{:S(2)}, u32[]{:S(2)}) collective-permute-start(bf16[144,512]{1,0:T(8,128)(2,1)} %get-tuple-element.31.own), channel_id=1, source_target_pairs={{0,1},{1,2},{2,3},{3,4},{4,5},{5,6},{6,7},{7,8},{8,9},{9,10},{10,1... | collective-permute-start | bytes 442376 | tf_op jit(solution)/shard_map/ppermute | solution.py:383
  11.2 19.4 %collective-permute-start.2 = (bf16[144,512]{1,0:T(8,128)(2,1)}, bf16[144,512]{1,0:T(8,128)(2,1)S(1)}, u32[]{:S(2)}, u32[]{:S(2)}) collective-permute-start(bf16[144,512]{1,0:T(8,128)(2,1)} %get-tuple-element.30.own), channel_id=1, source_target_pairs={{0,1},{2,3},{4,5},{6,7},{8,9},{10,11},{12,13},{14,15},{16,17},{18,... | collective-permute-start | bytes 442376 | tf_op jit(solution)/shard_map/ppermute | solution.py:383
  18.5 0.7 copy-start.2
  19.2 3.0 %copy-start.1 = (bf16[144,512]{1,0:T(8,128)(2,1)S(1)}, bf16[144,512]{1,0:T(8,128)(2,1)}, u32[]{:S(2)}) copy-start(bf16[144,512]{1,0:T(8,128)(2,1)} %get-tuple-element.31.own) | copy-start | bytes 442372
  27.4 3.4 %collective-permute-start.4 = (bf16[144,512]{1,0:T(8,128)(2,1)S(1)}, bf16[144,512]{1,0:T(8,128)(2,1)S(1)}, u32[]{:S(2)}, u32[]{:S(2)}) collective-permute-start(bf16[144,512]{1,0:T(8,128)(2,1)S(1)} %collective-permute-done.1.two_even), channel_id=1, source_target_pairs={{0,1},{2,3},{4,5},{6,7},{8,9},{10,11},{12,13},{14,15},{16,17},{18,... | collective-permute-start | bytes 442376 | tf_op jit(solution)/shard_map/ppermute | solution.py:383
  28.7 3.9 %collective-permute-start.3 = (bf16[144,512]{1,0:T(8,128)(2,1)S(1)}, bf16[144,512]{1,0:T(8,128)(2,1)S(1)}, u32[]{:S(2)}, u32[]{:S(2)}) collective-permute-start(bf16[144,512]{1,0:T(8,128)(2,1)S(1)} %collective-permute-done.one.one_even), channel_id=1, source_target_pairs={{0,1},{2,3},{4,5},{6,7},{8,9},{10,11},{12,13},{14,15},{16,17},{18,... | collective-permute-start | bytes 442376 | tf_op jit(solution)/shard_map/ppermute | solution.py:383
  30.0 2.5 %copy-start.3 = (bf16[144,512]{1,0:T(8,128)(2,1)S(1)}, bf16[144,512]{1,0:T(8,128)(2,1)}, u32[]{:S(2)}) copy-start(bf16[144,512]{1,0:T(8,128)(2,1)} %get-tuple-element.30.own) | copy-start | bytes 442372

commit v6 on v5

--- a/solution.py
+++ b/solution.py
@@ -40,11 +40,11 @@
 
 
 def prepare_kernel(frozen, low, up, light, heavy):
-    low_k, low_v = low[0, RANK : 2 * RANK, :], low[0, 2 * RANK :, :]
+    low_q, low_k, low_v = (low[0, i * RANK : (i + 1) * RANK, :] for i in range(3))
     wide = KV_HEADS * D_HEAD
     keys = (frozen[0, :, :wide].astype(F32) + 2.0 * t_mul(low_k, up[:, :wide])).astype(BF16)
     values = (frozen[0, :, wide:].astype(F32) + 2.0 * t_mul(low_v, up[:, wide:])).astype(BF16)
-    tail = jnp.concatenate([low_k, low_v, jnp.zeros((RANK, 2 * D_HEAD), BF16)], axis=1)
+    tail = jnp.concatenate([low_k, low_v, low_q, jnp.zeros((RANK, D_HEAD), BF16)], axis=1)
     half = 2 * D_HEAD
 
     def write(plain, moved):
@@ -66,15 +66,30 @@
         write(heavy, light)
 
 
-def stack_kernel(query, grad, low, up_q, queries, grads):
-    found = (query[0].astype(F32) + 2.0 * t_mul(low[0, :RANK, :], up_q[...])).astype(BF16)
-    for i in range(SHARE):
-        rows, cols = slice(i * ROWS, (i + 1) * ROWS), slice(i * D_HEAD, (i + 1) * D_HEAD)
-        queries[rows, :] = found[:, cols]
-        grads[rows, :] = grad[0, :, cols]
-
-
-def attend(place, head, all_queries, all_grads, low_q, ups, blocks, closed, attended, terms):
+def stack_kernel(query, grad, low_all, up, queries, grads, held, low, sems):
+    copies = [pltpu.make_async_copy(low_all.at[0, pl.ds(0, RANK), :], low, sems.at[0])]
+    for i in range(KV_HEADS):
+        wide = query.at[0, :, pl.ds(i * WIDE, WIDE)]
+        copies.append(pltpu.make_async_copy(wide, held.at[i], sems.at[1 + i]))
+    for i in range(HEADS):
+        head = grad.at[0, :, pl.ds(i * D_HEAD, D_HEAD)]
+        place = grads.at[pl.ds(i * ROWS, ROWS), :]
+        copies.append(pltpu.make_async_copy(head, place, sems.at[1 + KV_HEADS + i]))
+    for copy in copies:
+        copy.start()
+    copies[0].wait()
+    for i in range(KV_HEADS):
+        added = 2.0 * t_mul(low[...], up[:, i * WIDE : (i + 1) * WIDE])
+        copies[1 + i].wait()
+        found = (held[i].astype(F32) + added).astype(BF16)
+        for k in range(SHARE):
+            rows = slice((i * SHARE + k) * ROWS, (i * SHARE + k + 1) * ROWS)
+            queries[rows, :] = found[:, k * D_HEAD : (k + 1) * D_HEAD]
+    for copy in copies[1 + KV_HEADS :]:
+        copy.wait()
+
+
+def attend(place, head, all_queries, all_grads, ups, blocks, closed, attended, terms):
     up_rows, up_k, up_v = ups
     key_cols = pl.ds(pl.multiple_of(head * D_HEAD, D_HEAD), D_HEAD)
     value_cols = pl.ds(pl.multiple_of((head + 2) * D_HEAD, D_HEAD), D_HEAD)
@@ -85,6 +100,7 @@
     tail = slice(ROWS, MESSAGE)
     low_k = jnp.concatenate([b(tail, slice(0, D_HEAD)) for b in blocks], axis=1)
     low_v = jnp.concatenate([b(tail, slice(D_HEAD, 2 * D_HEAD)) for b in blocks], axis=1)
+    low_q = blocks[0](tail, slice(2 * D_HEAD, 3 * D_HEAD))
     keys_t = keys.T
     values_t = values.T
     wide = 2 * ROWS
@@ -130,7 +146,7 @@
     return 2.0 * low_grad, 2.0 * mul_t(up_k, grad_keys), 2.0 * mul_t(up_v, grad_values)
 
 
-def light_heads(place, query, grad, low, up, blocks, closed, attended, terms, low_terms, held, sems):
+def light_heads(place, query, grad, up, blocks, closed, attended, terms, low_terms, held, sems):
     sums, copies = [], []
     for head in range(2):
         chosen = place[0] * 2 + head
@@ -140,7 +156,7 @@
             for first, width in ((0, WIDE), (HEADS, D_HEAD), (HEADS + KV_HEADS, D_HEAD))
         ]
         found = attend(
-            place, head, query[rows, :], grad[rows, :], low[0, :RANK, :], ups, blocks, closed,
+            place, head, query[rows, :], grad[rows, :], ups, blocks, closed,
             lambda k, head=head: held.at[head, 0, :, k * D_HEAD : (k + 1) * D_HEAD],
             lambda i, chosen=chosen: terms.at[2 * chosen + i],
         )
@@ -159,15 +175,15 @@
         copy.wait()
 
 
-def early_kernel(place, query, grad, low, up, own, attended, terms, low_terms, held, sems):
+def early_kernel(place, query, grad, up, own, attended, terms, low_terms, held, sems):
     @pl.when(place[2] == 1)
     def _():
         blocks = [lambda r, c: own[r, c]]
-        light_heads(place, query, grad, low, up, blocks, [], attended, terms, low_terms, held, sems)
+        light_heads(place, query, grad, up, blocks, [], attended, terms, low_terms, held, sems)
 
 
 def light_kernel(
-    place, query, grad, low, up, own, one, terms_before, low_before, _attended,
+    place, query, grad, up, own, one, terms_before, low_before, _attended,
     attended, terms, low_terms, held, sems,
 ):
     @pl.when(place[2] == 1)
@@ -179,12 +195,12 @@
     def _():
         blocks = [lambda r, c: own[r, c], lambda r, c: one[r, c]]
         light_heads(
-            place, query, grad, low, up, blocks, [True], attended, terms, low_terms, held, sems
+            place, query, grad, up, blocks, [True], attended, terms, low_terms, held, sems
         )
 
 
 def heavy_kernel(
-    place, query, grad, low, up_q, up_k, up_v, own, one_even, one_odd, two_even, two_odd, three, before,
+    place, query, grad, up_q, up_k, up_v, own, one_even, one_odd, two_even, two_odd, three, before,
     _attended, _terms, attended, terms, mine, back_one, back_two, back_three,
 ):
     odd = place[1] == 1
@@ -204,7 +220,7 @@
 
     ups = (up_q[...], up_k[...], up_v[...])
     by_query, by_key, by_value = attend(
-        place, pl.program_id(0), query[...], grad[...], low[0, :RANK, :], ups, blocks, [False, False, True],
+        place, pl.program_id(0), query[...], grad[...], ups, blocks, [False, False, True],
         lambda k: attended.at[0, :, k * D_HEAD : (k + 1) * D_HEAD],
         lambda i: terms.at[i],
     )
@@ -238,7 +254,6 @@
     return [
         stacked,
         stacked,
-        whole(1, 3 * RANK, ROWS),
         at_half(RANK, WIDE),
         at_half(RANK, D_HEAD, HEADS),
         at_half(RANK, D_HEAD, HEADS + KV_HEADS),
@@ -388,48 +403,45 @@
     wide_out = jax.ShapeDtypeStruct((1, ROWS, HEADS * D_HEAD), BF16)
     terms_out = jax.ShapeDtypeStruct((2 * KV_HEADS, PART, D_HEAD), BF16)
     stacked_out = jax.ShapeDtypeStruct((HEADS * ROWS, D_HEAD), BF16)
-    wide_block = pl.BlockSpec((1, ROWS, WIDE), lambda i: (0, 0, i))
-    stacked_block = pl.BlockSpec((SHARE * ROWS, D_HEAD), lambda i: (i, 0))
+    vmem, anywhere = pl.BlockSpec(memory_space=pltpu.VMEM), pl.BlockSpec(memory_space=pl.ANY)
     queries, grads = pl.pallas_call(
         stack_kernel,
         out_shape=(stacked_out, stacked_out),
-        grid=(KV_HEADS,),
-        in_specs=[
-            wide_block,
-            wide_block,
-            only(1, 3 * RANK, ROWS),
-            pl.BlockSpec((RANK, WIDE), lambda i: (0, i)),
+        in_specs=[anywhere] * 3 + [vmem],
+        out_specs=[vmem] * 2,
+        scratch_shapes=[
+            pltpu.VMEM((KV_HEADS, ROWS, WIDE), BF16),
+            pltpu.VMEM((RANK, D_HEAD), BF16),
+            pltpu.SemaphoreType.DMA((1 + KV_HEADS + HEADS,)),
         ],
-        out_specs=[stacked_block, stacked_block],
         compiler_params=pltpu.CompilerParams(vmem_limit_bytes=51 * 1024 * 1024),
         cost_estimate=pl.CostEstimate(
             flops=2 * ROWS * RANK * WIDE * 4, bytes_accessed=16 * ROWS * WIDE * 2, transcendentals=0
         ),
         name="stack",
     )(frozen_query, output_gradient, columns_first, adapter_up_weight)
-    arguments = (queries, grads, columns_first) + (adapter_up_weight,) * 3
-    light_arguments = (light_place, queries, grads, columns_first, adapter_up_weight, light)
+    arguments = (queries, grads) + (adapter_up_weight,) * 3
+    light_arguments = (light_place, queries, grads, adapter_up_weight, light)
     light_outs = (wide_out, terms_out, jax.ShapeDtypeStruct((3 * RANK, 2 * ROWS), F32))
-    vmem = pl.BlockSpec(memory_space=pltpu.VMEM)
     light_call = functools.partial(
         pl.pallas_call,
         out_shape=light_outs,
-        out_specs=[pl.BlockSpec(memory_space=pl.ANY), vmem, vmem],
+        out_specs=[anywhere, vmem, vmem],
         scratch_shapes=[pltpu.VMEM((2, 1, ROWS, WIDE), BF16), pltpu.SemaphoreType.DMA((2,))],
         compiler_params=pltpu.CompilerParams(vmem_limit_bytes=28 * 1024 * 1024),
         cost_estimate=cost(2),
     )
     in_smem = [pl.BlockSpec(memory_space=pltpu.SMEM)]
     attended, terms, low_terms = light_call(
-        early_kernel, in_specs=in_smem + [vmem] * 5, name="early_heads"
+        early_kernel, in_specs=in_smem + [vmem] * 4, name="early_heads"
     )(*light_arguments)
     one, two_even, attended = lax.optimization_barrier((one, two_even, attended))
     two_odd = send(one, 1, 2)
     three = send(two_even, 1, 2)
     attended, terms, low_terms = light_call(
         light_kernel,
-        in_specs=in_smem + [vmem] * 8 + [pl.BlockSpec(memory_space=pl.ANY)],
-        input_output_aliases={9: 0},
+        in_specs=in_smem + [vmem] * 7 + [anywhere],
+        input_output_aliases={8: 0},
         name="light_heads",
     )(*light_arguments, one, terms, low_terms, attended)
     back_out = jax.ShapeDtypeStruct((2 * RANK, ROWS), F32)
@@ -446,7 +458,7 @@
             + [pl.BlockSpec(memory_space=pl.ANY)] * 2,
             out_specs=[wide_half(), term_half(), whole(3 * RANK, ROWS)] + [back_spec] * 3,
         ),
-        input_output_aliases={14: 0, 15: 1},
+        input_output_aliases={13: 0, 14: 1},
         compiler_params=params(),
         cost_estimate=cost(4),
         name="heavy_heads",

time: 93.2 us -> 93.2 us (level)
  no operation moved by 1% of the time
where the time goes in v6:
time: 93.2 us; the launch traced here: 92.8 us
  blocking collectives  53.1 us (57%)
  starting transfers between devices  18.4 us (20%)
  Pallas kernels  15.6 us (17%)
  waiting for transfers between devices  4.01 us (4%)
    all_to_all x4, blocking collectives, exchange(): return lax.all_to_all(value, ('dp', 'ctx'), 0, 0, axis_index_groups=groups)  53.1 us
    ppermute x5, starting transfers between devices, send(): lax.ppermute(value, 'ctx', [(i, (i + by) % spans) for i in range(0, spans...  18.4 us
    pallas_call x1, Pallas kernels, shards(): pl.pallas_call(heavy_kernel, out_shape=(wide_out, terms_out, jax.ShapeDty...  6.52 us
    ppermute x5, waiting for transfers between devices, send(): lax.ppermute(value, 'ctx', [(i, (i + by) % spans) for i in range(0, spans...  4.01 us
    pallas_call x1, Pallas kernels, shards(): light_call(early_kernel, in_specs=in_smem + [vmem] * 4, name='early_heads')  3.37 us
    pallas_call x1, Pallas kernels, shards(): pl.pallas_call(stack_kernel, out_shape=(stacked_out, stacked_out), in_spe...  2.29 us
    pallas_call x1, Pallas kernels, shards(): pl.pallas_call(prepare_kernel, out_shape=(message, message), grid=(1,), i...  1.99 us
  transfers between devices with their start and end apart: 5, of which 3 were waited for; matrix products, arithmetic and copies ran while one was open for 0% of the time, Pallas kernels for 7%

profile of v6, /device:TPU:1, one launch (start us, length us, event | category | flops | bytes accessed | tf_op | source)
XLA Modules:
  0.0 92.8 jit_solution(3434640323634130207)
XLA Ops:
  0.6 2.0 %prepare.1 = (bf16[144,512]{1,0:T(8,128)(2,1)}, bf16[144,512]{1,0:T(8,128)(2,1)}) custom-call(bf16[1,128,1024]{2,1,0:T(8,128)(2,1)} %frozen.1, bf16[1,48,128]{2,1,0:T(8,128)(2,1)} %bitcast.6, bf16[16,5120]{1,0:T(8,128)(2,1)} %up_v.1), custom_call_target="tpu_custom_call" | custom-call | tf_op jit(solution)/shard_map/prepare/pallas_call | solution.py:383
  2.6 6.6 %collective-permute-start.1 = (bf16[144,512]{1,0:T(8,128)(2,1)}, bf16[144,512]{1,0:T(8,128)(2,1)S(1)}, u32[]{:S(2)}, u32[]{:S(2)}) collective-permute-start(bf16[144,512]{1,0:T(8,128)(2,1)} %get-tuple-element.31.own), channel_id=1, source_target_pairs={{0,2},{2,4},{4,6},{6,8},{8,10},{10,12},{12,14},{14,16},{16,18},{18... | collective-permute-start | bytes 442376 | tf_op jit(solution)/shard_map/ppermute | solution.py:398
  9.3 1.9 %collective-permute-start = (bf16[144,512]{1,0:T(8,128)(2,1)}, bf16[144,512]{1,0:T(8,128)(2,1)S(1)}, u32[]{:S(2)}, u32[]{:S(2)}) collective-permute-start(bf16[144,512]{1,0:T(8,128)(2,1)} %get-tuple-element.31.own), channel_id=1, source_target_pairs={{0,1},{1,2},{2,3},{3,4},{4,5},{5,6},{6,7},{7,8},{8,9},{9,10},{10,1... | collective-permute-start | bytes 442376 | tf_op jit(solution)/shard_map/ppermute | solution.py:398
  11.2 7.3 %collective-permute-start.2 = (bf16[144,512]{1,0:T(8,128)(2,1)}, bf16[144,512]{1,0:T(8,128)(2,1)S(1)}, u32[]{:S(2)}, u32[]{:S(2)}) collective-permute-start(bf16[144,512]{1,0:T(8,128)(2,1)} %get-tuple-element.30.own), channel_id=1, source_target_pairs={{0,1},{2,3},{4,5},{6,7},{8,9},{10,11},{12,13},{14,15},{16,17},{18,... | collective-permute-start | bytes 442376 | tf_op jit(solution)/shard_map/ppermute | solution.py:398
  18.5 0.0 copy-start.2
  18.6 0.7 copy-done.2
  19.2 2.3 %stack.31 = (bf16[4096,128]{1,0:T(8,128)(2,1)S(1)}, bf16[4096,128]{1,0:T(8,128)(2,1)S(1)}) custom-call(bf16[1,128,4096]{2,1,0:T(8,128)(2,1)} %query.1, bf16[1,128,4096]{2,1,0:T(8,128)(2,1)} %grad.1, bf16[1,48,128]{2,1,0:T(8,128)(2,1)S(1)} %bitcast.7, bf16[16,5120]{1,0:T(8,128)(2,1)S(1)} %copy-done), custom_call_target="tpu_custom_call" | custom-call | flops 16777216 | bytes 4194304 | tf_op jit(solution)/shard_map/stack/pallas_call | solution.py:407
  21.5 0.1 pad_add_fusion.1.place
  21.6 3.4 %early_heads.1 = (bf16[1,128,4096]{2,1,0:T(8,128)(2,1)}, bf16[8,80,128]{2,1,0:T(8,128)(2,1)S(1)}, f32[48,256]{1,0:T(8,128)S(1)}) custom-call(s32[3]{0:T(128)S(1)} %pad_add_fusion.1.place, bf16[4096,128]{1,0:T(8,128)(2,1)S(1)} %get-tuple-element.28.query, bf16[4096,128]{1,0:T(8,128)(2,1)S(1)} %get-tuple-element.29.grad, bf16[16,5120]{1,0:T(8,128)(2,1)S(1)} %copy-done, ...), custom_call_target="tpu_custom_call" | custom-call | flops 805306368 | bytes 1572864 | tf_op jit(solution)/shard_map/early_heads/pallas_call | solution.py:435
  25.0 2.4 %collective-permute-done.1.two_even = bf16[144,512]{1,0:T(8,128)(2,1)S(1)} collective-permute-done((bf16[144,512]{1,0:T(8,128)(2,1)}, bf16[144,512]{1,0:T(8,128)(2,1)S(1)}, u32[]{:S(2)}, u32[]{:S(2)}) %collective-permute-start.1) | collective-permute-done | bytes 147488 | tf_op jit(solution)/shard_map/ppermute | solution.py:398
  27.4 0.0 collective-permute-done.one.one_even
  27.4 1.3 %collective-permute-start.4 = (bf16[144,512]{1,0:T(8,128)(2,1)S(1)}, bf16[144,512]{1,0:T(8,128)(2,1)S(1)}, u32[]{:S(2)}, u32[]{:S(2)}) collective-permute-start(bf16[144,512]{1,0:T(8,128)(2,1)S(1)} %collective-permute-done.1.two_even), channel_id=1, source_target_pairs={{0,1},{2,3},{4,5},{6,7},{8,9},{10,11},{12,13},{14,15},{16,17},{18,... | collective-permute-start | bytes 442376 | tf_op jit(solution)/shard_map/ppermute | solution.py:398
  28.6 1.3 %collective-permute-start.3 = (bf16[144,512]{1,0:T(8,128)(2,1)S(1)}, bf16[144,512]{1,0:T(8,128)(2,1)S(1)}, u32[]{:S(2)}, u32[]{:S(2)}) collective-permute-start(bf16[144,512]{1,0:T(8,128)(2,1)S(1)} %collective-permute-done.one.one_even), channel_id=1, source_target_pairs={{0,1},{2,3},{4,5},{6,7},{8,9},{10,11},{12,13},{14,15},{16,17},{18,... | collective-permute-start | bytes 442376 | tf_op jit(solution)/shard_map/ppermute | solution.py:398
  30.0 0.1 pad_add_fusion.place
  30.0 0.6 light_heads.1
  30.6 0.1 collective-permute-done.4.three
  30.7 1.6 %collective-permute-done.3.two_odd = bf16[144,512]{1,0:T(8,128)(2,1)S(1)} collective-permute-done((bf16[144,512]{1,0:T(8,128)(2,1)S(1)}, bf16[144,512]{1,0:T(8,128)(2,1)S(1)}, u32[]{:S(2)}, u32[]{:S(2)}) %collective-permute-start.3) | collective-permute-done | bytes 147488 | tf_op jit(solution)/shard_map/ppermute | solution.py:398
  32.3 6.5 %heavy_heads.1 = (bf16[1,128,4096]{2,1,0:T(8,128)(2,1)}, bf16[8,80,128]{2,1,0:T(8,128)(2,1)S(1)}, f32[48,128]{1,0:T(8,128)S(1)}, f32[32,128]{1,0:T(8,128)S(1)}, ...) custom-call(s32[2]{0:T(128)S(1)} %pad_add_fusion.place, ...), custom_call_target="tpu_custom_call", output_to_operand_aliasing={{0}: (13, {}), {1}: (14, {})} | custom-call | flops 1610612736 | bytes 1572864 | tf_op jit(solution)/shard_map/heavy_heads/pallas_call | solution.py:449
  38.8 11.5 %all_to_all.20.parts = bf16[8,80,128]{2,1,0:T(8,128)(2,1)S(1)} all-to-all(bf16[8,80,128]{2,1,0:T(8,128)(2,1)S(1)} %get-tuple-element.42), channel_id=1, replica_groups={{0,64,16,80,32,96,48,112},{1,65,17,81,33,97,49,113},{2,66,18,82,34,98,5..., dimensions={0} | all-to-all | bytes 327680 | tf_op jit(solution)/shard_map/all_to_all | solution.py:277
  50.4 13.0 %all_to_all.21.parts = bf16[8,112,128]{2,1,0:T(8,128)(2,1)S(1)} all-to-all(bf16[8,112,128]{2,1,0:T(8,128)(2,1)S(1)} %along.1), channel_id=1, replica_groups={{0,1,2,3,4,5,6,7},{64,65,66,67,68,69,70,71},{128,129,130,131,132,133,13..., dimensions={0} | all-to-all | bytes 458752 | tf_op jit(solution)/shard_map/all_to_all | solution.py:277
  63.4 0.1 beside.1
  63.4 15.8 %all_to_all.22.parts = bf16[8,112,128]{2,1,0:T(8,128)(2,1)S(1)} all-to-all(bf16[8,112,128]{2,1,0:T(8,128)(2,1)S(1)} %get-tuple-element.46), channel_id=1, replica_groups={{0,128,256,384,8,136,264,392},{64,192,320,448,72,200,328,456},{1,129,25..., dimensions={0} | all-to-all | bytes 458752 | tf_op jit(solution)/shard_map/all_to_all | solution.py:277
  79.3 12.7 %all_to_all.23.parts = bf16[8,112,128]{2,1,0:T(8,128)(2,1)S(1)} all-to-all(bf16[8,112,128]{2,1,0:T(8,128)(2,1)S(1)} %get-tuple-element.47), channel_id=1, replica_groups={{0,64,16,80,32,96,48,112},{1,65,17,81,33,97,49,113},{2,66,18,82,34,98,5..., dimensions={0} | all-to-all | bytes 458752 | tf_op jit(solution)/shard_map/all_to_all | solution.py:277
  92.0 0.8 assemble.1
  (9 shorter events, 0.1 us)
Async XLA Ops:
  0.6 17.9 %copy-start = (bf16[16,5120]{1,0:T(8,128)(2,1)S(1)}, bf16[16,5120]{1,0:T(8,128)(2,1)}, u32[]{:S(2)}) copy-start(bf16[16,5120]{1,0:T(8,128)(2,1)} %up_v.1) | copy-start | bytes 491524
  2.6 24.7 %collective-permute-start.1 = (bf16[144,512]{1,0:T(8,128)(2,1)}, bf16[144,512]{1,0:T(8,128)(2,1)S(1)}, u32[]{:S(2)}, u32[]{:S(2)}) collective-permute-start(bf16[144,512]{1,0:T(8,128)(2,1)} %get-tuple-element.31.own), channel_id=1, source_target_pairs={{0,2},{2,4},{4,6},{6,8},{8,10},{10,12},{12,14},{14,16},{16,18},{18... | collective-permute-start | bytes 442376 | tf_op jit(solution)/shard_map/ppermute | solution.py:398
  9.3 18.1 %collective-permute-start = (bf16[144,512]{1,0:T(8,128)(2,1)}, bf16[144,512]{1,0:T(8,128)(2,1)S(1)}, u32[]{:S(2)}, u32[]{:S(2)}) collective-permute-start(bf16[144,512]{1,0:T(8,128)(2,1)} %get-tuple-element.31.own), channel_id=1, source_target_pairs={{0,1},{1,2},{2,3},{3,4},{4,5},{5,6},{6,7},{7,8},{8,9},{9,10},{10,1... | collective-permute-start | bytes 442376 | tf_op jit(solution)/shard_map/ppermute | solution.py:398
  11.2 19.4 %collective-permute-start.2 = (bf16[144,512]{1,0:T(8,128)(2,1)}, bf16[144,512]{1,0:T(8,128)(2,1)S(1)}, u32[]{:S(2)}, u32[]{:S(2)}) collective-permute-start(bf16[144,512]{1,0:T(8,128)(2,1)} %get-tuple-element.30.own), channel_id=1, source_target_pairs={{0,1},{2,3},{4,5},{6,7},{8,9},{10,11},{12,13},{14,15},{16,17},{18,... | collective-permute-start | bytes 442376 | tf_op jit(solution)/shard_map/ppermute | solution.py:398
  18.5 0.7 copy-start.2
  19.2 2.4 %copy-start.1 = (bf16[144,512]{1,0:T(8,128)(2,1)S(1)}, bf16[144,512]{1,0:T(8,128)(2,1)}, u32[]{:S(2)}) copy-start(bf16[144,512]{1,0:T(8,128)(2,1)} %get-tuple-element.31.own) | copy-start | bytes 442372
  27.4 3.4 %collective-permute-start.4 = (bf16[144,512]{1,0:T(8,128)(2,1)S(1)}, bf16[144,512]{1,0:T(8,128)(2,1)S(1)}, u32[]{:S(2)}, u32[]{:S(2)}) collective-permute-start(bf16[144,512]{1,0:T(8,128)(2,1)S(1)} %collective-permute-done.1.two_even), channel_id=1, source_target_pairs={{0,1},{2,3},{4,5},{6,7},{8,9},{10,11},{12,13},{14,15},{16,17},{18,... | collective-permute-start | bytes 442376 | tf_op jit(solution)/shard_map/ppermute | solution.py:398
  28.6 3.6 %collective-permute-start.3 = (bf16[144,512]{1,0:T(8,128)(2,1)S(1)}, bf16[144,512]{1,0:T(8,128)(2,1)S(1)}, u32[]{:S(2)}, u32[]{:S(2)}) collective-permute-start(bf16[144,512]{1,0:T(8,128)(2,1)S(1)} %collective-permute-done.one.one_even), channel_id=1, source_target_pairs={{0,1},{2,3},{4,5},{6,7},{8,9},{10,11},{12,13},{14,15},{16,17},{18,... | collective-permute-start | bytes 442376 | tf_op jit(solution)/shard_map/ppermute | solution.py:398
  30.0 2.3 %copy-start.3 = (bf16[144,512]{1,0:T(8,128)(2,1)S(1)}, bf16[144,512]{1,0:T(8,128)(2,1)}, u32[]{:S(2)}) copy-start(bf16[144,512]{1,0:T(8,128)(2,1)} %get-tuple-element.30.own) | copy-start | bytes 442372

commit v7 on v6

--- a/solution.py
+++ b/solution.py
@@ -399,7 +399,6 @@
 
     one = send(light, 1)
     two_even = send(light, 2, 2)
-    one_odd = send(heavy, 1, 2)
     wide_out = jax.ShapeDtypeStruct((1, ROWS, HEADS * D_HEAD), BF16)
     terms_out = jax.ShapeDtypeStruct((2 * KV_HEADS, PART, D_HEAD), BF16)
     stacked_out = jax.ShapeDtypeStruct((HEADS * ROWS, D_HEAD), BF16)
@@ -420,6 +419,8 @@
         ),
         name="stack",
     )(frozen_query, output_gradient, columns_first, adapter_up_weight)
+    queries, sent = lax.optimization_barrier((queries, heavy))
+    one_odd = send(sent, 1, 2)
     arguments = (queries, grads) + (adapter_up_weight,) * 3
     light_arguments = (light_place, queries, grads, adapter_up_weight, light)
     light_outs = (wide_out, terms_out, jax.ShapeDtypeStruct((3 * RANK, 2 * ROWS), F32))
@@ -435,9 +436,10 @@
     attended, terms, low_terms = light_call(
         early_kernel, in_specs=in_smem + [vmem] * 4, name="early_heads"
     )(*light_arguments)
-    one, two_even, attended = lax.optimization_barrier((one, two_even, attended))
+    two_even, attended = lax.optimization_barrier((two_even, attended))
+    three = send(two_even, 1, 2)
+    one, attended = lax.optimization_barrier((one, attended))
     two_odd = send(one, 1, 2)
-    three = send(two_even, 1, 2)
     attended, terms, low_terms = light_call(
         light_kernel,
         in_specs=in_smem + [vmem] * 7 + [anywhere],

time: 93.2 us -> 93.2 us (level)
  no operation moved by 1% of the time
where the time goes in v7:
time: 93.2 us; the launch traced here: 92.8 us
  blocking collectives  53 us (57%)
  starting transfers between devices  18.6 us (20%)
  Pallas kernels  15.6 us (17%)
  waiting for transfers between devices  4.71 us (5%)
    all_to_all x4, blocking collectives, exchange(): return lax.all_to_all(value, ('dp', 'ctx'), 0, 0, axis_index_groups=groups)  53 us
    ppermute x5, starting transfers between devices, send(): lax.ppermute(value, 'ctx', [(i, (i + by) % spans) for i in range(0, spans...  18.6 us
    pallas_call x1, Pallas kernels, shards(): pl.pallas_call(heavy_kernel, out_shape=(wide_out, terms_out, jax.ShapeDty...  6.5 us
    ppermute x5, waiting for transfers between devices, send(): lax.ppermute(value, 'ctx', [(i, (i + by) % spans) for i in range(0, spans...  4.71 us
    pallas_call x1, Pallas kernels, shards(): light_call(early_kernel, in_specs=in_smem + [vmem] * 4, name='early_heads')  3.37 us
    pallas_call x1, Pallas kernels, shards(): pl.pallas_call(stack_kernel, out_shape=(stacked_out, stacked_out), in_spe...  2.26 us
    pallas_call x1, Pallas kernels, shards(): pl.pallas_call(prepare_kernel, out_shape=(message, message), grid=(1,), i...  1.99 us
  transfers between devices with their start and end apart: 5, of which 3 were waited for; matrix products, arithmetic and copies ran while one was open for 0% of the time, Pallas kernels for 7%

profile of v7, /device:TPU:1, one launch (start us, length us, event | category | flops | bytes accessed | tf_op | source)
XLA Modules:
  0.0 92.8 jit_solution(2258814565781604238)
XLA Ops:
  0.6 0.0 copy-start
  0.7 2.0 %prepare.1 = (bf16[144,512]{1,0:T(8,128)(2,1)}, bf16[144,512]{1,0:T(8,128)(2,1)}) custom-call(bf16[1,128,1024]{2,1,0:T(8,128)(2,1)} %frozen.1, bf16[1,48,128]{2,1,0:T(8,128)(2,1)} %bitcast.6, bf16[16,5120]{1,0:T(8,128)(2,1)} %up_v.1), custom_call_target="tpu_custom_call" | custom-call | tf_op jit(solution)/shard_map/prepare/pallas_call | solution.py:383
  2.6 6.8 %collective-permute-start.1 = (bf16[144,512]{1,0:T(8,128)(2,1)}, bf16[144,512]{1,0:T(8,128)(2,1)S(1)}, u32[]{:S(2)}, u32[]{:S(2)}) collective-permute-start(bf16[144,512]{1,0:T(8,128)(2,1)} %get-tuple-element.35.own), channel_id=1, source_target_pairs={{0,2},{2,4},{4,6},{6,8},{8,10},{10,12},{12,14},{14,16},{16,18},{18... | collective-permute-start | bytes 442376 | tf_op jit(solution)/shard_map/ppermute | solution.py:398
  9.4 1.9 %collective-permute-start = (bf16[144,512]{1,0:T(8,128)(2,1)}, bf16[144,512]{1,0:T(8,128)(2,1)S(1)}, u32[]{:S(2)}, u32[]{:S(2)}) collective-permute-start(bf16[144,512]{1,0:T(8,128)(2,1)} %get-tuple-element.35.own), channel_id=1, source_target_pairs={{0,1},{1,2},{2,3},{3,4},{4,5},{5,6},{6,7},{7,8},{8,9},{9,10},{10,1... | collective-permute-start | bytes 442376 | tf_op jit(solution)/shard_map/ppermute | solution.py:398
  11.4 2.3 %stack.31 = (bf16[4096,128]{1,0:T(8,128)(2,1)S(1)}, bf16[4096,128]{1,0:T(8,128)(2,1)S(1)}) custom-call(bf16[1,128,4096]{2,1,0:T(8,128)(2,1)} %query.1, bf16[1,128,4096]{2,1,0:T(8,128)(2,1)} %grad.1, bf16[1,48,128]{2,1,0:T(8,128)(2,1)S(1)} %bitcast.7, bf16[16,5120]{1,0:T(8,128)(2,1)S(1)} %copy-done), custom_call_target="tpu_custom_call" | custom-call | flops 16777216 | bytes 4194304 | tf_op jit(solution)/shard_map/stack/pallas_call | solution.py:406
  13.6 7.3 %collective-permute-start.2 = (bf16[144,512]{1,0:T(8,128)(2,1)S(1)}, bf16[144,512]{1,0:T(8,128)(2,1)S(1)}, u32[]{:S(2)}, u32[]{:S(2)}) collective-permute-start(bf16[144,512]{1,0:T(8,128)(2,1)S(1)} %copy-done.3), channel_id=1, source_target_pairs={{0,1},{2,3},{4,5},{6,7},{8,9},{10,11},{12,13},{14,15},{16,17},{18,... | collective-permute-start | bytes 442376 | tf_op jit(solution)/shard_map/ppermute | solution.py:398
  21.0 0.1 pad_add_fusion.1.place
  21.1 3.4 %early_heads.1 = (bf16[1,128,4096]{2,1,0:T(8,128)(2,1)}, bf16[8,80,128]{2,1,0:T(8,128)(2,1)S(1)}, f32[48,256]{1,0:T(8,128)S(1)}) custom-call(s32[3]{0:T(128)S(1)} %pad_add_fusion.1.place, bf16[4096,128]{1,0:T(8,128)(2,1)S(1)} %get-tuple-element.33.query, bf16[4096,128]{1,0:T(8,128)(2,1)S(1)} %get-tuple-element.34.grad, bf16[16,5120]{1,0:T(8,128)(2,1)S(1)} %copy-done, ...), custom_call_target="tpu_custom_call" | custom-call | flops 805306368 | bytes 1572864 | tf_op jit(solution)/shard_map/early_heads/pallas_call | solution.py:436
  24.4 3.0 %collective-permute-done.1.two_even = bf16[144,512]{1,0:T(8,128)(2,1)S(1)} collective-permute-done((bf16[144,512]{1,0:T(8,128)(2,1)}, bf16[144,512]{1,0:T(8,128)(2,1)S(1)}, u32[]{:S(2)}, u32[]{:S(2)}) %collective-permute-start.1) | collective-permute-done | bytes 147488 | tf_op jit(solution)/shard_map/ppermute | solution.py:398
  27.5 0.0 collective-permute-done.one.one_even
  27.5 1.3 %collective-permute-start.3 = (bf16[144,512]{1,0:T(8,128)(2,1)S(1)}, bf16[144,512]{1,0:T(8,128)(2,1)S(1)}, u32[]{:S(2)}, u32[]{:S(2)}) collective-permute-start(bf16[144,512]{1,0:T(8,128)(2,1)S(1)} %collective-permute-done.one.one_even), channel_id=1, source_target_pairs={{0,1},{2,3},{4,5},{6,7},{8,9},{10,11},{12,13},{14,15},{16,17},{18,... | collective-permute-start | bytes 442376 | tf_op jit(solution)/shard_map/ppermute | solution.py:398
  28.8 1.3 %collective-permute-start.4 = (bf16[144,512]{1,0:T(8,128)(2,1)S(1)}, bf16[144,512]{1,0:T(8,128)(2,1)S(1)}, u32[]{:S(2)}, u32[]{:S(2)}) collective-permute-start(bf16[144,512]{1,0:T(8,128)(2,1)S(1)} %collective-permute-done.1.two_even), channel_id=1, source_target_pairs={{0,1},{2,3},{4,5},{6,7},{8,9},{10,11},{12,13},{14,15},{16,17},{18,... | collective-permute-start | bytes 442376 | tf_op jit(solution)/shard_map/ppermute | solution.py:398
  30.1 0.1 pad_add_fusion.place
  30.2 0.6 light_heads.1
  30.8 0.0 collective-permute-done.2.one_odd
  30.8 0.1 collective-permute-done.3.two_odd
  30.9 1.6 %collective-permute-done.4.three = bf16[144,512]{1,0:T(8,128)(2,1)S(1)} collective-permute-done((bf16[144,512]{1,0:T(8,128)(2,1)S(1)}, bf16[144,512]{1,0:T(8,128)(2,1)S(1)}, u32[]{:S(2)}, u32[]{:S(2)}) %collective-permute-start.4) | collective-permute-done | bytes 147488 | tf_op jit(solution)/shard_map/ppermute | solution.py:398
  32.4 6.5 %heavy_heads.1 = (bf16[1,128,4096]{2,1,0:T(8,128)(2,1)}, bf16[8,80,128]{2,1,0:T(8,128)(2,1)S(1)}, f32[48,128]{1,0:T(8,128)S(1)}, f32[32,128]{1,0:T(8,128)S(1)}, ...) custom-call(s32[2]{0:T(128)S(1)} %pad_add_fusion.place, ...), custom_call_target="tpu_custom_call", output_to_operand_aliasing={{0}: (13, {}), {1}: (14, {})} | custom-call | flops 1610612736 | bytes 1572864 | tf_op jit(solution)/shard_map/heavy_heads/pallas_call | solution.py:451
  38.9 11.5 %all_to_all.20.parts = bf16[8,80,128]{2,1,0:T(8,128)(2,1)S(1)} all-to-all(bf16[8,80,128]{2,1,0:T(8,128)(2,1)S(1)} %get-tuple-element.48), channel_id=1, replica_groups={{0,64,16,80,32,96,48,112},{1,65,17,81,33,97,49,113},{2,66,18,82,34,98,5..., dimensions={0} | all-to-all | bytes 327680 | tf_op jit(solution)/shard_map/all_to_all | solution.py:277
  50.5 13.0 %all_to_all.21.parts = bf16[8,112,128]{2,1,0:T(8,128)(2,1)S(1)} all-to-all(bf16[8,112,128]{2,1,0:T(8,128)(2,1)S(1)} %along.1), channel_id=1, replica_groups={{0,1,2,3,4,5,6,7},{64,65,66,67,68,69,70,71},{128,129,130,131,132,133,13..., dimensions={0} | all-to-all | bytes 458752 | tf_op jit(solution)/shard_map/all_to_all | solution.py:277
  63.5 0.1 beside.1
  63.6 15.7 %all_to_all.22.parts = bf16[8,112,128]{2,1,0:T(8,128)(2,1)S(1)} all-to-all(bf16[8,112,128]{2,1,0:T(8,128)(2,1)S(1)} %get-tuple-element.52), channel_id=1, replica_groups={{0,128,256,384,8,136,264,392},{64,192,320,448,72,200,328,456},{1,129,25..., dimensions={0} | all-to-all | bytes 458752 | tf_op jit(solution)/shard_map/all_to_all | solution.py:277
  79.3 12.7 %all_to_all.23.parts = bf16[8,112,128]{2,1,0:T(8,128)(2,1)S(1)} all-to-all(bf16[8,112,128]{2,1,0:T(8,128)(2,1)S(1)} %get-tuple-element.53), channel_id=1, replica_groups={{0,64,16,80,32,96,48,112},{1,65,17,81,33,97,49,113},{2,66,18,82,34,98,5..., dimensions={0} | all-to-all | bytes 458752 | tf_op jit(solution)/shard_map/all_to_all | solution.py:277
  92.0 0.8 assemble.1
  (9 shorter events, 0.1 us)
Async XLA Ops:
  0.6 10.7 %copy-start = (bf16[16,5120]{1,0:T(8,128)(2,1)S(1)}, bf16[16,5120]{1,0:T(8,128)(2,1)}, u32[]{:S(2)}) copy-start(bf16[16,5120]{1,0:T(8,128)(2,1)} %up_v.1) | copy-start | bytes 491524
  0.6 10.7 %copy-start.2 = (bf16[1,128,48]{1,2,0:T(8,128)(2,1)S(1)}, bf16[1,128,48]{1,2,0:T(8,128)(2,1)}, u32[]{:S(2)}) copy-start(bf16[1,128,48]{1,2,0:T(8,128)(2,1)} %param.7) | copy-start | bytes 36868
  2.6 11.0 %copy-start.3 = (bf16[144,512]{1,0:T(8,128)(2,1)S(1)}, bf16[144,512]{1,0:T(8,128)(2,1)}, u32[]{:S(2)}) copy-start(bf16[144,512]{1,0:T(8,128)(2,1)} %get-tuple-element.39.own) | copy-start | bytes 442372
  2.6 18.4 %copy-start.1 = (bf16[144,512]{1,0:T(8,128)(2,1)S(1)}, bf16[144,512]{1,0:T(8,128)(2,1)}, u32[]{:S(2)}) copy-start(bf16[144,512]{1,0:T(8,128)(2,1)} %get-tuple-element.35.own) | copy-start | bytes 442372
  2.6 24.9 %collective-permute-start.1 = (bf16[144,512]{1,0:T(8,128)(2,1)}, bf16[144,512]{1,0:T(8,128)(2,1)S(1)}, u32[]{:S(2)}, u32[]{:S(2)}) collective-permute-start(bf16[144,512]{1,0:T(8,128)(2,1)} %get-tuple-element.35.own), channel_id=1, source_target_pairs={{0,2},{2,4},{4,6},{6,8},{8,10},{10,12},{12,14},{14,16},{16,18},{18... | collective-permute-start | bytes 442376 | tf_op jit(solution)/shard_map/ppermute | solution.py:398
  9.4 18.1 %collective-permute-start = (bf16[144,512]{1,0:T(8,128)(2,1)}, bf16[144,512]{1,0:T(8,128)(2,1)S(1)}, u32[]{:S(2)}, u32[]{:S(2)}) collective-permute-start(bf16[144,512]{1,0:T(8,128)(2,1)} %get-tuple-element.35.own), channel_id=1, source_target_pairs={{0,1},{1,2},{2,3},{3,4},{4,5},{5,6},{6,7},{7,8},{8,9},{9,10},{10,1... | collective-permute-start | bytes 442376 | tf_op jit(solution)/shard_map/ppermute | solution.py:398
  13.6 17.1 %collective-permute-start.2 = (bf16[144,512]{1,0:T(8,128)(2,1)S(1)}, bf16[144,512]{1,0:T(8,128)(2,1)S(1)}, u32[]{:S(2)}, u32[]{:S(2)}) collective-permute-start(bf16[144,512]{1,0:T(8,128)(2,1)S(1)} %copy-done.3), channel_id=1, source_target_pairs={{0,1},{2,3},{4,5},{6,7},{8,9},{10,11},{12,13},{14,15},{16,17},{18,... | collective-permute-start | bytes 442376 | tf_op jit(solution)/shard_map/ppermute | solution.py:398
  27.5 3.4 %collective-permute-start.3 = (bf16[144,512]{1,0:T(8,128)(2,1)S(1)}, bf16[144,512]{1,0:T(8,128)(2,1)S(1)}, u32[]{:S(2)}, u32[]{:S(2)}) collective-permute-start(bf16[144,512]{1,0:T(8,128)(2,1)S(1)} %collective-permute-done.one.one_even), channel_id=1, source_target_pairs={{0,1},{2,3},{4,5},{6,7},{8,9},{10,11},{12,13},{14,15},{16,17},{18,... | collective-permute-start | bytes 442376 | tf_op jit(solution)/shard_map/ppermute | solution.py:398
  28.8 3.6 %collective-permute-start.4 = (bf16[144,512]{1,0:T(8,128)(2,1)S(1)}, bf16[144,512]{1,0:T(8,128)(2,1)S(1)}, u32[]{:S(2)}, u32[]{:S(2)}) collective-permute-start(bf16[144,512]{1,0:T(8,128)(2,1)S(1)} %collective-permute-done.1.two_even), channel_id=1, source_target_pairs={{0,1},{2,3},{4,5},{6,7},{8,9},{10,11},{12,13},{14,15},{16,17},{18,... | collective-permute-start | bytes 442376 | tf_op jit(solution)/shard_map/ppermute | solution.py:398

commit v8 on v4

--- a/solution.py
+++ b/solution.py
@@ -65,12 +65,27 @@
         write(heavy, light)
 
 
-def stack_kernel(query, grad, low, up_q, queries, grads):
-    found = (query[0].astype(F32) + 2.0 * t_mul(low[0, :RANK, :], up_q[...])).astype(BF16)
-    for i in range(SHARE):
-        rows, cols = slice(i * ROWS, (i + 1) * ROWS), slice(i * D_HEAD, (i + 1) * D_HEAD)
-        queries[rows, :] = found[:, cols]
-        grads[rows, :] = grad[0, :, cols]
+def stack_kernel(query, grad, low_all, up, queries, grads, held, low, sems):
+    copies = [pltpu.make_async_copy(low_all.at[0, pl.ds(0, RANK), :], low, sems.at[0])]
+    for i in range(KV_HEADS):
+        wide = query.at[0, :, pl.ds(i * WIDE, WIDE)]
+        copies.append(pltpu.make_async_copy(wide, held.at[i], sems.at[1 + i]))
+    for i in range(HEADS):
+        head = grad.at[0, :, pl.ds(i * D_HEAD, D_HEAD)]
+        place = grads.at[pl.ds(i * ROWS, ROWS), :]
+        copies.append(pltpu.make_async_copy(head, place, sems.at[1 + KV_HEADS + i]))
+    for copy in copies:
+        copy.start()
+    copies[0].wait()
+    for i in range(KV_HEADS):
+        added = 2.0 * t_mul(low[...], up[:, i * WIDE : (i + 1) * WIDE])
+        copies[1 + i].wait()
+        found = (held[i].astype(F32) + added).astype(BF16)
+        for k in range(SHARE):
+            rows = slice((i * SHARE + k) * ROWS, (i * SHARE + k + 1) * ROWS)
+            queries[rows, :] = found[:, k * D_HEAD : (k + 1) * D_HEAD]
+    for copy in copies[1 + KV_HEADS :]:
+        copy.wait()
 
 
 def attend(place, query, grad, low, up_q, up_k, up_v, blocks, closed, attended, terms):
@@ -355,20 +370,18 @@
     wide_out = jax.ShapeDtypeStruct((1, ROWS, HEADS * D_HEAD), BF16)
     terms_out = jax.ShapeDtypeStruct((2 * KV_HEADS, PART, D_HEAD), BF16)
     stacked_out = jax.ShapeDtypeStruct((HEADS * ROWS, D_HEAD), BF16)
-    wide_block = pl.BlockSpec((1, ROWS, WIDE), lambda i: (0, 0, i))
-    stacked_block = pl.BlockSpec((SHARE * ROWS, D_HEAD), lambda i: (i, 0))
+    vmem, anywhere = pl.BlockSpec(memory_space=pltpu.VMEM), pl.BlockSpec(memory_space=pl.ANY)
     queries, grads = pl.pallas_call(
         stack_kernel,
         out_shape=(stacked_out, stacked_out),
-        grid=(KV_HEADS,),
-        in_specs=[
-            wide_block,
-            wide_block,
-            only(1, 3 * RANK, ROWS),
-            pl.BlockSpec((RANK, WIDE), lambda i: (0, i)),
+        in_specs=[anywhere] * 3 + [vmem],
+        out_specs=[vmem] * 2,
+        scratch_shapes=[
+            pltpu.VMEM((KV_HEADS, ROWS, WIDE), BF16),
+            pltpu.VMEM((RANK, D_HEAD), BF16),
+            pltpu.SemaphoreType.DMA((1 + KV_HEADS + HEADS,)),
         ],
-        out_specs=[stacked_block, stacked_block],
-        compiler_params=pltpu.CompilerParams(vmem_limit_bytes=16 * 1024 * 1024),
+        compiler_params=pltpu.CompilerParams(vmem_limit_bytes=51 * 1024 * 1024),
         cost_estimate=pl.CostEstimate(
             flops=2 * ROWS * RANK * WIDE * 4, bytes_accessed=16 * ROWS * WIDE * 2, transcendentals=0
         ),

time: 91.9 us -> 91 us (level)
  local copies, waits for them, and re-layouts: 3.14 us -> 0.69 us
  waiting for transfers between devices: 4.35 us -> 5.76 us
    unnamed x12 -> x8, local copies, waits for them, and re-layouts: 3.14 us -> 0.69 us
    ppermute x5, waiting for transfers between devices: 4.35 us -> 5.76 us  [send(): lax.ppermute(value, 'ctx', [(i, (i + by) % spans) for i in range(0, spans...]
    pallas_call x1, Pallas kernels: 1.26 us -> 2.29 us  [shards(): pl.pallas_call(stack_kernel, out_shape=(stacked_out, stacked_out), in_spe...]
  transfers between devices with their start and end apart: 5 -> 5, of which waited for: 1 -> 1; matrix products, arithmetic and copies ran while one was open for 0% -> 0% of each run, Pallas kernels for 7% -> 8%
where the time goes in v8:
time: 91 us; the launch traced here: 90.6 us
  blocking collectives  48.4 us (53%)
  starting transfers between devices  18.4 us (20%)
  Pallas kernels  16.3 us (18%)
  waiting for transfers between devices  5.76 us (6%)
    all_to_all x4, blocking collectives, exchange(): return lax.all_to_all(value, ('dp', 'ctx'), 0, 0, axis_index_groups=groups)  48.4 us
    ppermute x5, starting transfers between devices, send(): lax.ppermute(value, 'ctx', [(i, (i + by) % spans) for i in range(0, spans...  18.4 us
    pallas_call x1, Pallas kernels, shards(): pl.pallas_call(heavy_kernel, out_shape=(wide_out, terms_out, jax.ShapeDty...  6.51 us
    ppermute x5, waiting for transfers between devices, send(): lax.ppermute(value, 'ctx', [(i, (i + by) % spans) for i in range(0, spans...  5.76 us
    pallas_call x1, Pallas kernels, shards(): pl.pallas_call(light_kernel, out_shape=(wide_out, terms_out, jax.ShapeDty...  4.67 us
    pallas_call x1, Pallas kernels, shards(): pl.pallas_call(stack_kernel, out_shape=(stacked_out, stacked_out), in_spe...  2.29 us
    pallas_call x1, Pallas kernels, shards(): pl.pallas_call(prepare_kernel, out_shape=(message, message), grid=(1,), i...  1.99 us
  transfers between devices with their start and end apart: 5, of which 1 were waited for; matrix products, arithmetic and copies ran while one was open for 0% of the time, Pallas kernels for 8%

profile of v8, /device:TPU:1, one launch (start us, length us, event | category | flops | bytes accessed | tf_op | source)
XLA Modules:
  0.0 90.6 jit_solution(4205939878934403742)
XLA Ops:
  0.6 2.0 %prepare.1 = (bf16[144,512]{1,0:T(8,128)(2,1)}, bf16[144,512]{1,0:T(8,128)(2,1)}) custom-call(bf16[1,128,1024]{2,1,0:T(8,128)(2,1)} %frozen.1, bf16[1,48,128]{2,1,0:T(8,128)(2,1)} %bitcast.5, bf16[16,5120]{1,0:T(8,128)(2,1)} %up_v.3), custom_call_target="tpu_custom_call" | custom-call | tf_op jit(solution)/shard_map/prepare/pallas_call | solution.py:348
  2.6 6.6 %collective-permute-start.2 = (bf16[144,512]{1,0:T(8,128)(2,1)}, bf16[144,512]{1,0:T(8,128)(2,1)S(1)}, u32[]{:S(2)}, u32[]{:S(2)}) collective-permute-start(bf16[144,512]{1,0:T(8,128)(2,1)} %get-tuple-element.25.own), channel_id=1, source_target_pairs={{0,2},{2,4},{4,6},{6,8},{8,10},{10,12},{12,14},{14,16},{16,18},{18... | collective-permute-start | bytes 442376 | tf_op jit(solution)/shard_map/ppermute | solution.py:363
  9.3 1.9 %collective-permute-start = (bf16[144,512]{1,0:T(8,128)(2,1)}, bf16[144,512]{1,0:T(8,128)(2,1)S(1)}, u32[]{:S(2)}, u32[]{:S(2)}) collective-permute-start(bf16[144,512]{1,0:T(8,128)(2,1)} %get-tuple-element.25.own), channel_id=1, source_target_pairs={{0,1},{1,2},{2,3},{3,4},{4,5},{5,6},{6,7},{7,8},{8,9},{9,10},{10,1... | collective-permute-start | bytes 442376 | tf_op jit(solution)/shard_map/ppermute | solution.py:363
  11.2 7.3 %collective-permute-start.1 = (bf16[144,512]{1,0:T(8,128)(2,1)}, bf16[144,512]{1,0:T(8,128)(2,1)S(1)}, u32[]{:S(2)}, u32[]{:S(2)}) collective-permute-start(bf16[144,512]{1,0:T(8,128)(2,1)} %get-tuple-element.24.own), channel_id=1, source_target_pairs={{0,1},{2,3},{4,5},{6,7},{8,9},{10,11},{12,13},{14,15},{16,17},{18,... | collective-permute-start | bytes 442376 | tf_op jit(solution)/shard_map/ppermute | solution.py:363
  18.5 0.0 copy-start.1
  18.6 0.7 copy-done.1
  19.2 2.3 %stack.22 = (bf16[4096,128]{1,0:T(8,128)(2,1)S(1)}, bf16[4096,128]{1,0:T(8,128)(2,1)S(1)}) custom-call(bf16[1,128,4096]{2,1,0:T(8,128)(2,1)} %query.1, bf16[1,128,4096]{2,1,0:T(8,128)(2,1)} %grad.1, bf16[1,48,128]{2,1,0:T(8,128)(2,1)S(1)} %bitcast.6, bf16[16,5120]{1,0:T(8,128)(2,1)S(1)} %copy-done), custom_call_target="tpu_custom_call" | custom-call | flops 16777216 | bytes 4194304 | tf_op jit(solution)/shard_map/stack/pallas_call | solution.py:374
  21.5 0.1 pad_add_fusion.place
  21.6 5.8 %collective-permute-done.2.two_even = bf16[144,512]{1,0:T(8,128)(2,1)S(1)} collective-permute-done((bf16[144,512]{1,0:T(8,128)(2,1)}, bf16[144,512]{1,0:T(8,128)(2,1)S(1)}, u32[]{:S(2)}, u32[]{:S(2)}) %collective-permute-start.2) | collective-permute-done | bytes 147488 | tf_op jit(solution)/shard_map/ppermute | solution.py:363
  27.4 1.3 %collective-permute-start.4 = (bf16[144,512]{1,0:T(8,128)(2,1)S(1)}, bf16[144,512]{1,0:T(8,128)(2,1)S(1)}, u32[]{:S(2)}, u32[]{:S(2)}) collective-permute-start(bf16[144,512]{1,0:T(8,128)(2,1)S(1)} %collective-permute-done.2.two_even), channel_id=1, source_target_pairs={{0,1},{2,3},{4,5},{6,7},{8,9},{10,11},{12,13},{14,15},{16,17},{18,... | collective-permute-start | bytes 442376 | tf_op jit(solution)/shard_map/ppermute | solution.py:363
  28.7 0.0 collective-permute-done.one.one_even
  28.7 1.3 %collective-permute-start.3 = (bf16[144,512]{1,0:T(8,128)(2,1)S(1)}, bf16[144,512]{1,0:T(8,128)(2,1)S(1)}, u32[]{:S(2)}, u32[]{:S(2)}) collective-permute-start(bf16[144,512]{1,0:T(8,128)(2,1)S(1)} %collective-permute-done.one.one_even), channel_id=1, source_target_pairs={{0,1},{2,3},{4,5},{6,7},{8,9},{10,11},{12,13},{14,15},{16,17},{18,... | collective-permute-start | bytes 442376 | tf_op jit(solution)/shard_map/ppermute | solution.py:363
  30.0 0.1 pad_add_fusion.1.place
  30.1 4.7 %light_heads.1 = (bf16[1,128,4096]{2,1,0:T(8,128)(2,1)}, bf16[8,80,128]{2,1,0:T(8,128)(2,1)S(1)}, f32[48,256]{1,0:T(8,128)S(1)}) custom-call(s32[2]{0:T(128)S(1)} %pad_add_fusion.1.place, bf16[4096,128]{1,0:T(8,128)(2,1)S(1)} %get-tuple-element.22.query, bf16[4096,128]{1,0:T(8,128)(2,1)S(1)} %get-tuple-element.23.grad, bf16[1,48,128]{2,1,0:T(8,128)(2,1)S(1)} %bitcast.7, ...), custom_call_target="tpu_custom_call" | custom-call | flops 805306368 | bytes 1572864 | tf_op jit(solution)/shard_map/light_heads/pallas_call | solution.py:391
  34.7 0.0 collective-permute-done.1.one_odd
  34.7 0.0 collective-permute-done.4.three
  34.7 0.0 collective-permute-done.3.two_odd
  34.7 6.5 %heavy_heads.1 = (bf16[1,128,4096]{2,1,0:T(8,128)(2,1)}, bf16[8,80,128]{2,1,0:T(8,128)(2,1)S(1)}, f32[48,128]{1,0:T(8,128)S(1)}, f32[32,128]{1,0:T(8,128)S(1)}, ...) custom-call(s32[2]{0:T(128)S(1)} %pad_add_fusion.place, ...), custom_call_target="tpu_custom_call", output_to_operand_aliasing={{0}: (14, {}), {1}: (15, {})} | custom-call | flops 1610612736 | bytes 1572864 | tf_op jit(solution)/shard_map/heavy_heads/pallas_call | solution.py:406
  41.3 10.6 %all_to_all.20.parts = bf16[8,80,128]{2,1,0:T(8,128)(2,1)S(1)} all-to-all(bf16[8,80,128]{2,1,0:T(8,128)(2,1)S(1)} %get-tuple-element.30), channel_id=1, replica_groups={{0,64,16,80,32,96,48,112},{1,65,17,81,33,97,49,113},{2,66,18,82,34,98,5..., dimensions={0} | all-to-all | bytes 327680 | tf_op jit(solution)/shard_map/all_to_all | solution.py:243
  51.9 12.2 %all_to_all.21.parts = bf16[8,112,128]{2,1,0:T(8,128)(2,1)S(1)} all-to-all(bf16[8,112,128]{2,1,0:T(8,128)(2,1)S(1)} %along.1), channel_id=1, replica_groups={{0,1,2,3,4,5,6,7},{64,65,66,67,68,69,70,71},{128,129,130,131,132,133,13..., dimensions={0} | all-to-all | bytes 458752 | tf_op jit(solution)/shard_map/all_to_all | solution.py:243
  64.0 0.1 beside.1
  64.1 13.3 %all_to_all.22.parts = bf16[8,112,128]{2,1,0:T(8,128)(2,1)S(1)} all-to-all(bf16[8,112,128]{2,1,0:T(8,128)(2,1)S(1)} %get-tuple-element.34), channel_id=1, replica_groups={{0,128,256,384,8,136,264,392},{64,192,320,448,72,200,328,456},{1,129,25..., dimensions={0} | all-to-all | bytes 458752 | tf_op jit(solution)/shard_map/all_to_all | solution.py:243
  77.5 12.3 %all_to_all.23.parts = bf16[8,112,128]{2,1,0:T(8,128)(2,1)S(1)} all-to-all(bf16[8,112,128]{2,1,0:T(8,128)(2,1)S(1)} %get-tuple-element.35), channel_id=1, replica_groups={{0,64,16,80,32,96,48,112},{1,65,17,81,33,97,49,113},{2,66,18,82,34,98,5..., dimensions={0} | all-to-all | bytes 458752 | tf_op jit(solution)/shard_map/all_to_all | solution.py:243
  89.8 0.8 assemble.1
  (8 shorter events, 0.1 us)
Async XLA Ops:
  0.6 17.9 %copy-start = (bf16[16,5120]{1,0:T(8,128)(2,1)S(1)}, bf16[16,5120]{1,0:T(8,128)(2,1)}, u32[]{:S(2)}) copy-start(bf16[16,5120]{1,0:T(8,128)(2,1)} %up_v.3) | copy-start | bytes 491524
  2.6 24.7 %collective-permute-start.2 = (bf16[144,512]{1,0:T(8,128)(2,1)}, bf16[144,512]{1,0:T(8,128)(2,1)S(1)}, u32[]{:S(2)}, u32[]{:S(2)}) collective-permute-start(bf16[144,512]{1,0:T(8,128)(2,1)} %get-tuple-element.25.own), channel_id=1, source_target_pairs={{0,2},{2,4},{4,6},{6,8},{8,10},{10,12},{12,14},{14,16},{16,18},{18... | collective-permute-start | bytes 442376 | tf_op jit(solution)/shard_map/ppermute | solution.py:363
  9.3 19.4 %collective-permute-start = (bf16[144,512]{1,0:T(8,128)(2,1)}, bf16[144,512]{1,0:T(8,128)(2,1)S(1)}, u32[]{:S(2)}, u32[]{:S(2)}) collective-permute-start(bf16[144,512]{1,0:T(8,128)(2,1)} %get-tuple-element.25.own), channel_id=1, source_target_pairs={{0,1},{1,2},{2,3},{3,4},{4,5},{5,6},{6,7},{7,8},{8,9},{9,10},{10,1... | collective-permute-start | bytes 442376 | tf_op jit(solution)/shard_map/ppermute | solution.py:363
  11.2 23.5 %collective-permute-start.1 = (bf16[144,512]{1,0:T(8,128)(2,1)}, bf16[144,512]{1,0:T(8,128)(2,1)S(1)}, u32[]{:S(2)}, u32[]{:S(2)}) collective-permute-start(bf16[144,512]{1,0:T(8,128)(2,1)} %get-tuple-element.24.own), channel_id=1, source_target_pairs={{0,1},{2,3},{4,5},{6,7},{8,9},{10,11},{12,13},{14,15},{16,17},{18,... | collective-permute-start | bytes 442376 | tf_op jit(solution)/shard_map/ppermute | solution.py:363
  18.5 0.7 copy-start.1
  19.2 10.8 %copy-start.3 = (bf16[144,512]{1,0:T(8,128)(2,1)S(1)}, bf16[144,512]{1,0:T(8,128)(2,1)}, u32[]{:S(2)}) copy-start(bf16[144,512]{1,0:T(8,128)(2,1)} %get-tuple-element.25.own) | copy-start | bytes 442372
  27.4 7.4 %collective-permute-start.4 = (bf16[144,512]{1,0:T(8,128)(2,1)S(1)}, bf16[144,512]{1,0:T(8,128)(2,1)S(1)}, u32[]{:S(2)}, u32[]{:S(2)}) collective-permute-start(bf16[144,512]{1,0:T(8,128)(2,1)S(1)} %collective-permute-done.2.two_even), channel_id=1, source_target_pairs={{0,1},{2,3},{4,5},{6,7},{8,9},{10,11},{12,13},{14,15},{16,17},{18,... | collective-permute-start | bytes 442376 | tf_op jit(solution)/shard_map/ppermute | solution.py:363
  28.7 6.1 %collective-permute-start.3 = (bf16[144,512]{1,0:T(8,128)(2,1)S(1)}, bf16[144,512]{1,0:T(8,128)(2,1)S(1)}, u32[]{:S(2)}, u32[]{:S(2)}) collective-permute-start(bf16[144,512]{1,0:T(8,128)(2,1)S(1)} %collective-permute-done.one.one_even), channel_id=1, source_target_pairs={{0,1},{2,3},{4,5},{6,7},{8,9},{10,11},{12,13},{14,15},{16,17},{18,... | collective-permute-start | bytes 442376 | tf_op jit(solution)/shard_map/ppermute | solution.py:363
  30.1 4.7 %copy-start.2 = (bf16[144,512]{1,0:T(8,128)(2,1)S(1)}, bf16[144,512]{1,0:T(8,128)(2,1)}, u32[]{:S(2)}) copy-start(bf16[144,512]{1,0:T(8,128)(2,1)} %get-tuple-element.24.own) | copy-start | bytes 442372

commit v9 on v6

--- a/solution.py
+++ b/solution.py
@@ -175,28 +175,9 @@
         copy.wait()
 
 
-def early_kernel(place, query, grad, up, own, attended, terms, low_terms, held, sems):
-    @pl.when(place[2] == 1)
-    def _():
-        blocks = [lambda r, c: own[r, c]]
-        light_heads(place, query, grad, up, blocks, [], attended, terms, low_terms, held, sems)
-
-
-def light_kernel(
-    place, query, grad, up, own, one, terms_before, low_before, _attended,
-    attended, terms, low_terms, held, sems,
-):
-    @pl.when(place[2] == 1)
-    def _():
-        terms[...] = terms_before[...]
-        low_terms[...] = low_before[...]
-
-    @pl.when(place[2] == 0)
-    def _():
-        blocks = [lambda r, c: own[r, c], lambda r, c: one[r, c]]
-        light_heads(
-            place, query, grad, up, blocks, [True], attended, terms, low_terms, held, sems
-        )
+def light_kernel(place, query, grad, up, own, one, attended, terms, low_terms, held, sems):
+    blocks = [lambda r, c: own[r, c], lambda r, c: one[r, c]]
+    light_heads(place, query, grad, up, blocks, [True], attended, terms, low_terms, held, sems)
 
 
 def heavy_kernel(
@@ -373,8 +354,7 @@
     position = lax.axis_index("ctx") % (GROUP // ROWS)
     light_half = position // 2
     odd = position % 2
-    early = lax.axis_index("ctx") % Z_SIZE == 0
-    light_place = jnp.stack([light_half, odd, early]).astype(jnp.int32)
+    light_place = jnp.stack([light_half, odd]).astype(jnp.int32)
     heavy_place = jnp.stack([1 - light_half, odd]).astype(jnp.int32)
     message = jax.ShapeDtypeStruct((MESSAGE, 4 * D_HEAD), BF16)
     message_spec = whole(MESSAGE, 4 * D_HEAD)
@@ -400,6 +380,8 @@
     one = send(light, 1)
     two_even = send(light, 2, 2)
     one_odd = send(heavy, 1, 2)
+    two_odd = send(one, 1, 2)
+    three = send(two_even, 1, 2)
     wide_out = jax.ShapeDtypeStruct((1, ROWS, HEADS * D_HEAD), BF16)
     terms_out = jax.ShapeDtypeStruct((2 * KV_HEADS, PART, D_HEAD), BF16)
     stacked_out = jax.ShapeDtypeStruct((HEADS * ROWS, D_HEAD), BF16)
@@ -433,17 +415,8 @@
     )
     in_smem = [pl.BlockSpec(memory_space=pltpu.SMEM)]
     attended, terms, low_terms = light_call(
-        early_kernel, in_specs=in_smem + [vmem] * 4, name="early_heads"
-    )(*light_arguments)
-    one, two_even, attended = lax.optimization_barrier((one, two_even, attended))
-    two_odd = send(one, 1, 2)
-    three = send(two_even, 1, 2)
-    attended, terms, low_terms = light_call(
-        light_kernel,
-        in_specs=in_smem + [vmem] * 7 + [anywhere],
-        input_output_aliases={8: 0},
-        name="light_heads",
-    )(*light_arguments, one, terms, low_terms, attended)
+        light_kernel, in_specs=in_smem + [vmem] * 5, name="light_heads"
+    )(*light_arguments, one)
     back_out = jax.ShapeDtypeStruct((2 * RANK, ROWS), F32)
     back_spec = whole(2 * RANK, ROWS)
     attended, terms, mine, *backs = pl.pallas_call(

time: 93.2 us -> 90.8 us (0.974)
  blocking collectives: 53.1 us -> 48.6 us
  waiting for transfers between devices: 4.01 us -> 5.75 us
    all_to_all x4, blocking collectives: 53.1 us -> 48.6 us  [exchange(): return lax.all_to_all(value, ('dp', 'ctx'), 0, 0, axis_index_groups=groups)]
    ppermute x5, waiting for transfers between devices: 4.01 us -> 5.75 us  [send(): lax.ppermute(value, 'ctx', [(i, (i + by) % spans) for i in range(0, spans...]
    pallas_call x2 -> x1, Pallas kernels: 3.95 us -> 4.28 us  [shards(): light_call(light_kernel, in_specs=in_smem + [vmem] * 5, name='light_heads')]
  transfers between devices with their start and end apart: 5 -> 5, of which waited for: 3 -> 1; matrix products, arithmetic and copies ran while one was open for 0% -> 0% of each run, Pallas kernels for 7% -> 7%
where the time goes in v9:
time: 90.8 us; the launch traced here: 90.4 us
  blocking collectives  48.6 us (54%)
  starting transfers between devices  18.4 us (20%)
  Pallas kernels  16 us (18%)
  waiting for transfers between devices  5.75 us (6%)
    all_to_all x4, blocking collectives, exchange(): return lax.all_to_all(value, ('dp', 'ctx'), 0, 0, axis_index_groups=groups)  48.6 us
    ppermute x5, starting transfers between devices, send(): lax.ppermute(value, 'ctx', [(i, (i + by) % spans) for i in range(0, spans...  18.4 us
    pallas_call x1, Pallas kernels, shards(): pl.pallas_call(heavy_kernel, out_shape=(wide_out, terms_out, jax.ShapeDty...  6.53 us
    ppermute x5, waiting for transfers between devices, send(): lax.ppermute(value, 'ctx', [(i, (i + by) % spans) for i in range(0, spans...  5.75 us
    pallas_call x1, Pallas kernels, shards(): light_call(light_kernel, in_specs=in_smem + [vmem] * 5, name='light_heads')  4.28 us
    pallas_call x1, Pallas kernels, shards(): pl.pallas_call(stack_kernel, out_shape=(stacked_out, stacked_out), in_spe...  2.29 us
    pallas_call x1, Pallas kernels, shards(): pl.pallas_call(prepare_kernel, out_shape=(message, message), grid=(1,), i...  1.99 us
  transfers between devices with their start and end apart: 5, of which 1 were waited for; matrix products, arithmetic and copies ran while one was open for 0% of the time, Pallas kernels for 7%

profile of v9, /device:TPU:1, one launch (start us, length us, event | category | flops | bytes accessed | tf_op | source)
XLA Modules:
  0.0 90.4 jit_solution(5037156139741750820)
XLA Ops:
  0.6 2.0 %prepare.1 = (bf16[144,512]{1,0:T(8,128)(2,1)}, bf16[144,512]{1,0:T(8,128)(2,1)}) custom-call(bf16[1,128,1024]{2,1,0:T(8,128)(2,1)} %frozen.1, bf16[1,48,128]{2,1,0:T(8,128)(2,1)} %bitcast.5, bf16[16,5120]{1,0:T(8,128)(2,1)} %up_v.1), custom_call_target="tpu_custom_call" | custom-call | tf_op jit(solution)/shard_map/prepare/pallas_call | solution.py:363
  2.6 6.6 %collective-permute-start.2 = (bf16[144,512]{1,0:T(8,128)(2,1)}, bf16[144,512]{1,0:T(8,128)(2,1)S(1)}, u32[]{:S(2)}, u32[]{:S(2)}) collective-permute-start(bf16[144,512]{1,0:T(8,128)(2,1)} %get-tuple-element.25.own), channel_id=1, source_target_pairs={{0,2},{2,4},{4,6},{6,8},{8,10},{10,12},{12,14},{14,16},{16,18},{18... | collective-permute-start | bytes 442376 | tf_op jit(solution)/shard_map/ppermute | solution.py:378
  9.3 1.9 %collective-permute-start = (bf16[144,512]{1,0:T(8,128)(2,1)}, bf16[144,512]{1,0:T(8,128)(2,1)S(1)}, u32[]{:S(2)}, u32[]{:S(2)}) collective-permute-start(bf16[144,512]{1,0:T(8,128)(2,1)} %get-tuple-element.25.own), channel_id=1, source_target_pairs={{0,1},{1,2},{2,3},{3,4},{4,5},{5,6},{6,7},{7,8},{8,9},{9,10},{10,1... | collective-permute-start | bytes 442376 | tf_op jit(solution)/shard_map/ppermute | solution.py:378
  11.2 7.3 %collective-permute-start.1 = (bf16[144,512]{1,0:T(8,128)(2,1)}, bf16[144,512]{1,0:T(8,128)(2,1)S(1)}, u32[]{:S(2)}, u32[]{:S(2)}) collective-permute-start(bf16[144,512]{1,0:T(8,128)(2,1)} %get-tuple-element.24.own), channel_id=1, source_target_pairs={{0,1},{2,3},{4,5},{6,7},{8,9},{10,11},{12,13},{14,15},{16,17},{18,... | collective-permute-start | bytes 442376 | tf_op jit(solution)/shard_map/ppermute | solution.py:378
  18.5 0.0 copy-start.1
  18.6 0.7 copy-done.1
  19.2 2.3 %stack.22 = (bf16[4096,128]{1,0:T(8,128)(2,1)S(1)}, bf16[4096,128]{1,0:T(8,128)(2,1)S(1)}) custom-call(bf16[1,128,4096]{2,1,0:T(8,128)(2,1)} %query.1, bf16[1,128,4096]{2,1,0:T(8,128)(2,1)} %grad.1, bf16[1,48,128]{2,1,0:T(8,128)(2,1)S(1)} %bitcast.6, bf16[16,5120]{1,0:T(8,128)(2,1)S(1)} %copy-done), custom_call_target="tpu_custom_call" | custom-call | flops 16777216 | bytes 4194304 | tf_op jit(solution)/shard_map/stack/pallas_call | solution.py:389
  21.5 0.1 pad_add_fusion.place
  21.6 5.7 %collective-permute-done.2.two_even = bf16[144,512]{1,0:T(8,128)(2,1)S(1)} collective-permute-done((bf16[144,512]{1,0:T(8,128)(2,1)}, bf16[144,512]{1,0:T(8,128)(2,1)S(1)}, u32[]{:S(2)}, u32[]{:S(2)}) %collective-permute-start.2) | collective-permute-done | bytes 147488 | tf_op jit(solution)/shard_map/ppermute | solution.py:378
  27.4 1.3 %collective-permute-start.4 = (bf16[144,512]{1,0:T(8,128)(2,1)S(1)}, bf16[144,512]{1,0:T(8,128)(2,1)S(1)}, u32[]{:S(2)}, u32[]{:S(2)}) collective-permute-start(bf16[144,512]{1,0:T(8,128)(2,1)S(1)} %collective-permute-done.2.two_even), channel_id=1, source_target_pairs={{0,1},{2,3},{4,5},{6,7},{8,9},{10,11},{12,13},{14,15},{16,17},{18,... | collective-permute-start | bytes 442376 | tf_op jit(solution)/shard_map/ppermute | solution.py:378
  28.6 0.0 collective-permute-done.one.one_even
  28.7 1.3 %collective-permute-start.3 = (bf16[144,512]{1,0:T(8,128)(2,1)S(1)}, bf16[144,512]{1,0:T(8,128)(2,1)S(1)}, u32[]{:S(2)}, u32[]{:S(2)}) collective-permute-start(bf16[144,512]{1,0:T(8,128)(2,1)S(1)} %collective-permute-done.one.one_even), channel_id=1, source_target_pairs={{0,1},{2,3},{4,5},{6,7},{8,9},{10,11},{12,13},{14,15},{16,17},{18,... | collective-permute-start | bytes 442376 | tf_op jit(solution)/shard_map/ppermute | solution.py:378
  30.0 0.1 pad_add_fusion.1.place
  30.0 4.3 %light_heads.1 = (bf16[1,128,4096]{2,1,0:T(8,128)(2,1)}, bf16[8,80,128]{2,1,0:T(8,128)(2,1)S(1)}, f32[48,256]{1,0:T(8,128)S(1)}) custom-call(s32[2]{0:T(128)S(1)} %pad_add_fusion.1.place, bf16[4096,128]{1,0:T(8,128)(2,1)S(1)} %get-tuple-element.22.query, bf16[4096,128]{1,0:T(8,128)(2,1)S(1)} %get-tuple-element.23.grad, bf16[16,5120]{1,0:T(8,128)(2,1)S(1)} %copy-done, ...), custom_call_target="tpu_custom_call" | custom-call | flops 805306368 | bytes 1572864 | tf_op jit(solution)/shard_map/light_heads/pallas_call | solution.py:417
  34.3 0.0 collective-permute-done.1.one_odd
  34.3 0.0 collective-permute-done.4.three
  34.4 0.0 collective-permute-done.3.two_odd
  34.4 6.5 %heavy_heads.1 = (bf16[1,128,4096]{2,1,0:T(8,128)(2,1)}, bf16[8,80,128]{2,1,0:T(8,128)(2,1)S(1)}, f32[48,128]{1,0:T(8,128)S(1)}, f32[32,128]{1,0:T(8,128)S(1)}, ...) custom-call(s32[2]{0:T(128)S(1)} %pad_add_fusion.place, ...), custom_call_target="tpu_custom_call", output_to_operand_aliasing={{0}: (13, {}), {1}: (14, {})} | custom-call | flops 1610612736 | bytes 1572864 | tf_op jit(solution)/shard_map/heavy_heads/pallas_call | solution.py:422
  40.9 10.6 %all_to_all.20.parts = bf16[8,80,128]{2,1,0:T(8,128)(2,1)S(1)} all-to-all(bf16[8,80,128]{2,1,0:T(8,128)(2,1)S(1)} %get-tuple-element.30), channel_id=1, replica_groups={{0,64,16,80,32,96,48,112},{1,65,17,81,33,97,49,113},{2,66,18,82,34,98,5..., dimensions={0} | all-to-all | bytes 327680 | tf_op jit(solution)/shard_map/all_to_all | solution.py:258
  51.5 12.2 %all_to_all.21.parts = bf16[8,112,128]{2,1,0:T(8,128)(2,1)S(1)} all-to-all(bf16[8,112,128]{2,1,0:T(8,128)(2,1)S(1)} %along.1), channel_id=1, replica_groups={{0,1,2,3,4,5,6,7},{64,65,66,67,68,69,70,71},{128,129,130,131,132,133,13..., dimensions={0} | all-to-all | bytes 458752 | tf_op jit(solution)/shard_map/all_to_all | solution.py:258
  63.7 0.1 beside.1
  63.7 13.2 %all_to_all.22.parts = bf16[8,112,128]{2,1,0:T(8,128)(2,1)S(1)} all-to-all(bf16[8,112,128]{2,1,0:T(8,128)(2,1)S(1)} %get-tuple-element.34), channel_id=1, replica_groups={{0,128,256,384,8,136,264,392},{64,192,320,448,72,200,328,456},{1,129,25..., dimensions={0} | all-to-all | bytes 458752 | tf_op jit(solution)/shard_map/all_to_all | solution.py:258
  76.9 12.7 %all_to_all.23.parts = bf16[8,112,128]{2,1,0:T(8,128)(2,1)S(1)} all-to-all(bf16[8,112,128]{2,1,0:T(8,128)(2,1)S(1)} %get-tuple-element.35), channel_id=1, replica_groups={{0,64,16,80,32,96,48,112},{1,65,17,81,33,97,49,113},{2,66,18,82,34,98,5..., dimensions={0} | all-to-all | bytes 458752 | tf_op jit(solution)/shard_map/all_to_all | solution.py:258
  89.6 0.8 assemble.1
  (8 shorter events, 0.1 us)
Async XLA Ops:
  0.6 17.9 %copy-start = (bf16[16,5120]{1,0:T(8,128)(2,1)S(1)}, bf16[16,5120]{1,0:T(8,128)(2,1)}, u32[]{:S(2)}) copy-start(bf16[16,5120]{1,0:T(8,128)(2,1)} %up_v.1) | copy-start | bytes 491524
  2.6 24.7 %collective-permute-start.2 = (bf16[144,512]{1,0:T(8,128)(2,1)}, bf16[144,512]{1,0:T(8,128)(2,1)S(1)}, u32[]{:S(2)}, u32[]{:S(2)}) collective-permute-start(bf16[144,512]{1,0:T(8,128)(2,1)} %get-tuple-element.25.own), channel_id=1, source_target_pairs={{0,2},{2,4},{4,6},{6,8},{8,10},{10,12},{12,14},{14,16},{16,18},{18... | collective-permute-start | bytes 442376 | tf_op jit(solution)/shard_map/ppermute | solution.py:378
  9.3 19.4 %collective-permute-start = (bf16[144,512]{1,0:T(8,128)(2,1)}, bf16[144,512]{1,0:T(8,128)(2,1)S(1)}, u32[]{:S(2)}, u32[]{:S(2)}) collective-permute-start(bf16[144,512]{1,0:T(8,128)(2,1)} %get-tuple-element.25.own), channel_id=1, source_target_pairs={{0,1},{1,2},{2,3},{3,4},{4,5},{5,6},{6,7},{7,8},{8,9},{9,10},{10,1... | collective-permute-start | bytes 442376 | tf_op jit(solution)/shard_map/ppermute | solution.py:378
  11.2 23.1 %collective-permute-start.1 = (bf16[144,512]{1,0:T(8,128)(2,1)}, bf16[144,512]{1,0:T(8,128)(2,1)S(1)}, u32[]{:S(2)}, u32[]{:S(2)}) collective-permute-start(bf16[144,512]{1,0:T(8,128)(2,1)} %get-tuple-element.24.own), channel_id=1, source_target_pairs={{0,1},{2,3},{4,5},{6,7},{8,9},{10,11},{12,13},{14,15},{16,17},{18,... | collective-permute-start | bytes 442376 | tf_op jit(solution)/shard_map/ppermute | solution.py:378
  18.5 0.7 copy-start.1
  19.2 10.8 %copy-start.3 = (bf16[144,512]{1,0:T(8,128)(2,1)S(1)}, bf16[144,512]{1,0:T(8,128)(2,1)}, u32[]{:S(2)}) copy-start(bf16[144,512]{1,0:T(8,128)(2,1)} %get-tuple-element.25.own) | copy-start | bytes 442372
  27.4 7.0 %collective-permute-start.4 = (bf16[144,512]{1,0:T(8,128)(2,1)S(1)}, bf16[144,512]{1,0:T(8,128)(2,1)S(1)}, u32[]{:S(2)}, u32[]{:S(2)}) collective-permute-start(bf16[144,512]{1,0:T(8,128)(2,1)S(1)} %collective-permute-done.2.two_even), channel_id=1, source_target_pairs={{0,1},{2,3},{4,5},{6,7},{8,9},{10,11},{12,13},{14,15},{16,17},{18,... | collective-permute-start | bytes 442376 | tf_op jit(solution)/shard_map/ppermute | solution.py:378
  28.7 5.7 %collective-permute-start.3 = (bf16[144,512]{1,0:T(8,128)(2,1)S(1)}, bf16[144,512]{1,0:T(8,128)(2,1)S(1)}, u32[]{:S(2)}, u32[]{:S(2)}) collective-permute-start(bf16[144,512]{1,0:T(8,128)(2,1)S(1)} %collective-permute-done.one.one_even), channel_id=1, source_target_pairs={{0,1},{2,3},{4,5},{6,7},{8,9},{10,11},{12,13},{14,15},{16,17},{18,... | collective-permute-start | bytes 442376 | tf_op jit(solution)/shard_map/ppermute | solution.py:378
  30.0 4.3 %copy-start.2 = (bf16[144,512]{1,0:T(8,128)(2,1)S(1)}, bf16[144,512]{1,0:T(8,128)(2,1)}, u32[]{:S(2)}) copy-start(bf16[144,512]{1,0:T(8,128)(2,1)} %get-tuple-element.24.own) | copy-start | bytes 442372

commit v10 on v9

--- a/solution.py
+++ b/solution.py
@@ -39,7 +39,17 @@
     return lax.dot_general(a, b, (((0,), (0,)), ((), ())), preferred_element_type=F32)
 
 
-def prepare_kernel(frozen, low, up, light, heavy):
+def prepare_kernel(frozen_from, low_from, up_from, light, heavy, frozen, low, up, sems):
+    columns = pl.ds(HEADS * D_HEAD, 2 * KV_HEADS * D_HEAD)
+    copies = [
+        pltpu.make_async_copy(low_from, low, sems.at[0]),
+        pltpu.make_async_copy(up_from.at[:, columns], up, sems.at[1]),
+        pltpu.make_async_copy(frozen_from, frozen, sems.at[2]),
+    ]
+    for copy in copies:
+        copy.start()
+    for copy in copies:
+        copy.wait()
     low_q, low_k, low_v = (low[0, i * RANK : (i + 1) * RANK, :] for i in range(3))
     wide = KV_HEADS * D_HEAD
     keys = (frozen[0, :, :wide].astype(F32) + 2.0 * t_mul(low_k, up[:, :wide])).astype(BF16)
@@ -363,13 +373,14 @@
     light, heavy = pl.pallas_call(
         prepare_kernel,
         out_shape=(message, message),
-        grid=(1,),
-        in_specs=[
-            only(1, ROWS, 8 * D_HEAD),
-            only(1, 3 * RANK, ROWS),
-            pl.BlockSpec((RANK, 8 * D_HEAD), lambda i: (0, HEADS // 8)),
+        in_specs=[pl.BlockSpec(memory_space=pl.ANY)] * 3,
+        out_specs=[pl.BlockSpec(memory_space=pltpu.VMEM)] * 2,
+        scratch_shapes=[
+            pltpu.VMEM((1, ROWS, 8 * D_HEAD), BF16),
+            pltpu.VMEM((1, 3 * RANK, ROWS), BF16),
+            pltpu.VMEM((RANK, 8 * D_HEAD), BF16),
+            pltpu.SemaphoreType.DMA((3,)),
         ],
-        out_specs=[only(MESSAGE, 4 * D_HEAD)] * 2,
         compiler_params=pltpu.CompilerParams(vmem_limit_bytes=56 * 1024 * 1024),
         name="prepare",
     )(frozen_key_value, columns_first, adapter_up_weight)

time: 90.8 us -> 90.9 us (level)
  no operation moved by 1% of the time
where the time goes in v10:
time: 90.9 us; the launch traced here: 90.5 us
  blocking collectives  48.6 us (53%)
  starting transfers between devices  18.4 us (20%)
  Pallas kernels  16 us (18%)
  waiting for transfers between devices  5.74 us (6%)
    all_to_all x4, blocking collectives, exchange(): return lax.all_to_all(value, ('dp', 'ctx'), 0, 0, axis_index_groups=groups)  48.6 us
    ppermute x5, starting transfers between devices, send(): lax.ppermute(value, 'ctx', [(i, (i + by) % spans) for i in range(0, spans...  18.4 us
    pallas_call x1, Pallas kernels, shards(): pl.pallas_call(heavy_kernel, out_shape=(wide_out, terms_out, jax.ShapeDty...  6.52 us
    ppermute x5, waiting for transfers between devices, send(): lax.ppermute(value, 'ctx', [(i, (i + by) % spans) for i in range(0, spans...  5.74 us
    pallas_call x1, Pallas kernels, shards(): light_call(light_kernel, in_specs=in_smem + [vmem] * 5, name='light_heads')  4.28 us
    pallas_call x1, Pallas kernels, shards(): pl.pallas_call(stack_kernel, out_shape=(stacked_out, stacked_out), in_spe...  2.29 us
    pallas_call x1, Pallas kernels, shards(): pl.pallas_call(prepare_kernel, out_shape=(message, message), in_specs=[pl...  2.04 us
  transfers between devices with their start and end apart: 5, of which 1 were waited for; matrix products, arithmetic and copies ran while one was open for 0% of the time, Pallas kernels for 7%

profile of v10, /device:TPU:1, one launch (start us, length us, event | category | flops | bytes accessed | tf_op | source)
XLA Modules:
  0.0 90.5 jit_solution(8622338877709558754)
XLA Ops:
  0.6 2.0 %prepare.1 = (bf16[144,512]{1,0:T(8,128)(2,1)}, bf16[144,512]{1,0:T(8,128)(2,1)}) custom-call(bf16[1,128,1024]{2,1,0:T(8,128)(2,1)} %frozen_from.1, bf16[1,48,128]{2,1,0:T(8,128)(2,1)} %bitcast.5, bf16[16,5120]{1,0:T(8,128)(2,1)} %up_v.1), custom_call_target="tpu_custom_call" | custom-call | tf_op jit(solution)/shard_map/prepare/pallas_call | solution.py:373
  2.7 6.6 %collective-permute-start.2 = (bf16[144,512]{1,0:T(8,128)(2,1)}, bf16[144,512]{1,0:T(8,128)(2,1)S(1)}, u32[]{:S(2)}, u32[]{:S(2)}) collective-permute-start(bf16[144,512]{1,0:T(8,128)(2,1)} %get-tuple-element.25.own), channel_id=1, source_target_pairs={{0,2},{2,4},{4,6},{6,8},{8,10},{10,12},{12,14},{14,16},{16,18},{18... | collective-permute-start | bytes 442376 | tf_op jit(solution)/shard_map/ppermute | solution.py:389
  9.3 1.9 %collective-permute-start = (bf16[144,512]{1,0:T(8,128)(2,1)}, bf16[144,512]{1,0:T(8,128)(2,1)S(1)}, u32[]{:S(2)}, u32[]{:S(2)}) collective-permute-start(bf16[144,512]{1,0:T(8,128)(2,1)} %get-tuple-element.25.own), channel_id=1, source_target_pairs={{0,1},{1,2},{2,3},{3,4},{4,5},{5,6},{6,7},{7,8},{8,9},{9,10},{10,1... | collective-permute-start | bytes 442376 | tf_op jit(solution)/shard_map/ppermute | solution.py:389
  11.3 7.3 %collective-permute-start.1 = (bf16[144,512]{1,0:T(8,128)(2,1)}, bf16[144,512]{1,0:T(8,128)(2,1)S(1)}, u32[]{:S(2)}, u32[]{:S(2)}) collective-permute-start(bf16[144,512]{1,0:T(8,128)(2,1)} %get-tuple-element.24.own), channel_id=1, source_target_pairs={{0,1},{2,3},{4,5},{6,7},{8,9},{10,11},{12,13},{14,15},{16,17},{18,... | collective-permute-start | bytes 442376 | tf_op jit(solution)/shard_map/ppermute | solution.py:389
  18.6 0.0 copy-start.1
  18.6 0.7 copy-done.1
  19.3 2.3 %stack.22 = (bf16[4096,128]{1,0:T(8,128)(2,1)S(1)}, bf16[4096,128]{1,0:T(8,128)(2,1)S(1)}) custom-call(bf16[1,128,4096]{2,1,0:T(8,128)(2,1)} %query.1, bf16[1,128,4096]{2,1,0:T(8,128)(2,1)} %grad.1, bf16[1,48,128]{2,1,0:T(8,128)(2,1)S(1)} %bitcast.6, bf16[16,5120]{1,0:T(8,128)(2,1)S(1)} %copy-done), custom_call_target="tpu_custom_call" | custom-call | flops 16777216 | bytes 4194304 | tf_op jit(solution)/shard_map/stack/pallas_call | solution.py:400
  21.6 0.1 pad_add_fusion.place
  21.7 5.7 %collective-permute-done.2.two_even = bf16[144,512]{1,0:T(8,128)(2,1)S(1)} collective-permute-done((bf16[144,512]{1,0:T(8,128)(2,1)}, bf16[144,512]{1,0:T(8,128)(2,1)S(1)}, u32[]{:S(2)}, u32[]{:S(2)}) %collective-permute-start.2) | collective-permute-done | bytes 147488 | tf_op jit(solution)/shard_map/ppermute | solution.py:389
  27.4 1.3 %collective-permute-start.4 = (bf16[144,512]{1,0:T(8,128)(2,1)S(1)}, bf16[144,512]{1,0:T(8,128)(2,1)S(1)}, u32[]{:S(2)}, u32[]{:S(2)}) collective-permute-start(bf16[144,512]{1,0:T(8,128)(2,1)S(1)} %collective-permute-done.2.two_even), channel_id=1, source_target_pairs={{0,1},{2,3},{4,5},{6,7},{8,9},{10,11},{12,13},{14,15},{16,17},{18,... | collective-permute-start | bytes 442376 | tf_op jit(solution)/shard_map/ppermute | solution.py:389
  28.7 0.0 collective-permute-done.one.one_even
  28.7 1.3 %collective-permute-start.3 = (bf16[144,512]{1,0:T(8,128)(2,1)S(1)}, bf16[144,512]{1,0:T(8,128)(2,1)S(1)}, u32[]{:S(2)}, u32[]{:S(2)}) collective-permute-start(bf16[144,512]{1,0:T(8,128)(2,1)S(1)} %collective-permute-done.one.one_even), channel_id=1, source_target_pairs={{0,1},{2,3},{4,5},{6,7},{8,9},{10,11},{12,13},{14,15},{16,17},{18,... | collective-permute-start | bytes 442376 | tf_op jit(solution)/shard_map/ppermute | solution.py:389
  30.0 0.1 pad_add_fusion.1.place
  30.1 4.3 %light_heads.1 = (bf16[1,128,4096]{2,1,0:T(8,128)(2,1)}, bf16[8,80,128]{2,1,0:T(8,128)(2,1)S(1)}, f32[48,256]{1,0:T(8,128)S(1)}) custom-call(s32[2]{0:T(128)S(1)} %pad_add_fusion.1.place, bf16[4096,128]{1,0:T(8,128)(2,1)S(1)} %get-tuple-element.22.query, bf16[4096,128]{1,0:T(8,128)(2,1)S(1)} %get-tuple-element.23.grad, bf16[16,5120]{1,0:T(8,128)(2,1)S(1)} %copy-done, ...), custom_call_target="tpu_custom_call" | custom-call | flops 805306368 | bytes 1572864 | tf_op jit(solution)/shard_map/light_heads/pallas_call | solution.py:428
  34.4 0.0 collective-permute-done.1.one_odd
  34.4 0.0 collective-permute-done.4.three
  34.4 0.0 collective-permute-done.3.two_odd
  34.4 6.5 %heavy_heads.1 = (bf16[1,128,4096]{2,1,0:T(8,128)(2,1)}, bf16[8,80,128]{2,1,0:T(8,128)(2,1)S(1)}, f32[48,128]{1,0:T(8,128)S(1)}, f32[32,128]{1,0:T(8,128)S(1)}, ...) custom-call(s32[2]{0:T(128)S(1)} %pad_add_fusion.place, ...), custom_call_target="tpu_custom_call", output_to_operand_aliasing={{0}: (13, {}), {1}: (14, {})} | custom-call | flops 1610612736 | bytes 1572864 | tf_op jit(solution)/shard_map/heavy_heads/pallas_call | solution.py:433
  40.9 10.6 %all_to_all.20.parts = bf16[8,80,128]{2,1,0:T(8,128)(2,1)S(1)} all-to-all(bf16[8,80,128]{2,1,0:T(8,128)(2,1)S(1)} %get-tuple-element.30), channel_id=1, replica_groups={{0,64,16,80,32,96,48,112},{1,65,17,81,33,97,49,113},{2,66,18,82,34,98,5..., dimensions={0} | all-to-all | bytes 327680 | tf_op jit(solution)/shard_map/all_to_all | solution.py:268
  51.6 12.2 %all_to_all.21.parts = bf16[8,112,128]{2,1,0:T(8,128)(2,1)S(1)} all-to-all(bf16[8,112,128]{2,1,0:T(8,128)(2,1)S(1)} %along.1), channel_id=1, replica_groups={{0,1,2,3,4,5,6,7},{64,65,66,67,68,69,70,71},{128,129,130,131,132,133,13..., dimensions={0} | all-to-all | bytes 458752 | tf_op jit(solution)/shard_map/all_to_all | solution.py:268
  63.7 0.1 beside.1
  63.8 13.2 %all_to_all.22.parts = bf16[8,112,128]{2,1,0:T(8,128)(2,1)S(1)} all-to-all(bf16[8,112,128]{2,1,0:T(8,128)(2,1)S(1)} %get-tuple-element.34), channel_id=1, replica_groups={{0,128,256,384,8,136,264,392},{64,192,320,448,72,200,328,456},{1,129,25..., dimensions={0} | all-to-all | bytes 458752 | tf_op jit(solution)/shard_map/all_to_all | solution.py:268
  77.0 12.7 %all_to_all.23.parts = bf16[8,112,128]{2,1,0:T(8,128)(2,1)S(1)} all-to-all(bf16[8,112,128]{2,1,0:T(8,128)(2,1)S(1)} %get-tuple-element.35), channel_id=1, replica_groups={{0,64,16,80,32,96,48,112},{1,65,17,81,33,97,49,113},{2,66,18,82,34,98,5..., dimensions={0} | all-to-all | bytes 458752 | tf_op jit(solution)/shard_map/all_to_all | solution.py:268
  89.7 0.8 assemble.1
  (8 shorter events, 0.1 us)
Async XLA Ops:
  0.6 18.0 %copy-start = (bf16[16,5120]{1,0:T(8,128)(2,1)S(1)}, bf16[16,5120]{1,0:T(8,128)(2,1)}, u32[]{:S(2)}) copy-start(bf16[16,5120]{1,0:T(8,128)(2,1)} %up_v.1) | copy-start | bytes 491524
  2.7 24.7 %collective-permute-start.2 = (bf16[144,512]{1,0:T(8,128)(2,1)}, bf16[144,512]{1,0:T(8,128)(2,1)S(1)}, u32[]{:S(2)}, u32[]{:S(2)}) collective-permute-start(bf16[144,512]{1,0:T(8,128)(2,1)} %get-tuple-element.25.own), channel_id=1, source_target_pairs={{0,2},{2,4},{4,6},{6,8},{8,10},{10,12},{12,14},{14,16},{16,18},{18... | collective-permute-start | bytes 442376 | tf_op jit(solution)/shard_map/ppermute | solution.py:389
  9.3 19.4 %collective-permute-start = (bf16[144,512]{1,0:T(8,128)(2,1)}, bf16[144,512]{1,0:T(8,128)(2,1)S(1)}, u32[]{:S(2)}, u32[]{:S(2)}) collective-permute-start(bf16[144,512]{1,0:T(8,128)(2,1)} %get-tuple-element.25.own), channel_id=1, source_target_pairs={{0,1},{1,2},{2,3},{3,4},{4,5},{5,6},{6,7},{7,8},{8,9},{9,10},{10,1... | collective-permute-start | bytes 442376 | tf_op jit(solution)/shard_map/ppermute | solution.py:389
  11.3 23.1 %collective-permute-start.1 = (bf16[144,512]{1,0:T(8,128)(2,1)}, bf16[144,512]{1,0:T(8,128)(2,1)S(1)}, u32[]{:S(2)}, u32[]{:S(2)}) collective-permute-start(bf16[144,512]{1,0:T(8,128)(2,1)} %get-tuple-element.24.own), channel_id=1, source_target_pairs={{0,1},{2,3},{4,5},{6,7},{8,9},{10,11},{12,13},{14,15},{16,17},{18,... | collective-permute-start | bytes 442376 | tf_op jit(solution)/shard_map/ppermute | solution.py:389
  18.6 0.7 copy-start.1
  19.3 10.8 %copy-start.3 = (bf16[144,512]{1,0:T(8,128)(2,1)S(1)}, bf16[144,512]{1,0:T(8,128)(2,1)}, u32[]{:S(2)}) copy-start(bf16[144,512]{1,0:T(8,128)(2,1)} %get-tuple-element.25.own) | copy-start | bytes 442372
  27.4 7.0 %collective-permute-start.4 = (bf16[144,512]{1,0:T(8,128)(2,1)S(1)}, bf16[144,512]{1,0:T(8,128)(2,1)S(1)}, u32[]{:S(2)}, u32[]{:S(2)}) collective-permute-start(bf16[144,512]{1,0:T(8,128)(2,1)S(1)} %collective-permute-done.2.two_even), channel_id=1, source_target_pairs={{0,1},{2,3},{4,5},{6,7},{8,9},{10,11},{12,13},{14,15},{16,17},{18,... | collective-permute-start | bytes 442376 | tf_op jit(solution)/shard_map/ppermute | solution.py:389
  28.7 5.7 %collective-permute-start.3 = (bf16[144,512]{1,0:T(8,128)(2,1)S(1)}, bf16[144,512]{1,0:T(8,128)(2,1)S(1)}, u32[]{:S(2)}, u32[]{:S(2)}) collective-permute-start(bf16[144,512]{1,0:T(8,128)(2,1)S(1)} %collective-permute-done.one.one_even), channel_id=1, source_target_pairs={{0,1},{2,3},{4,5},{6,7},{8,9},{10,11},{12,13},{14,15},{16,17},{18,... | collective-permute-start | bytes 442376 | tf_op jit(solution)/shard_map/ppermute | solution.py:389
  30.1 4.3 %copy-start.2 = (bf16[144,512]{1,0:T(8,128)(2,1)S(1)}, bf16[144,512]{1,0:T(8,128)(2,1)}, u32[]{:S(2)}) copy-start(bf16[144,512]{1,0:T(8,128)(2,1)} %get-tuple-element.24.own) | copy-start | bytes 442372
